TPU v7x, 32 devices: a whole 2x2x4 slice. The times are simulated.
32 devices in a mesh: pos: 8 (over y, x, core), wt: 4 (over z).
Axes of the slice: x: 2, y: 2, z: 4, core: 2. Of those that a mesh axis runs over, the one named last changes fastest.
Arguments:
- features: bfloat16 [65536, 384], P(('pos', 'wt')), may hold values from -6 to 6
- row_order: int32 [65536], P(('pos', 'wt')), may hold values from 0 to 2047, as said below
- switch_in: bfloat16 [768, 1536], P('wt'), may hold values from -0.21875 to 0.21875
- switch_out: bfloat16 [1536, 768], P('wt'), may hold values from -0.15625 to 0.15625
- hidden_bias: float32 [1536], replicated, may hold values from -3 to 3
Outputs:
- switched: bfloat16 [65536, 384], P(('pos', 'wt'))
Inputs may be any that keep to these rules, and one draw needn't show every extreme that they name: `row_order`: each aligned block of 2048 entries holds every number 0 to 2047 once.
All inputs are finite; a program needn't handle non-finite values.
Results may differ from a plain program's by a relative error of at most 0.0059.
Values may be sent and summed in bfloat16 or wider, within the bound.
No kernel may reach another device: no remote copies, remote signals or barrier semaphores. Data moves between devices by JAX's collectives and lax.ppermute only.
A program may use at most 64 MiB of HBM per device.

v0:
```python
import jax
import jax.numpy as jnp
from jax import lax
from jax.sharding import PartitionSpec as P


def switch_rows(pair, switch_in, switch_out, hidden_bias):
    hidden = jnp.dot(pair, switch_in, preferred_element_type=jnp.float32) + hidden_bias
    hidden = jax.nn.gelu(hidden, approximate=False).astype(jnp.bfloat16)
    mixed = 0.8 * pair.astype(jnp.float32) + 0.6 * jnp.dot(
        hidden, switch_out, preferred_element_type=jnp.float32
    )
    return mixed.astype(jnp.bfloat16)


def grouped_levels(received, level_bits, switch_in, switch_out, hidden_bias):
    blocks_all = received.shape[0]
    items = received.shape[1]
    width = received.shape[2]
    state = received
    for level_bit in level_bits:
        distance = 2**level_bit
        grouped = state.reshape(blocks_all // (2 * distance), 2, distance, items, width)
        pair = jnp.concatenate([grouped[:, 0], grouped[:, 1]], axis=-1).reshape(-1, 2 * width)
        mixed = switch_rows(pair, switch_in, switch_out, hidden_bias)
        mixed = mixed.reshape(blocks_all // (2 * distance), distance, items, 2 * width)
        state = jnp.stack([mixed[..., :width], mixed[..., width:]], axis=1).reshape(
            blocks_all, items, width
        )
    return state


def body(features, row_order, switch_in, switch_out, hidden_bias):
    rows_here = features.shape[0]
    width = features.shape[1]
    state = jnp.take(features, row_order, axis=0)
    full_in, full_out = (
        lax.all_gather(switch_in, "wt", axis=0, tiled=True),
        lax.all_gather(switch_out, "wt", axis=0, tiled=True),
    )
    pos_count = lax.axis_size("pos")
    log_pos = pos_count.bit_length() - 1
    level_bits = (0, log_pos // 2, log_pos - 1)
    shaped = state.reshape(pos_count, rows_here // pos_count, width)
    updated = grouped_levels(
        lax.all_to_all(shaped, "pos", split_axis=0, concat_axis=0, tiled=True),
        level_bits,
        full_in,
        full_out,
        hidden_bias,
    )
    restored = lax.all_to_all(updated, "pos", split_axis=0, concat_axis=0, tiled=True)
    state = restored.reshape(rows_here, width)
    return state


def solution(mesh):
    in_specs = (P(("pos", "wt"), None), P(("pos", "wt")), P("wt", None), P("wt", None), P())
    out_specs = P(("pos", "wt"), None)
    return jax.shard_map(body, mesh=mesh, in_specs=in_specs, out_specs=out_specs, check_vma=False)
```

profile of v0, /device:TPU:0, one launch (start us, length us, event | category | flops | bytes accessed | tf_op | source)
XLA Modules:
  0.0 211.0 jit_solution(14884733400088368324)
XLA Ops:
  6.5 0.7 all-gather.3.cloned.1.call-update
  7.3 0.7 all-gather.5.cloned.1.call-update
  8.0 0.7 compare_and_fusion
  8.7 0.7 fusion.52
  9.4 7.4 %gather_fusion = bf16[2048,384]{1,0:T(8,128)(2,1)S(1)} fusion(bf16[2048,384]{1,0:T(8,128)(2,1)S(1)} %copy-done, s32[2048]{0:T(1024)S(1)} %fusion.52), kind=kCustom, calls=%fused_computation | custom fusion | bytes 3153920 | tf_op jit(solution)/shard_map/jit(_take)/gather | solution.py:36
  16.9 0.5 broadcast_select_fusion
  17.4 25.9 %all_to_all.10 = bf16[8,256,384]{2,1,0:T(8,128)(2,1)S(1)} all-to-all(bf16[8,256,384]{2,1,0:T(8,128)(2,1)S(1)} %broadcast_select_fusion), channel_id=1, replica_groups=mesh['pos'=8,'wt'=4] {'pos'}, dimensions={0} | all-to-all | bytes 3145728 | tf_op jit(solution)/shard_map/all_to_all | solution.py:46
  43.3 1.3 fusion.151
  44.6 17.5 %all-gather.3.cloned.1.call-done = bf16[768,1536]{1,0:T(8,128)(2,1)} async-done(((bf16[192,1536]{1,0:T(8,128)(2,1)}), bf16[768,1536]{1,0:T(8,128)(2,1)}) %all-gather.3.cloned.1.call-update) | async-done | bytes 2359312 | tf_op jit(solution)/shard_map/all_gather | solution.py:38
  62.1 50.9 %all-gather.5.cloned.1.call-done = bf16[1536,768]{1,0:T(8,128)(2,1)} async-done(((bf16[384,768]{1,0:T(8,128)(2,1)}), bf16[1536,768]{1,0:T(8,128)(2,1)}) %all-gather.5.cloned.1.call-update) | async-done | bytes 2359312 | tf_op jit(solution)/shard_map/all_gather | solution.py:39
  113.0 20.4 %add_convert_fusion.2 = bf16[1024,768]{1,0:T(8,128)(2,1)S(1)} fusion(bf16[1536,768]{1,0:T(8,128)(2,1)} %all-gather.5.cloned.1.call-done, bf16[768,1536]{1,0:T(8,128)(2,1)} %all-gather.3.cloned.1.call-done, f32[1536]{0:T(1024)S(1)} %copy-done.1, bf16[1024,384]{1,0:T(8,128)(2,1)} %bitcast.45, bf16[1024,384]{1,0:T(8,128)(2,1)} %bitcast.44), kind=kOutput, calls=%fused_computation.60 | convolution fusion | flops 4945084416 | bytes 7870464 | tf_op jit(solution)/shard_map/dot_general | solution.py:10
  133.4 0.2 fusion.150
  133.6 0.2 fusion.51
  133.8 1.0 copy.12
  134.8 1.0 copy.13
  135.8 20.4 %add_convert_fusion.1 = bf16[1024,768]{1,0:T(8,128)(2,1)S(1)} fusion(bf16[1536,768]{1,0:T(8,128)(2,1)} %all-gather.5.cloned.1.call-done, bf16[768,1536]{1,0:T(8,128)(2,1)} %all-gather.3.cloned.1.call-done, f32[1536]{0:T(1024)S(1)} %copy-done.1, bf16[1024,384]{1,0:T(8,128)(2,1)} %bitcast.43, bf16[1024,384]{1,0:T(8,128)(2,1)} %bitcast.42), kind=kOutput, calls=%fused_computation.59 | convolution fusion | flops 4945084416 | bytes 7870464 | tf_op jit(solution)/shard_map/dot_general | solution.py:10
  156.1 0.2 slice_bitcast_fusion.3
  156.3 0.2 pad_maximum_fusion
  156.5 1.3 fusion.149
  157.8 20.4 %add_convert_fusion = bf16[1024,768]{1,0:T(8,128)(2,1)S(1)} fusion(bf16[1536,768]{1,0:T(8,128)(2,1)} %all-gather.5.cloned.1.call-done, bf16[768,1536]{1,0:T(8,128)(2,1)} %all-gather.3.cloned.1.call-done, f32[1536]{0:T(1024)S(1)} %copy-done.1, bf16[1024,384]{1,0:T(8,128)(2,1)} %bitcast.47, bf16[1024,384]{1,0:T(8,128)(2,1)} %bitcast.46), kind=kOutput, calls=%fused_computation.58 | convolution fusion | flops 4945084416 | bytes 7870464 | tf_op jit(solution)/shard_map/dot_general | solution.py:10
  178.2 0.2 slice_bitcast_fusion.1
  178.4 0.2 pad_maximum_fusion.1
  178.6 24.4 %all_to_all.11 = bf16[8,256,384]{2,1,0:T(8,128)(2,1)S(1)} all-to-all(bf16[8,256,384]{2,1,0:T(8,128)(2,1)S(1)} %bitcast.35), channel_id=1, replica_groups=mesh['pos'=8,'wt'=4] {'pos'}, dimensions={0} | all-to-all | bytes 3145728 | tf_op jit(solution)/shard_map/all_to_all | solution.py:52
  203.0 1.1 copy.15
  (7 shorter events, 0.1 us)
Async XLA Ops:
  6.5 2.9 %copy-start = (bf16[2048,384]{1,0:T(8,128)(2,1)S(1)}, bf16[2048,384]{1,0:T(8,128)(2,1)}, u32[]{:S(2)}) copy-start(bf16[2048,384]{1,0:T(8,128)(2,1)} %param.5) | copy-start | bytes 4718596
  6.5 55.6 %all-gather.3.cloned.1.call-start = ((), (), s32[]{:S(2)}) async-start(), calls=%async_computation.2 | async-start | bytes 2949120 | tf_op jit(solution)/shard_map/all_gather | solution.py:38
  7.3 105.8 %all-gather.5.cloned.1.call-start = ((), (), s32[]{:S(2)}) async-start(), calls=%async_computation.3 | async-start | bytes 2949120 | tf_op jit(solution)/shard_map/all_gather | solution.py:39
  43.3 69.7 %copy-start.1 = (f32[1536]{0:T(1024)S(1)}, f32[1536]{0:T(1024)}, u32[]{:S(2)}) copy-start(f32[1536]{0:T(1024)} %param.9) | copy-start | bytes 18436
Sparse Core Ops, SparseCore 0:
  8.9 53.1 all-gather.2
  63.7 49.2 all-gather.4
where the time goes:
time: 211 us
  waiting for transfers between devices  69.8 us (33%)
  matrix products  61.2 us (29%)
  blocking collectives  50.4 us (24%)
  local copies, waits for them, and re-layouts  13.7 us (6%)
  between operations  13.5 us (6%)
  other arithmetic  2.4 us (1%)
    dot_general x3, matrix products, switch_rows(): jnp.dot(hidden, switch_out, preferred_element_type=jnp.float32)  61.2 us
    all_gather x1, waiting for transfers between devices, body(): lax.all_gather(switch_out, 'wt', axis=0, tiled=True)  50.9 us
    all_to_all x1, blocking collectives, body(): lax.all_to_all(shaped, 'pos', split_axis=0, concat_axis=0, tiled=True)  25.9 us
    all_to_all x1, blocking collectives, body(): lax.all_to_all(updated, 'pos', split_axis=0, concat_axis=0, tiled=True)  24.4 us
    all_gather x1, waiting for transfers between devices, body(): lax.all_gather(switch_in, 'wt', axis=0, tiled=True)  17.5 us
    gather x1, local copies, waits for them, and re-layouts, body(): state = jnp.take(features, row_order, axis=0)  7.45 us
  transfers between devices with their start and end apart: 2, of which 2 were waited for; matrix products, arithmetic and copies ran while one was open for 5% of the time, Pallas kernels for 0%

commit v1 on v0

v1 whole, which is shorter than its diff:
```python
import functools

import jax
import jax.numpy as jnp
import numpy as np
from jax import lax
from jax.experimental import pallas as pl
from jax.experimental.pallas import tpu as pltpu
from jax.sharding import PartitionSpec as P

MEMBERS = 8
LEVELS = 3
GROUPS = 2
LANES = 128
INV_SQRT2 = np.float32(np.sqrt(0.5))

VMEM = pl.BlockSpec(memory_space=pltpu.VMEM)
SMEM = pl.BlockSpec(memory_space=pltpu.SMEM)
ANY = pl.BlockSpec(memory_space=pl.ANY)


def limits(mib):
    return pltpu.CompilerParams(vmem_limit_bytes=mib * 2**20)


def cost(flops, moved):
    return pl.CostEstimate(flops=int(flops), bytes_accessed=int(moved), transcendentals=0)


def gather_kernel(group, meta_ref, order_ref, features_ref, *rest):
    out_refs, hot_ref = rest[:MEMBERS], rest[MEMBERS]
    rows = features_ref.shape[0]
    me = meta_ref[0]
    lane = lax.broadcasted_iota(jnp.int32, (LANES, LANES), 1)
    for k in range(MEMBERS):
        taken = order_ref[pl.ds(group * MEMBERS + jnp.bitwise_xor(me, k), 1), :]
        column = jnp.broadcast_to(taken, (LANES, LANES)).T
        for j in range(rows // LANES):
            hit = jnp.where(column == lane + j * LANES, 1.0, 0.0)
            hot_ref[k * LANES : (k + 1) * LANES, j * LANES : (j + 1) * LANES] = hit.astype(jnp.bfloat16)
    taken_rows = jnp.dot(hot_ref[...], features_ref[...], preferred_element_type=jnp.float32)
    for k in range(MEMBERS):
        out_refs[k][...] = taken_rows[k * LANES : (k + 1) * LANES].astype(jnp.bfloat16)


def gather_group(group, meta, order, features):
    rows, width = features.shape
    block = jax.ShapeDtypeStruct((LANES, width), features.dtype)
    return pl.pallas_call(
        functools.partial(gather_kernel, group),
        out_shape=[block] * MEMBERS,
        in_specs=[SMEM, VMEM, VMEM],
        out_specs=[VMEM] * MEMBERS,
        scratch_shapes=[pltpu.VMEM((MEMBERS * LANES, rows), features.dtype)],
        compiler_params=limits(32),
        cost_estimate=cost(2 * MEMBERS * LANES * rows * width, 4 * rows * width),
    )(meta, order, features)


def place_kernel(n_wt, slice_rows, meta_ref, in_ref, out_ref, *rest):
    pieces, all_ref, sems = rest[:-2], rest[-2], rest[-1]
    me, my_wt = meta_ref[0], meta_ref[1]
    depth, half = in_ref.shape[0], in_ref.shape[1] // 2
    in_rows = depth * n_wt
    out_rows = out_ref.shape[0]
    cuts_in = depth // slice_rows
    copies = []

    def send(src, row, size):
        row = pl.multiple_of(row, 16)
        copies.append(pltpu.make_async_copy(src, all_ref.at[pl.ds(row, size), :], sems.at[len(copies)]))
        copies[-1].start()

    send(in_ref.at[:, pl.ds(0, half)], my_wt * depth, depth)
    send(in_ref.at[:, pl.ds(half, half)], in_rows + my_wt * depth, depth)
    send(out_ref, 2 * in_rows + my_wt * out_rows, out_rows)
    at = 0
    for k in range(1, n_wt):
        q = jnp.bitwise_xor(my_wt, k)

        def row_of(s):
            low = q * depth + s * slice_rows
            high = in_rows + q * depth + (s - cuts_in) * slice_rows
            last = 2 * in_rows + q * out_rows + (s - 2 * cuts_in) * slice_rows
            return jnp.where(s < cuts_in, low, jnp.where(s < 2 * cuts_in, high, last))

        for c in range(4):
            send(pieces[at], row_of(jnp.bitwise_xor(me, 2 * c)), slice_rows)
            at += 1
        for c in range(4):
            s = jnp.bitwise_xor(me, 2 * c + 1)
            send(pieces[at].at[pl.ds(c * slice_rows, slice_rows), :], row_of(s), slice_rows)
        at += 1
    for copy in copies:
        copy.wait()


def place(n_wt, meta, switch_in, switch_out, pieces):
    slice_rows, half = pieces[0].shape
    rows = n_wt * (2 * switch_in.shape[0] + switch_out.shape[0])
    n_copies = 3 + MEMBERS * (n_wt - 1)
    return pl.pallas_call(
        functools.partial(place_kernel, n_wt, slice_rows),
        out_shape=jax.ShapeDtypeStruct((rows, half), switch_in.dtype),
        in_specs=[SMEM] + [ANY] * (2 + len(pieces)),
        out_specs=VMEM,
        scratch_shapes=[pltpu.SemaphoreType.DMA((n_copies,))],
        compiler_params=limits(16),
        cost_estimate=cost(0, 4 * rows * half),
    )(meta, switch_in, switch_out, *pieces)


def levels_kernel(in_rows, meta_ref, weights_ref, bias_ref, *rest):
    in_refs, out_refs, state = rest[:MEMBERS], rest[MEMBERS : 2 * MEMBERS], rest[2 * MEMBERS]
    width = state.shape[2]
    pair_width = 2 * width
    half = weights_ref.shape[1]
    me = meta_ref[0]
    for k in range(MEMBERS):
        state[jnp.bitwise_xor(me, k)] = in_refs[k][...]
    chunk = half
    n_chunks = 2 * half // chunk
    for level in range(LEVELS):
        bit = 1 << level
        lower = [i for i in range(MEMBERS) if not i & bit]
        pair = jnp.concatenate(
            [jnp.concatenate([state[i], state[i | bit]], axis=1) for i in lower], axis=0
        )
        total = None
        for c in range(n_chunks):
            first = weights_ref[c * pair_width : (c + 1) * pair_width, :]
            hidden = jnp.dot(pair, first, preferred_element_type=jnp.float32)
            hidden = hidden + bias_ref[:, c * chunk : (c + 1) * chunk]
            hidden = 0.5 * hidden * (1.0 + lax.erf(hidden * INV_SQRT2))
            base = 2 * pair_width + c * chunk
            second = weights_ref[base : base + chunk, :]
            term = jnp.dot(hidden.astype(jnp.bfloat16), second, preferred_element_type=jnp.float32)
            total = term if total is None else total + term
        mixed = (0.8 * pair.astype(jnp.float32) + 0.6 * total).astype(jnp.bfloat16)
        for j, i in enumerate(lower):
            rows = mixed[j * LANES : (j + 1) * LANES]
            state[i] = rows[:, :width]
            state[i | bit] = rows[:, width:]
    for k in range(MEMBERS):
        out_refs[k][...] = state[jnp.bitwise_xor(me, k)]


def run_levels(meta, weights, bias, blocks, in_rows):
    rows, width = blocks[0].shape
    flops = LEVELS * MEMBERS // 2 * rows * 2 * weights.size
    return pl.pallas_call(
        functools.partial(levels_kernel, in_rows),
        out_shape=[jax.ShapeDtypeStruct((rows, width), blocks[0].dtype)] * MEMBERS,
        in_specs=[SMEM] + [VMEM] * (2 + MEMBERS),
        out_specs=[VMEM] * MEMBERS,
        scratch_shapes=[pltpu.VMEM((MEMBERS, rows, width), blocks[0].dtype)],
        compiler_params=limits(40),
        cost_estimate=cost(flops, 2 * weights.size),
    )(meta, weights, bias, *blocks)


def finish_kernel(meta_ref, *rest):
    blocks, out_ref, sems = rest[:-2], rest[-2], rest[-1]
    rows = blocks[0].shape[0]
    me = meta_ref[0]
    copies = []
    for n, block in enumerate(blocks):
        at = (n // MEMBERS) * MEMBERS + jnp.bitwise_xor(me, n % MEMBERS)
        dst = out_ref.at[pl.ds(pl.multiple_of(at * rows, LANES), rows), :]
        copies.append(pltpu.make_async_copy(block, dst, sems.at[n]))
        copies[-1].start()
    for copy in copies:
        copy.wait()


def finish(meta, blocks):
    rows, width = blocks[0].shape
    return pl.pallas_call(
        finish_kernel,
        out_shape=jax.ShapeDtypeStruct((rows * len(blocks), width), blocks[0].dtype),
        in_specs=[SMEM] + [ANY] * len(blocks),
        out_specs=ANY,
        scratch_shapes=[pltpu.SemaphoreType.DMA((len(blocks),))],
        compiler_params=limits(16),
        cost_estimate=cost(0, 4 * rows * len(blocks) * width),
    )(meta, *blocks)


def body(features, row_order, switch_in, switch_out, hidden_bias):
    n_pos, n_wt = lax.axis_size("pos"), lax.axis_size("wt")
    log_pos = n_pos.bit_length() - 1
    bits = (0, log_pos // 2, log_pos - 1)
    rows = features.shape[0]
    assert len(set(bits)) == LEVELS and rows == GROUPS * MEMBERS * LANES

    def spread(k):
        return sum(((k >> j) & 1) << bit for j, bit in enumerate(bits))

    def swap_pos(x, k):
        return lax.ppermute(x, "pos", [(i, i ^ spread(k)) for i in range(n_pos)])

    def swap_wt(x, k):
        return lax.ppermute(x, "wt", [(i, i ^ k) for i in range(n_wt)])

    here = lax.axis_index("pos")
    me = sum(((here >> bit) & 1) << j for j, bit in enumerate(bits))
    meta = jnp.stack([me, lax.axis_index("wt")]).astype(jnp.int32)

    depth, half = switch_in.shape[0], switch_in.shape[1] // 2
    mine = jnp.concatenate([switch_in[:, :half], switch_in[:, half:], switch_out], axis=0)
    slice_rows = mine.shape[0] // MEMBERS
    assert half == switch_out.shape[1] and depth % slice_rows == 0
    mine = lax.dynamic_slice_in_dim(mine, me * slice_rows, slice_rows, axis=0)
    fetched = [swap_wt(mine, k) for k in range(1, n_wt)]

    order = row_order.reshape(rows // LANES, LANES)
    sent = [gather_group(g, meta, order, features) for g in range(GROUPS)]
    arrived = [[s[0]] + [swap_pos(s[k], k) for k in range(1, MEMBERS)] for s in sent]

    pieces = []
    for piece in fetched:
        shared = [piece] + [swap_pos(piece, 2 * c) for c in (1, 2, 3)]
        pieces += shared + [swap_pos(jnp.concatenate(shared, axis=0), 1)]
    weights = place(n_wt, meta, switch_in, switch_out, pieces)

    bias = hidden_bias.reshape(1, -1)
    done = []
    for blocks in arrived:
        made = run_levels(meta, weights, bias, blocks, depth * n_wt)
        done += [made[0]] + [swap_pos(made[k], k) for k in range(1, MEMBERS)]
    return finish(meta, done)


def solution(mesh):
    in_specs = (P(("pos", "wt"), None), P(("pos", "wt")), P("wt", None), P("wt", None), P())
    out_specs = P(("pos", "wt"), None)
    return jax.shard_map(body, mesh=mesh, in_specs=in_specs, out_specs=out_specs, check_vma=False)
```

time: 211 us -> 114 us (0.54)
  matrix products: 61.2 us -> 0 us
  blocking collectives: 50.4 us -> 0 us
  waiting for transfers between devices: 69.8 us -> 25.6 us
  starting transfers between devices: 0.04 us -> 43.6 us
  Pallas kernels: 0 us -> 34.3 us
  between operations: 13.5 us -> 0.39 us
  local copies, waits for them, and re-layouts: 13.7 us -> 5.28 us
    all_gather x2 -> x0, waiting for transfers between devices: 68.4 us -> none  [the longest x1 50.9 us: body(): lax.all_gather(switch_out, 'wt', axis=0, tiled=True)]
    dot_general x3 -> x0, matrix products: 61.2 us -> none  [switch_rows(): jnp.dot(hidden, switch_out, preferred_element_type=jnp.float32)]
    all_to_all x2 -> x0, blocking collectives: 50.4 us -> none  [the longest x1 25.9 us: body(): lax.all_to_all(shaped, 'pos', split_axis=0, concat_axis=0, tiled=True)]
    ppermute x0 -> x43, starting transfers between devices: none -> 43.6 us  [the longest x40 37.8 us: swap_pos(): return lax.ppermute(x, 'pos', [(i, i ^ spread(k)) for i in range(n_pos)])]
    pallas_call x0 -> x6, Pallas kernels: none -> 34.3 us  [the longest x2 19.7 us: run_levels(): pl.pallas_call(functools.partial(levels_kernel, in_rows), out_shape=[jax....]
    ppermute x0 -> x43, waiting for transfers between devices: none -> 25.6 us  [the longest x40 17.2 us: swap_pos(): return lax.ppermute(x, 'pos', [(i, i ^ spread(k)) for i in range(n_pos)])]
    gather x1 -> x0, local copies, waits for them, and re-layouts: 7.45 us -> none  [body(): state = jnp.take(features, row_order, axis=0)]
    concatenate x0 -> x4, other arithmetic: none -> 2.73 us  [the longest x3 2.57 us: body(): pieces += shared + [swap_pos(jnp.concatenate(shared, axis=0), 1)]]
  transfers between devices with their start and end apart: 2 -> 43, of which waited for: 2 -> 11; matrix products, arithmetic and copies ran while one was open for 5% -> 2% of each run, Pallas kernels for 0% -> 29%
where the time goes in v1:
time: 114 us; the launch traced here: 112 us
  starting transfers between devices  43.6 us (38%)
  Pallas kernels  34.3 us (30%)
  waiting for transfers between devices  25.6 us (22%)
  local copies, waits for them, and re-layouts  5.28 us (5%)
  other arithmetic  2.8 us (2%)
    ppermute x40, starting transfers between devices, swap_pos(): return lax.ppermute(x, 'pos', [(i, i ^ spread(k)) for i in range(n_pos)])  37.8 us
    pallas_call x2, Pallas kernels, run_levels(): pl.pallas_call(functools.partial(levels_kernel, in_rows), out_shape=[jax....  19.7 us
    ppermute x40, waiting for transfers between devices, swap_pos(): return lax.ppermute(x, 'pos', [(i, i ^ spread(k)) for i in range(n_pos)])  17.2 us
    ppermute x3, waiting for transfers between devices, swap_wt(): return lax.ppermute(x, 'wt', [(i, i ^ k) for i in range(n_wt)])  8.35 us
    pallas_call x1, Pallas kernels, place(): pl.pallas_call(functools.partial(place_kernel, n_wt, slice_rows), out_sha...  6.47 us
    pallas_call x2, Pallas kernels, gather_group(): pl.pallas_call(functools.partial(gather_kernel, group), out_shape=[block]...  6.33 us
    ppermute x3, starting transfers between devices, swap_wt(): return lax.ppermute(x, 'wt', [(i, i ^ k) for i in range(n_wt)])  5.76 us
    unnamed x26, local copies, waits for them, and re-layouts  4.13 us
  transfers between devices with their start and end apart: 43, of which 11 were waited for; matrix products, arithmetic and copies ran while one was open for 2% of the time, Pallas kernels for 29%

profile of v1, /device:TPU:0, one launch (start us, length us, event | category | flops | bytes accessed | tf_op | source)
XLA Modules:
  0.0 111.9 jit_solution(15001002357701290810)
XLA Ops:
  1.4 5.1 %collective-permute-start.10 = (bf16[96,768]{1,0:T(8,128)(2,1)S(1)}, bf16[96,768]{1,0:T(8,128)(2,1)S(1)}, u32[]{:S(2)}, u32[]{:S(2)}) collective-permute-start(bf16[96,768]{1,0:T(8,128)(2,1)S(1)} %fusion.1), channel_id=1, source_target_pairs={{0,3},{1,2},{2,1},{3,0},{4,7},{5,6},{6,5},{7,4},{8,11},{9,10},{10,... | collective-permute-start | bytes 442376 | tf_op jit(solution)/shard_map/ppermute | solution.py:203
  7.2 4.1 %collective-permute-done.10.rest_10_ = bf16[96,768]{1,0:T(8,128)(2,1)S(1)} collective-permute-done((bf16[96,768]{1,0:T(8,128)(2,1)S(1)}, bf16[96,768]{1,0:T(8,128)(2,1)S(1)}, u32[]{:S(2)}, u32[]{:S(2)}) %collective-permute-start.10) | collective-permute-done | bytes 147488 | tf_op jit(solution)/shard_map/ppermute | solution.py:203
  11.3 1.7 %collective-permute-start.11 = (bf16[96,768]{1,0:T(8,128)(2,1)S(1)}, bf16[96,768]{1,0:T(8,128)(2,1)S(1)}, u32[]{:S(2)}, u32[]{:S(2)}) collective-permute-start(bf16[96,768]{1,0:T(8,128)(2,1)S(1)} %collective-permute-done.10.rest_10_), channel_id=1, source_target_pairs={{0,8},{4,12},{8,0},{12,4},{16,24},{20,28},{24,16},{28,20},{1,9},{5... | collective-permute-start | bytes 442376 | tf_op jit(solution)/shard_map/ppermute | solution.py:200
  13.0 1.5 %collective-permute-start.12 = (bf16[96,768]{1,0:T(8,128)(2,1)S(1)}, bf16[96,768]{1,0:T(8,128)(2,1)S(1)}, u32[]{:S(2)}, u32[]{:S(2)}) collective-permute-start(bf16[96,768]{1,0:T(8,128)(2,1)S(1)} %collective-permute-done.10.rest_10_), channel_id=1, source_target_pairs={{0,16},{4,20},{8,24},{12,28},{16,0},{20,4},{24,8},{28,12},{1,17},{... | collective-permute-start | bytes 442376 | tf_op jit(solution)/shard_map/ppermute | solution.py:200
  14.8 4.2 %collective-permute-done.5.rest_5_ = bf16[96,768]{1,0:T(8,128)(2,1)S(1)} collective-permute-done((bf16[96,768]{1,0:T(8,128)(2,1)S(1)}, bf16[96,768]{1,0:T(8,128)(2,1)S(1)}, u32[]{:S(2)}, u32[]{:S(2)}) %collective-permute-start.5) | collective-permute-done | bytes 147488 | tf_op jit(solution)/shard_map/ppermute | solution.py:203
  19.0 1.5 %collective-permute-start.6 = (bf16[96,768]{1,0:T(8,128)(2,1)S(1)}, bf16[96,768]{1,0:T(8,128)(2,1)S(1)}, u32[]{:S(2)}, u32[]{:S(2)}) collective-permute-start(bf16[96,768]{1,0:T(8,128)(2,1)S(1)} %collective-permute-done.5.rest_5_), channel_id=1, source_target_pairs={{0,8},{4,12},{8,0},{12,4},{16,24},{20,28},{24,16},{28,20},{1,9},{5... | collective-permute-start | bytes 442376 | tf_op jit(solution)/shard_map/ppermute | solution.py:200
  20.5 1.5 %collective-permute-start.7 = (bf16[96,768]{1,0:T(8,128)(2,1)S(1)}, bf16[96,768]{1,0:T(8,128)(2,1)S(1)}, u32[]{:S(2)}, u32[]{:S(2)}) collective-permute-start(bf16[96,768]{1,0:T(8,128)(2,1)S(1)} %collective-permute-done.5.rest_5_), channel_id=1, source_target_pairs={{0,16},{4,20},{8,24},{12,28},{16,0},{20,4},{24,8},{28,12},{1,17},{... | collective-permute-start | bytes 442376 | tf_op jit(solution)/shard_map/ppermute | solution.py:200
  22.5 1.5 %collective-permute-start.1 = (bf16[96,768]{1,0:T(8,128)(2,1)S(1)}, bf16[96,768]{1,0:T(8,128)(2,1)S(1)}, u32[]{:S(2)}, u32[]{:S(2)}) collective-permute-start(bf16[96,768]{1,0:T(8,128)(2,1)S(1)} %collective-permute-done.rest_0_), channel_id=1, source_target_pairs={{0,8},{4,12},{8,0},{12,4},{16,24},{20,28},{24,16},{28,20},{1,9},{5... | collective-permute-start | bytes 442376 | tf_op jit(solution)/shard_map/ppermute | solution.py:200
  24.0 1.5 %collective-permute-start.2 = (bf16[96,768]{1,0:T(8,128)(2,1)S(1)}, bf16[96,768]{1,0:T(8,128)(2,1)S(1)}, u32[]{:S(2)}, u32[]{:S(2)}) collective-permute-start(bf16[96,768]{1,0:T(8,128)(2,1)S(1)} %collective-permute-done.rest_0_), channel_id=1, source_target_pairs={{0,16},{4,20},{8,24},{12,28},{16,0},{20,4},{24,8},{28,12},{1,17},{... | collective-permute-start | bytes 442376 | tf_op jit(solution)/shard_map/ppermute | solution.py:200
  25.5 2.7 %collective-permute-start.3 = (bf16[96,768]{1,0:T(8,128)(2,1)S(1)}, bf16[96,768]{1,0:T(8,128)(2,1)S(1)}, u32[]{:S(2)}, u32[]{:S(2)}) collective-permute-start(bf16[96,768]{1,0:T(8,128)(2,1)S(1)} %collective-permute-done.rest_0_), channel_id=1, source_target_pairs={{0,24},{4,28},{8,16},{12,20},{16,8},{20,12},{24,0},{28,4},{1,25},{... | collective-permute-start | bytes 442376 | tf_op jit(solution)/shard_map/ppermute | solution.py:200
  32.3 2.8 %collective-permute-done.2.rest_2_ = bf16[96,768]{1,0:T(8,128)(2,1)S(1)} collective-permute-done((bf16[96,768]{1,0:T(8,128)(2,1)S(1)}, bf16[96,768]{1,0:T(8,128)(2,1)S(1)}, u32[]{:S(2)}, u32[]{:S(2)}) %collective-permute-start.2) | collective-permute-done | bytes 147488 | tf_op jit(solution)/shard_map/ppermute | solution.py:200
  39.4 3.2 %shard_map.58 = (bf16[128,384]{1,0:T(8,128)(2,1)S(1)}, bf16[128,384]{1,0:T(8,128)(2,1)S(1)}, bf16[128,384]{1,0:T(8,128)(2,1)S(1)}, bf16[128,384]{1,0:T(8,128)(2,...) custom-call(s32[2]{0:T(128)S(1)} %pad_add_fusion.meta_ref, ...), custom_call_target="tpu_custom_call" | custom-call | flops 1610612736 | bytes 3145728 | tf_op jit(solution)/shard_map/pallas_call | solution.py:49
  44.8 4.0 %collective-permute-done.30.rest_2_ = bf16[128,384]{1,0:T(8,128)(2,1)S(1)} collective-permute-done((bf16[128,384]{1,0:T(8,128)(2,1)S(1)}, bf16[128,384]{1,0:T(8,128)(2,1)S(1)}, u32[]{:S(2)}, u32[]{:S(2)}) %collective-permute-start.30) | collective-permute-done | bytes 98336 | tf_op jit(solution)/shard_map/ppermute | solution.py:200
  49.9 3.2 %shard_map.56 = (bf16[128,384]{1,0:T(8,128)(2,1)S(1)}, bf16[128,384]{1,0:T(8,128)(2,1)S(1)}, bf16[128,384]{1,0:T(8,128)(2,1)S(1)}, bf16[128,384]{1,0:T(8,128)(2,...) custom-call(s32[2]{0:T(128)S(1)} %pad_add_fusion.meta_ref, ...), custom_call_target="tpu_custom_call" | custom-call | flops 1610612736 | bytes 3145728 | tf_op jit(solution)/shard_map/pallas_call | solution.py:49
  54.1 2.4 %collective-permute-start.35 = (bf16[128,384]{1,0:T(8,128)(2,1)S(1)}, bf16[128,384]{1,0:T(8,128)(2,1)S(1)}, u32[]{:S(2)}, u32[]{:S(2)}) collective-permute-start(bf16[128,384]{1,0:T(8,128)(2,1)S(1)} %get-tuple-element.60), channel_id=1, source_target_pairs={{0,28},{4,24},{8,20},{12,16},{16,12},{20,8},{24,4},{28,0},{1,29},{... | collective-permute-start | bytes 294920 | tf_op jit(solution)/shard_map/ppermute | solution.py:200
  57.1 6.5 %shard_map.55.weights_ref = bf16[3072,768]{1,0:T(8,128)(2,1)S(1)} custom-call(s32[2]{0:T(128)S(1)} %pad_add_fusion.meta_ref, bf16[192,1536]{1,0:T(8,128)(2,1)S(1)} %copy-done, bf16[384,768]{1,0:T(8,128)(2,1)S(1)} %copy-done.1, bf16[96,768]{1,0:T(8,128)(2,1)S(1)} %collective-permute-done.rest_0_, bf16[96,768]{1,0:T(8,128)(2,1)S(1)} %copy-done.5, ...), custom_call_target="tpu_custom_call" | custom-call | bytes 9437184 | tf_op jit(solution)/shard_map/pallas_call | solution.py:102
  67.3 2.1 %collective-permute-start.21 = (bf16[128,384]{1,0:T(8,128)(2,1)S(1)}, bf16[128,384]{1,0:T(8,128)(2,1)S(1)}, u32[]{:S(2)}, u32[]{:S(2)}) collective-permute-start(bf16[128,384]{1,0:T(8,128)(2,1)S(1)} %get-tuple-element.44), channel_id=1, source_target_pairs={{0,28},{4,24},{8,20},{12,16},{16,12},{20,8},{24,4},{28,0},{1,29},{... | collective-permute-start | bytes 294920 | tf_op jit(solution)/shard_map/ppermute | solution.py:200
  69.4 9.7 %shard_map.59 = (bf16[128,384]{1,0:T(8,128)(2,1)S(1)}, bf16[128,384]{1,0:T(8,128)(2,1)S(1)}, bf16[128,384]{1,0:T(8,128)(2,1)S(1)}, bf16[128,384]{1,0:T(8,128)(2,...) custom-call(s32[2]{0:T(128)S(1)} %pad_add_fusion.meta_ref, ...), custom_call_target="tpu_custom_call" | custom-call | flops 7247757312 | bytes 4718592 | tf_op jit(solution)/shard_map/pallas_call | solution.py:151
  83.1 10.0 %shard_map.57 = (bf16[128,384]{1,0:T(8,128)(2,1)S(1)}, bf16[128,384]{1,0:T(8,128)(2,1)S(1)}, bf16[128,384]{1,0:T(8,128)(2,1)S(1)}, bf16[128,384]{1,0:T(8,128)(2,...) custom-call(s32[2]{0:T(128)S(1)} %pad_add_fusion.meta_ref, ...), custom_call_target="tpu_custom_call" | custom-call | flops 7247757312 | bytes 4718592 | tf_op jit(solution)/shard_map/pallas_call | solution.py:151
  93.7 1.8 %collective-permute-start.42 = (bf16[128,384]{1,0:T(8,128)(2,1)S(1)}, bf16[128,384]{1,0:T(8,128)(2,1)S(1)}, u32[]{:S(2)}, u32[]{:S(2)}) collective-permute-start(bf16[128,384]{1,0:T(8,128)(2,1)S(1)} %get-tuple-element.68), channel_id=1, source_target_pairs={{0,28},{4,24},{8,20},{12,16},{16,12},{20,8},{24,4},{28,0},{1,29},{... | collective-permute-start | bytes 294920 | tf_op jit(solution)/shard_map/ppermute | solution.py:200
  97.6 2.1 %collective-permute-done.41.rest_14_ = bf16[128,384]{1,0:T(8,128)(2,1)S(1)} collective-permute-done((bf16[128,384]{1,0:T(8,128)(2,1)S(1)}, bf16[128,384]{1,0:T(8,128)(2,1)S(1)}, u32[]{:S(2)}, u32[]{:S(2)}) %collective-permute-start.41) | collective-permute-done | bytes 98336 | tf_op jit(solution)/shard_map/ppermute | solution.py:200
  100.7 1.5 %collective-permute-start.26 = (bf16[128,384]{1,0:T(8,128)(2,1)S(1)}, bf16[128,384]{1,0:T(8,128)(2,1)S(1)}, u32[]{:S(2)}, u32[]{:S(2)}) collective-permute-start(bf16[128,384]{1,0:T(8,128)(2,1)S(1)} %get-tuple-element.50), channel_id=1, source_target_pairs={{0,20},{4,16},{8,28},{12,24},{16,4},{20,0},{24,12},{28,8},{1,21},{... | collective-permute-start | bytes 294920 | tf_op jit(solution)/shard_map/ppermute | solution.py:200
  105.0 4.9 %collective-permute-done.26.rest_5_ = bf16[128,384]{1,0:T(8,128)(2,1)S(1)} collective-permute-done((bf16[128,384]{1,0:T(8,128)(2,1)S(1)}, bf16[128,384]{1,0:T(8,128)(2,1)S(1)}, u32[]{:S(2)}, u32[]{:S(2)}) %collective-permute-start.26) | collective-permute-done | bytes 98336 | tf_op jit(solution)/shard_map/ppermute | solution.py:200
  109.9 1.8 %shard_map.60 = bf16[2048,384]{1,0:T(8,128)(2,1)} custom-call(s32[2]{0:T(128)S(1)} %pad_add_fusion.meta_ref, bf16[128,384]{1,0:T(8,128)(2,1)S(1)} %get-tuple-element.45.rest_0_, bf16[128,384]{1,0:T(8,128)(2,1)S(1)} %collective-permute-done.22.rest_1_, bf16[128,384]{1,0:T(8,128)(2,1)S(1)} %collective-permute-done.23.rest_2_, ...), custom_call_target="tpu_custom_call" | custom-call | bytes 3145728 | tf_op jit(solution)/shard_map/pallas_call | solution.py:178
  (101 shorter events, 30.1 us)
Async XLA Ops:
  1.4 9.9 %collective-permute-start.10 = (bf16[96,768]{1,0:T(8,128)(2,1)S(1)}, bf16[96,768]{1,0:T(8,128)(2,1)S(1)}, u32[]{:S(2)}, u32[]{:S(2)}) collective-permute-start(bf16[96,768]{1,0:T(8,128)(2,1)S(1)} %fusion.1), channel_id=1, source_target_pairs={{0,3},{1,2},{2,1},{3,0},{4,7},{5,6},{6,5},{7,4},{8,11},{9,10},{10,... | collective-permute-start | bytes 442376 | tf_op jit(solution)/shard_map/ppermute | solution.py:203
  6.5 12.5 %collective-permute-start.5 = (bf16[96,768]{1,0:T(8,128)(2,1)S(1)}, bf16[96,768]{1,0:T(8,128)(2,1)S(1)}, u32[]{:S(2)}, u32[]{:S(2)}) collective-permute-start(bf16[96,768]{1,0:T(8,128)(2,1)S(1)} %fusion.1), channel_id=1, source_target_pairs={{0,2},{1,3},{2,0},{3,1},{4,6},{5,7},{6,4},{7,5},{8,10},{9,11},{10,... | collective-permute-start | bytes 442376 | tf_op jit(solution)/shard_map/ppermute | solution.py:203
  6.5 14.0 %collective-permute-start = (bf16[96,768]{1,0:T(8,128)(2,1)S(1)}, bf16[96,768]{1,0:T(8,128)(2,1)S(1)}, u32[]{:S(2)}, u32[]{:S(2)}) collective-permute-start(bf16[96,768]{1,0:T(8,128)(2,1)S(1)} %fusion.1), channel_id=1, source_target_pairs={{0,1},{1,0},{2,3},{3,2},{4,5},{5,4},{6,7},{7,6},{8,9},{9,8},{10,11... | collective-permute-start | bytes 442376 | tf_op jit(solution)/shard_map/ppermute | solution.py:203
  11.3 10.7 %collective-permute-start.11 = (bf16[96,768]{1,0:T(8,128)(2,1)S(1)}, bf16[96,768]{1,0:T(8,128)(2,1)S(1)}, u32[]{:S(2)}, u32[]{:S(2)}) collective-permute-start(bf16[96,768]{1,0:T(8,128)(2,1)S(1)} %collective-permute-done.10.rest_10_), channel_id=1, source_target_pairs={{0,8},{4,12},{8,0},{12,4},{16,24},{20,28},{24,16},{28,20},{1,9},{5... | collective-permute-start | bytes 442376 | tf_op jit(solution)/shard_map/ppermute | solution.py:200
  22.5 9.8 %collective-permute-start.1 = (bf16[96,768]{1,0:T(8,128)(2,1)S(1)}, bf16[96,768]{1,0:T(8,128)(2,1)S(1)}, u32[]{:S(2)}, u32[]{:S(2)}) collective-permute-start(bf16[96,768]{1,0:T(8,128)(2,1)S(1)} %collective-permute-done.rest_0_), channel_id=1, source_target_pairs={{0,8},{4,12},{8,0},{12,4},{16,24},{20,28},{24,16},{28,20},{1,9},{5... | collective-permute-start | bytes 442376 | tf_op jit(solution)/shard_map/ppermute | solution.py:200
  24.0 11.1 %collective-permute-start.2 = (bf16[96,768]{1,0:T(8,128)(2,1)S(1)}, bf16[96,768]{1,0:T(8,128)(2,1)S(1)}, u32[]{:S(2)}, u32[]{:S(2)}) collective-permute-start(bf16[96,768]{1,0:T(8,128)(2,1)S(1)} %collective-permute-done.rest_0_), channel_id=1, source_target_pairs={{0,16},{4,20},{8,24},{12,28},{16,0},{20,4},{24,8},{28,12},{1,17},{... | collective-permute-start | bytes 442376 | tf_op jit(solution)/shard_map/ppermute | solution.py:200
  30.2 23.8 %collective-permute-start.14 = (bf16[384,768]{1,0:T(8,128)(2,1)}, bf16[384,768]{1,0:T(8,128)(2,1)S(1)}, u32[]{:S(2)}, u32[]{:S(2)}) collective-permute-start(bf16[384,768]{1,0:T(8,128)(2,1)} %pad_maximum_fusion.2), channel_id=1, source_target_pairs={{0,4},{4,0},{8,12},{12,8},{16,20},{20,16},{24,28},{28,24},{1,5},{5... | collective-permute-start | bytes 1769480 | tf_op jit(solution)/shard_map/ppermute | solution.py:200
  31.8 24.8 %collective-permute-start.9 = (bf16[384,768]{1,0:T(8,128)(2,1)}, bf16[384,768]{1,0:T(8,128)(2,1)S(1)}, u32[]{:S(2)}, u32[]{:S(2)}) collective-permute-start(bf16[384,768]{1,0:T(8,128)(2,1)} %pad_maximum_fusion.1), channel_id=1, source_target_pairs={{0,4},{4,0},{8,12},{12,8},{16,20},{20,16},{24,28},{28,24},{1,5},{5... | collective-permute-start | bytes 1769480 | tf_op jit(solution)/shard_map/ppermute | solution.py:200
  37.9 18.6 %collective-permute-start.4 = (bf16[384,768]{1,0:T(8,128)(2,1)}, bf16[384,768]{1,0:T(8,128)(2,1)S(1)}, u32[]{:S(2)}, u32[]{:S(2)}) collective-permute-start(bf16[384,768]{1,0:T(8,128)(2,1)} %pad_maximum_fusion), channel_id=1, source_target_pairs={{0,4},{4,0},{8,12},{12,8},{16,20},{20,16},{24,28},{28,24},{1,5},{5... | collective-permute-start | bytes 1769480 | tf_op jit(solution)/shard_map/ppermute | solution.py:200
  53.1 10.5 %collective-permute-start.33 = (bf16[128,384]{1,0:T(8,128)(2,1)S(1)}, bf16[128,384]{1,0:T(8,128)(2,1)S(1)}, u32[]{:S(2)}, u32[]{:S(2)}) collective-permute-start(bf16[128,384]{1,0:T(8,128)(2,1)S(1)} %get-tuple-element.58), channel_id=1, source_target_pairs={{0,20},{4,16},{8,28},{12,24},{16,4},{20,0},{24,12},{28,8},{1,21},{... | collective-permute-start | bytes 294920 | tf_op jit(solution)/shard_map/ppermute | solution.py:200
  53.5 11.5 %collective-permute-start.34 = (bf16[128,384]{1,0:T(8,128)(2,1)S(1)}, bf16[128,384]{1,0:T(8,128)(2,1)S(1)}, u32[]{:S(2)}, u32[]{:S(2)}) collective-permute-start(bf16[128,384]{1,0:T(8,128)(2,1)S(1)} %get-tuple-element.59), channel_id=1, source_target_pairs={{0,24},{4,28},{8,16},{12,20},{16,8},{20,12},{24,0},{28,4},{1,25},{... | collective-permute-start | bytes 294920 | tf_op jit(solution)/shard_map/ppermute | solution.py:200
  54.1 11.9 %collective-permute-start.35 = (bf16[128,384]{1,0:T(8,128)(2,1)S(1)}, bf16[128,384]{1,0:T(8,128)(2,1)S(1)}, u32[]{:S(2)}, u32[]{:S(2)}) collective-permute-start(bf16[128,384]{1,0:T(8,128)(2,1)S(1)} %get-tuple-element.60), channel_id=1, source_target_pairs={{0,28},{4,24},{8,20},{12,16},{16,12},{20,8},{24,4},{28,0},{1,29},{... | collective-permute-start | bytes 294920 | tf_op jit(solution)/shard_map/ppermute | solution.py:200
  56.5 10.2 %collective-permute-start.15 = (bf16[128,384]{1,0:T(8,128)(2,1)S(1)}, bf16[128,384]{1,0:T(8,128)(2,1)S(1)}, u32[]{:S(2)}, u32[]{:S(2)}) collective-permute-start(bf16[128,384]{1,0:T(8,128)(2,1)S(1)} %get-tuple-element.38), channel_id=1, source_target_pairs={{0,4},{4,0},{8,12},{12,8},{16,20},{20,16},{24,28},{28,24},{1,5},{5... | collective-permute-start | bytes 294920 | tf_op jit(solution)/shard_map/ppermute | solution.py:200
  56.5 10.8 %collective-permute-start.16 = (bf16[128,384]{1,0:T(8,128)(2,1)S(1)}, bf16[128,384]{1,0:T(8,128)(2,1)S(1)}, u32[]{:S(2)}, u32[]{:S(2)}) collective-permute-start(bf16[128,384]{1,0:T(8,128)(2,1)S(1)} %get-tuple-element.39), channel_id=1, source_target_pairs={{0,8},{4,12},{8,0},{12,4},{16,24},{20,28},{24,16},{28,20},{1,9},{5... | collective-permute-start | bytes 294920 | tf_op jit(solution)/shard_map/ppermute | solution.py:200
  63.5 15.6 %collective-permute-start.17 = (bf16[128,384]{1,0:T(8,128)(2,1)S(1)}, bf16[128,384]{1,0:T(8,128)(2,1)S(1)}, u32[]{:S(2)}, u32[]{:S(2)}) collective-permute-start(bf16[128,384]{1,0:T(8,128)(2,1)S(1)} %get-tuple-element.40), channel_id=1, source_target_pairs={{0,12},{4,8},{8,4},{12,0},{16,28},{20,24},{24,20},{28,16},{1,13},{... | collective-permute-start | bytes 294920 | tf_op jit(solution)/shard_map/ppermute | solution.py:200
  65.0 14.6 %collective-permute-start.18 = (bf16[128,384]{1,0:T(8,128)(2,1)S(1)}, bf16[128,384]{1,0:T(8,128)(2,1)S(1)}, u32[]{:S(2)}, u32[]{:S(2)}) collective-permute-start(bf16[128,384]{1,0:T(8,128)(2,1)S(1)} %get-tuple-element.41), channel_id=1, source_target_pairs={{0,16},{4,20},{8,24},{12,28},{16,0},{20,4},{24,8},{28,12},{1,17},{... | collective-permute-start | bytes 294920 | tf_op jit(solution)/shard_map/ppermute | solution.py:200
  66.0 14.0 %collective-permute-start.19 = (bf16[128,384]{1,0:T(8,128)(2,1)S(1)}, bf16[128,384]{1,0:T(8,128)(2,1)S(1)}, u32[]{:S(2)}, u32[]{:S(2)}) collective-permute-start(bf16[128,384]{1,0:T(8,128)(2,1)S(1)} %get-tuple-element.42), channel_id=1, source_target_pairs={{0,20},{4,16},{8,28},{12,24},{16,4},{20,0},{24,12},{28,8},{1,21},{... | collective-permute-start | bytes 294920 | tf_op jit(solution)/shard_map/ppermute | solution.py:200
  66.7 14.4 %collective-permute-start.20 = (bf16[128,384]{1,0:T(8,128)(2,1)S(1)}, bf16[128,384]{1,0:T(8,128)(2,1)S(1)}, u32[]{:S(2)}, u32[]{:S(2)}) collective-permute-start(bf16[128,384]{1,0:T(8,128)(2,1)S(1)} %get-tuple-element.43), channel_id=1, source_target_pairs={{0,24},{4,28},{8,16},{12,20},{16,8},{20,12},{24,0},{28,4},{1,25},{... | collective-permute-start | bytes 294920 | tf_op jit(solution)/shard_map/ppermute | solution.py:200
  67.3 14.8 %collective-permute-start.21 = (bf16[128,384]{1,0:T(8,128)(2,1)S(1)}, bf16[128,384]{1,0:T(8,128)(2,1)S(1)}, u32[]{:S(2)}, u32[]{:S(2)}) collective-permute-start(bf16[128,384]{1,0:T(8,128)(2,1)S(1)} %get-tuple-element.44), channel_id=1, source_target_pairs={{0,28},{4,24},{8,20},{12,16},{16,12},{20,8},{24,4},{28,0},{1,29},{... | collective-permute-start | bytes 294920 | tf_op jit(solution)/shard_map/ppermute | solution.py:200
  79.2 13.9 %collective-permute-start.36 = (bf16[128,384]{1,0:T(8,128)(2,1)S(1)}, bf16[128,384]{1,0:T(8,128)(2,1)S(1)}, u32[]{:S(2)}, u32[]{:S(2)}) collective-permute-start(bf16[128,384]{1,0:T(8,128)(2,1)S(1)} %get-tuple-element.62), channel_id=1, source_target_pairs={{0,4},{4,0},{8,12},{12,8},{16,20},{20,16},{24,28},{28,24},{1,5},{5... | collective-permute-start | bytes 294920 | tf_op jit(solution)/shard_map/ppermute | solution.py:200
  79.6 14.1 %collective-permute-start.37 = (bf16[128,384]{1,0:T(8,128)(2,1)S(1)}, bf16[128,384]{1,0:T(8,128)(2,1)S(1)}, u32[]{:S(2)}, u32[]{:S(2)}) collective-permute-start(bf16[128,384]{1,0:T(8,128)(2,1)S(1)} %get-tuple-element.63), channel_id=1, source_target_pairs={{0,8},{4,12},{8,0},{12,4},{16,24},{20,28},{24,16},{28,20},{1,9},{5... | collective-permute-start | bytes 294920 | tf_op jit(solution)/shard_map/ppermute | solution.py:200
  80.0 15.6 %collective-permute-start.38 = (bf16[128,384]{1,0:T(8,128)(2,1)S(1)}, bf16[128,384]{1,0:T(8,128)(2,1)S(1)}, u32[]{:S(2)}, u32[]{:S(2)}) collective-permute-start(bf16[128,384]{1,0:T(8,128)(2,1)S(1)} %get-tuple-element.64), channel_id=1, source_target_pairs={{0,12},{4,8},{8,4},{12,0},{16,28},{20,24},{24,20},{28,16},{1,13},{... | collective-permute-start | bytes 294920 | tf_op jit(solution)/shard_map/ppermute | solution.py:200
  81.1 15.1 %collective-permute-start.39 = (bf16[128,384]{1,0:T(8,128)(2,1)S(1)}, bf16[128,384]{1,0:T(8,128)(2,1)S(1)}, u32[]{:S(2)}, u32[]{:S(2)}) collective-permute-start(bf16[128,384]{1,0:T(8,128)(2,1)S(1)} %get-tuple-element.65), channel_id=1, source_target_pairs={{0,16},{4,20},{8,24},{12,28},{16,0},{20,4},{24,8},{28,12},{1,17},{... | collective-permute-start | bytes 294920 | tf_op jit(solution)/shard_map/ppermute | solution.py:200
  82.1 14.5 %collective-permute-start.40 = (bf16[128,384]{1,0:T(8,128)(2,1)S(1)}, bf16[128,384]{1,0:T(8,128)(2,1)S(1)}, u32[]{:S(2)}, u32[]{:S(2)}) collective-permute-start(bf16[128,384]{1,0:T(8,128)(2,1)S(1)} %get-tuple-element.66), channel_id=1, source_target_pairs={{0,20},{4,16},{8,28},{12,24},{16,4},{20,0},{24,12},{28,8},{1,21},{... | collective-permute-start | bytes 294920 | tf_op jit(solution)/shard_map/ppermute | solution.py:200
  (32 other events, 201.2 us)

commit v2 on v1

v2 whole, which is shorter than its diff:
```python
import functools

import jax
import jax.numpy as jnp
import numpy as np
from jax import lax
from jax.experimental import pallas as pl
from jax.experimental.pallas import tpu as pltpu
from jax.sharding import PartitionSpec as P

MEMBERS = 8
CHIPS = MEMBERS // 2
LEVELS = 3
MODES = {1: 'S1', 2: 'S2', 3: 'S2'}
GROUPS = 2
LANES = 128
INV_SQRT2 = np.float32(np.sqrt(0.5))

VMEM = pl.BlockSpec(memory_space=pltpu.VMEM)
SMEM = pl.BlockSpec(memory_space=pltpu.SMEM)
ANY = pl.BlockSpec(memory_space=pl.ANY)


def limits(mib):
    return pltpu.CompilerParams(vmem_limit_bytes=mib * 2**20)


def cost(flops, moved):
    return pl.CostEstimate(flops=int(flops), bytes_accessed=int(moved), transcendentals=0)


def gather_kernel(meta_ref, order_ref, features_ref, *rest):
    out_refs, hot_ref = rest[:CHIPS], rest[CHIPS]
    rows, width = features_ref.shape
    share = rows // MEMBERS
    tiles = share // LANES
    me = meta_ref[0]
    lane = lax.broadcasted_iota(jnp.int32, (LANES, LANES), 1)
    for chip in range(CHIPS):
        for n in range(2 * tiles):
            member = jnp.bitwise_xor(me, 2 * chip + n // tiles)
            taken = order_ref[pl.ds(member * tiles + n % tiles, 1), :]
            column = jnp.broadcast_to(taken, (LANES, LANES)).T
            for j in range(rows // LANES):
                hit = jnp.where(column == lane + j * LANES, 1.0, 0.0)
                hot_ref[n * LANES : (n + 1) * LANES, j * LANES : (j + 1) * LANES] = hit.astype(jnp.bfloat16)
        found = jnp.dot(hot_ref[...], features_ref[...], preferred_element_type=jnp.float32)
        out_refs[chip][...] = found.astype(jnp.bfloat16).reshape(2, share, width)


def gather(meta, order, features):
    rows, width = features.shape
    share = rows // MEMBERS
    return pl.pallas_call(
        gather_kernel,
        out_shape=[jax.ShapeDtypeStruct((2, share, width), features.dtype)] * CHIPS,
        in_specs=[SMEM, VMEM, VMEM],
        out_specs=[VMEM] * CHIPS,
        scratch_shapes=[pltpu.VMEM((2 * share, rows), features.dtype)],
        compiler_params=limits(32),
        cost_estimate=cost(2 * rows * rows * width, 4 * rows * width),
    )(meta, order, features)


def place_kernel(n_wt, plan, meta_ref, in_ref, out_ref, *rest):
    parts, all_ref = rest[:-1], rest[-1]
    me, my_wt = meta_ref[0], meta_ref[1]
    depth, half = in_ref.shape[0], in_ref.shape[1] // 2
    in_rows, out_rows = depth * n_wt, out_ref.shape[0]

    def put(quarter, row, value):
        left, right = quarter * depth + row, in_rows + quarter * depth + row - depth
        last = 2 * in_rows + quarter * out_rows + row - 2 * depth
        row = jnp.where(row < depth, left, jnp.where(row < 2 * depth, right, last))
        all_ref[pl.ds(pl.multiple_of(row, 16), value.shape[0]), :] = value

    put(my_wt, 0, in_ref[:, :half])
    put(my_wt, depth, in_ref[:, half:])
    put(my_wt, 2 * depth, out_ref[...])
    for part, pieces in zip(parts, plan, strict=True):
        base = 0
        for k, flip, rows_of in pieces:
            for row, size in rows_of(jnp.bitwise_xor(me, flip)):
                put(jnp.bitwise_xor(my_wt, k), row, part[base : base + size, :])
                base += size


def place(n_wt, plan, meta, switch_in, switch_out, parts):
    half = switch_in.shape[1] // 2
    rows = n_wt * (2 * switch_in.shape[0] + switch_out.shape[0])
    return pl.pallas_call(
        functools.partial(place_kernel, n_wt, plan),
        out_shape=jax.ShapeDtypeStruct((rows, half), switch_in.dtype),
        in_specs=[SMEM] + [VMEM] * (2 + len(parts)),
        out_specs=VMEM,
        compiler_params=limits(24),
        cost_estimate=cost(0, 4 * rows * half),
    )(meta, switch_in, switch_out, *parts)


def levels_kernel(meta_ref, weights_ref, bias_ref, *rest):
    in_refs, other_ref = rest[:CHIPS], rest[CHIPS]
    out_refs, state = rest[CHIPS + 1 : 2 * CHIPS + 1], rest[2 * CHIPS + 1]
    rows, width = state.shape[1:]
    pair_width = 2 * width
    half = weights_ref.shape[1]
    me = meta_ref[0]
    for c in range(CHIPS):
        state[jnp.bitwise_xor(me, 2 * c)] = in_refs[c][0]
        state[jnp.bitwise_xor(me, 2 * c + 1)] = other_ref[c]
    for level in range(LEVELS):
        bit = 1 << level
        lower = [i for i in range(MEMBERS) if not i & bit]
        pair = jnp.concatenate(
            [jnp.concatenate([state[i], state[i | bit]], axis=1) for i in lower], axis=0
        )
        made = []
        for c in range(2):
            first = weights_ref[c * pair_width : (c + 1) * pair_width, :]
            hidden = jnp.dot(pair, first, preferred_element_type=jnp.float32)
            hidden = hidden + bias_ref[:, c * half : (c + 1) * half]
            hidden = 0.5 * hidden * (1.0 + lax.erf(hidden * INV_SQRT2))
            made.append(hidden.astype(jnp.bfloat16))
        second = weights_ref[2 * pair_width :, :]
        total = jnp.dot(jnp.concatenate(made, axis=1), second, preferred_element_type=jnp.float32)
        mixed = (0.8 * pair.astype(jnp.float32) + 0.6 * total).astype(jnp.bfloat16)
        for j, i in enumerate(lower):
            made = mixed[j * rows : (j + 1) * rows]
            state[i] = made[:, :width]
            state[i | bit] = made[:, width:]
    for c in range(CHIPS):
        out_refs[c][0] = state[jnp.bitwise_xor(me, 2 * c)]
        out_refs[c][1] = state[jnp.bitwise_xor(me, 2 * c + 1)]


def run_levels(meta, weights, bias, blocks, others):
    _, rows, width = blocks[0].shape
    flops = LEVELS * MEMBERS // 2 * rows * 2 * weights.size
    return pl.pallas_call(
        levels_kernel,
        out_shape=[jax.ShapeDtypeStruct((2, rows, width), blocks[0].dtype)] * CHIPS,
        in_specs=[SMEM] + [VMEM] * (3 + CHIPS),
        out_specs=[VMEM] * CHIPS,
        scratch_shapes=[pltpu.VMEM((MEMBERS, rows, width), blocks[0].dtype)],
        compiler_params=limits(40),
        cost_estimate=cost(flops, 2 * weights.size),
    )(meta, weights, bias, *blocks, others)


def finish_kernel(meta_ref, *rest):
    arrays, out_ref, sems = rest[:-2], rest[-2], rest[-1]
    per_group = CHIPS + 1
    rows = arrays[0].shape[1]
    share = rows * (len(arrays) // per_group)
    me = meta_ref[0]
    copies = []

    def put(src, member, group):
        dst = out_ref.at[pl.ds(pl.multiple_of(member * share + group * rows, 16), rows), :]
        copies.append(pltpu.make_async_copy(src, dst, sems.at[len(copies)]))
        copies[-1].start()

    for group in range(len(arrays) // per_group):
        held = arrays[group * per_group : (group + 1) * per_group]
        for c in range(CHIPS):
            put(held[c].at[0], jnp.bitwise_xor(me, 2 * c), group)
            put(held[CHIPS].at[c], jnp.bitwise_xor(me, 2 * c + 1), group)
    for copy in copies:
        copy.wait()


def finish(meta, arrays):
    _, rows, width = arrays[0].shape
    n_blocks = len(arrays) // (CHIPS + 1) * MEMBERS
    return pl.pallas_call(
        finish_kernel,
        out_shape=jax.ShapeDtypeStruct((rows * n_blocks, width), arrays[0].dtype),
        in_specs=[SMEM] + [VMEM] * len(arrays),
        out_specs=ANY,
        scratch_shapes=[pltpu.SemaphoreType.DMA((n_blocks,))],
        compiler_params=limits(16),
        cost_estimate=cost(0, 4 * rows * n_blocks * width),
    )(meta, *arrays)


def body(features, row_order, switch_in, switch_out, hidden_bias):
    n_pos, n_wt = lax.axis_size("pos"), lax.axis_size("wt")
    log_pos = n_pos.bit_length() - 1
    bits = (0, log_pos // 2, log_pos - 1)
    rows = features.shape[0]
    assert len(set(bits)) == LEVELS and rows % (GROUPS * MEMBERS * LANES) == 0

    def spread(k):
        return sum(((k >> j) & 1) << bit for j, bit in enumerate(bits))

    def swap_pos(x, k):
        return lax.ppermute(x, "pos", [(i, i ^ spread(k)) for i in range(n_pos)])

    def swap_wt(x, k):
        return lax.ppermute(x, "wt", [(i, i ^ k) for i in range(n_wt)])

    here = lax.axis_index("pos")
    me = sum(((here >> bit) & 1) << j for j, bit in enumerate(bits))
    meta = jnp.stack([me, lax.axis_index("wt")]).astype(jnp.int32)

    half = switch_in.shape[1] // 2
    quarter = jnp.concatenate([switch_in[:, :half], switch_in[:, half:], switch_out], axis=0)
    depth, total = switch_in.shape[0], quarter.shape[0]
    assert total == 4 * depth

    eighth_rows = total // MEMBERS

    def halves(me):
        return [((me & 1) * (total // 2) + n * depth, depth) for n in range(2)]

    def eighth(me):
        return [(me * eighth_rows, eighth_rows)]

    def left(me):
        return [(((me >> 1) & 1) * 2 * eighth_rows + (me & 1) * eighth_rows, eighth_rows)]

    def right(me):
        return [(total // 2 + ((me >> 2) & 1) * 2 * eighth_rows + (me & 1) * eighth_rows, eighth_rows)]

    def cut(*pieces):
        taken = [lax.dynamic_slice_in_dim(quarter, row, size, axis=0) for p in pieces for row, size in p(me)]
        return jnp.concatenate(taken, axis=0) if len(taken) > 1 else taken[0]

    def after(x, *earlier):
        return lax.optimization_barrier((x, earlier))[0]

    def join(xs):
        return jnp.concatenate(xs, axis=0) if len(xs) > 1 else xs[0]

    share = rows // MEMBERS
    kinds = {"S1": (halves,), "S2": (left, right), "S4": (eighth,)}
    sources = {mode: cut(*kinds[mode]) for mode in sorted(set(MODES.values()))}

    def cross(pairs):
        pairs = [pairs[0]] + [swap_pos(pairs[c], 2 * c) for c in range(1, CHIPS)]
        return pairs, swap_pos(jnp.stack([p[1] for p in pairs]), 1)

    parts, plan = [], []

    def spread_parts(owned):
        held = [(o, [(k, 0, p) for p in kinds[MODES[k]]]) for k, o in owned]
        for c in (1, 2, 3):
            payload, pieces = [], []
            for k, own in owned:
                mode = MODES[k]
                if mode == "S4":
                    payload.append(own)
                    pieces.append((k, 2 * c, eighth))
                if mode == "S2" and c < 3:
                    payload.append(own[:eighth_rows] if c == 1 else own[eighth_rows:])
                    pieces.append((k, 2 * c, left if c == 1 else right))
            if payload:
                held.append((swap_pos(join(payload), 2 * c), pieces))
        held.append((swap_pos(join([h[0] for h in held]), 1), [(k, flip + 1, p) for h in held for k, flip, p in h[1]]))
        for part, pieces in held:
            parts.append(part)
            plan.append(pieces)
        return held

    def get(k, *deps):
        src = sources[MODES[k]]
        return swap_wt(after(src, *deps) if deps else src, k)

    def gather_all():
        return gather(meta, row_order.reshape(rows // LANES, LANES), features)

    size = share // GROUPS

    def halve(first):
        return [([p[:, g * size : (g + 1) * size] for p in first[0]], first[1][:, g * size : (g + 1) * size]) for g in range(GROUPS)]

    owned = {k: get(k) for k in range(1, n_wt)}
    first = cross(gather_all())
    for k in range(1, n_wt):
        spread_parts([(k, owned[k])])
    split = halve(first)
    weights = place(n_wt, plan, meta, switch_in, switch_out, parts)
    bias = hidden_bias.reshape(1, -1)
    done = []
    for group in range(GROUPS):
        kept, received = cross(run_levels(meta, weights, bias, *split[group]))
        done += kept + [received]
    return finish(meta, done)


def solution(mesh):
    in_specs = (P(("pos", "wt"), None), P(("pos", "wt")), P("wt", None), P("wt", None), P())
    out_specs = P(("pos", "wt"), None)
    return jax.shard_map(body, mesh=mesh, in_specs=in_specs, out_specs=out_specs, check_vma=False)
```

time: 114 us -> 84.1 us (0.74)
  the two profiles are of different devices: /device:TPU:0 before, /device:TPU:17 now
where the time goes in v2:
time: 84.1 us; the launch traced here: 83.9 us
  starting transfers between devices  30.9 us (37%)
  Pallas kernels  25.5 us (30%)
  waiting for transfers between devices  21.6 us (26%)
  local copies, waits for them, and re-layouts  3.19 us (4%)
  other arithmetic  2.18 us (3%)
    ppermute x19, starting transfers between devices, swap_pos(): return lax.ppermute(x, 'pos', [(i, i ^ spread(k)) for i in range(n_pos)])  27.5 us
    pallas_call x2, Pallas kernels, run_levels(): pl.pallas_call(levels_kernel, out_shape=[jax.ShapeDtypeStruct((2, rows, w...  17.5 us
    ppermute x19, waiting for transfers between devices, swap_pos(): return lax.ppermute(x, 'pos', [(i, i ^ spread(k)) for i in range(n_pos)])  12 us
    ppermute x3, waiting for transfers between devices, swap_wt(): return lax.ppermute(x, 'wt', [(i, i ^ k) for i in range(n_wt)])  9.67 us
    pallas_call x1, Pallas kernels, gather(): pl.pallas_call(gather_kernel, out_shape=[jax.ShapeDtypeStruct((2, share,...  5.34 us
    ppermute x3, starting transfers between devices, swap_wt(): return lax.ppermute(x, 'wt', [(i, i ^ k) for i in range(n_wt)])  3.38 us
    pallas_call x1, Pallas kernels, finish(): pl.pallas_call(finish_kernel, out_shape=jax.ShapeDtypeStruct((rows * n_bl...  1.81 us
    concatenate x2, other arithmetic, cut(): return jnp.concatenate(taken, axis=0) if len(taken) > 1 else taken[0]  1.69 us
  transfers between devices with their start and end apart: 22, of which 10 were waited for; matrix products, arithmetic and copies ran while one was open for 3% of the time, Pallas kernels for 17%

profile of v2, /device:TPU:17, one launch (start us, length us, event | category | flops | bytes accessed | tf_op | source)
XLA Modules:
  0.0 83.9 jit_solution(14969073937025854014)
XLA Ops:
  2.6 3.2 %collective-permute-start.2 = (bf16[192,768]{1,0:T(8,128)(2,1)}, bf16[192,768]{1,0:T(8,128)(2,1)S(1)}, u32[]{:S(2)}, u32[]{:S(2)}) collective-permute-start(bf16[192,768]{1,0:T(8,128)(2,1)} %pad_maximum_fusion.7), channel_id=1, source_target_pairs={{0,2},{1,3},{2,0},{3,1},{4,6},{5,7},{6,4},{7,5},{8,10},{9,11},{10,... | collective-permute-start | bytes 884744 | tf_op jit(solution)/shard_map/ppermute | solution.py:200
  8.0 5.3 %shard_map.56 = (bf16[2,256,384]{2,1,0:T(8,128)(2,1)S(1)}, bf16[2,256,384]{2,1,0:T(8,128)(2,1)S(1)}, bf16[2,256,384]{2,1,0:T(8,128)(2,1)S(1)}, bf16[2,256,384]{2,1,0:T(8,128)(2,1)S(1)}) custom-call(s32[2]{0:T(128)S(1)} %pad_add_fusion.meta_ref, s32[16,128]{1,0:T(8,128)S(1)} %bitcast.3, bf16[2048,384]{1,0:T(8,128)(2,1)S(1)} %copy-done.2), custom_call_target="tpu_custom_call" | custom-call | flops 3221225472 | bytes 3145728 | tf_op jit(solution)/shard_map/pallas_call | solution.py:54
  13.3 1.3 %collective-permute-start.10 = (bf16[2,256,384]{2,1,0:T(8,128)(2,1)S(1)}, bf16[2,256,384]{2,1,0:T(8,128)(2,1)S(1)}, u32[]{:S(2)}, u32[]{:S(2)}) collective-permute-start(bf16[2,256,384]{2,1,0:T(8,128)(2,1)S(1)} %get-tuple-element.18), channel_id=1, source_target_pairs={{0,8},{4,12},{8,0},{12,4},{16,24},{20,28},{24,16},{28,20},{1,9},{5... | collective-permute-start | bytes 1179656 | tf_op jit(solution)/shard_map/ppermute | solution.py:197
  15.9 7.2 %collective-permute-done.6.rest_6_ = bf16[192,768]{1,0:T(8,128)(2,1)S(1)} collective-permute-done((bf16[192,768]{1,0:T(8,128)(2,1)}, bf16[192,768]{1,0:T(8,128)(2,1)S(1)}, u32[]{:S(2)}, u32[]{:S(2)}) %collective-permute-start.6) | collective-permute-done | bytes 294944 | tf_op jit(solution)/shard_map/ppermute | solution.py:200
  23.2 2.2 %collective-permute-start.12 = (bf16[2,256,384]{2,1,0:T(8,128)(2,1)S(1)}, bf16[2,256,384]{2,1,0:T(8,128)(2,1)S(1)}, u32[]{:S(2)}, u32[]{:S(2)}) collective-permute-start(bf16[2,256,384]{2,1,0:T(8,128)(2,1)S(1)} %get-tuple-element.20), channel_id=1, source_target_pairs={{0,24},{4,28},{8,16},{12,20},{16,8},{20,12},{24,0},{28,4},{1,25},{... | collective-permute-start | bytes 1179656 | tf_op jit(solution)/shard_map/ppermute | solution.py:197
  25.4 2.4 %collective-permute-done.2.rest_2_ = bf16[192,768]{1,0:T(8,128)(2,1)S(1)} collective-permute-done((bf16[192,768]{1,0:T(8,128)(2,1)}, bf16[192,768]{1,0:T(8,128)(2,1)S(1)}, u32[]{:S(2)}, u32[]{:S(2)}) %collective-permute-start.2) | collective-permute-done | bytes 294944 | tf_op jit(solution)/shard_map/ppermute | solution.py:200
  29.0 1.3 %collective-permute-start.8 = (bf16[96,768]{1,0:T(8,128)(2,1)S(1)}, bf16[96,768]{1,0:T(8,128)(2,1)S(1)}, u32[]{:S(2)}, u32[]{:S(2)}) collective-permute-start(bf16[96,768]{1,0:T(8,128)(2,1)S(1)} %get-tuple-element.45), channel_id=1, source_target_pairs={{0,16},{4,20},{8,24},{12,28},{16,0},{20,4},{24,8},{28,12},{1,17},{... | collective-permute-start | bytes 442376 | tf_op jit(solution)/shard_map/ppermute | solution.py:197
  30.7 1.3 %collective-permute-done.12 = bf16[2,256,384]{2,1,0:T(8,128)(2,1)S(1)} collective-permute-done((bf16[2,256,384]{2,1,0:T(8,128)(2,1)S(1)}, bf16[2,256,384]{2,1,0:T(8,128)(2,1)S(1)}, u32[]{:S(2)}, u32[]{:S(2)}) %collective-permute-start.12) | collective-permute-done | bytes 393248 | tf_op jit(solution)/shard_map/ppermute | solution.py:197
  32.0 1.2 %collective-permute-start.4 = (bf16[96,768]{1,0:T(8,128)(2,1)S(1)}, bf16[96,768]{1,0:T(8,128)(2,1)S(1)}, u32[]{:S(2)}, u32[]{:S(2)}) collective-permute-start(bf16[96,768]{1,0:T(8,128)(2,1)S(1)} %get-tuple-element.47), channel_id=1, source_target_pairs={{0,16},{4,20},{8,24},{12,28},{16,0},{20,4},{24,8},{28,12},{1,17},{... | collective-permute-start | bytes 442376 | tf_op jit(solution)/shard_map/ppermute | solution.py:197
  33.4 1.8 %collective-permute-done.7.rest_7_ = bf16[96,768]{1,0:T(8,128)(2,1)S(1)} collective-permute-done((bf16[96,768]{1,0:T(8,128)(2,1)S(1)}, bf16[96,768]{1,0:T(8,128)(2,1)S(1)}, u32[]{:S(2)}, u32[]{:S(2)}) %collective-permute-start.7) | collective-permute-done | bytes 147488 | tf_op jit(solution)/shard_map/ppermute | solution.py:197
  35.2 5.3 %collective-permute-start.13 = (bf16[4,256,384]{2,1,0:T(8,128)(2,1)S(1)}, bf16[4,256,384]{2,1,0:T(8,128)(2,1)S(1)}, u32[]{:S(2)}, u32[]{:S(2)}) collective-permute-start(bf16[4,256,384]{2,1,0:T(8,128)(2,1)S(1)} %pad_maximum_fusion.1), channel_id=1, source_target_pairs={{0,4},{4,0},{8,12},{12,8},{16,20},{20,16},{24,28},{28,24},{1,5},{5... | collective-permute-start | bytes 2359304 | tf_op jit(solution)/shard_map/ppermute | solution.py:197
  40.8 3.2 %collective-permute-start.5 = (bf16[384,768]{1,0:T(8,128)(2,1)S(1)}, bf16[384,768]{1,0:T(8,128)(2,1)S(1)}, u32[]{:S(2)}, u32[]{:S(2)}) collective-permute-start(bf16[384,768]{1,0:T(8,128)(2,1)S(1)} %pad_maximum_fusion.3), channel_id=1, source_target_pairs={{0,4},{4,0},{8,12},{12,8},{16,20},{20,16},{24,28},{28,24},{1,5},{5... | collective-permute-start | bytes 1769480 | tf_op jit(solution)/shard_map/ppermute | solution.py:197
  44.3 1.3 %collective-permute-done.5.rest_5_ = bf16[384,768]{1,0:T(8,128)(2,1)S(1)} collective-permute-done((bf16[384,768]{1,0:T(8,128)(2,1)S(1)}, bf16[384,768]{1,0:T(8,128)(2,1)S(1)}, u32[]{:S(2)}, u32[]{:S(2)}) %collective-permute-start.5) | collective-permute-done | bytes 589856 | tf_op jit(solution)/shard_map/ppermute | solution.py:197
  47.3 8.9 %shard_map.58 = (bf16[2,128,384]{2,1,0:T(8,128)(2,1)S(1)}, bf16[2,128,384]{2,1,0:T(8,128)(2,1)S(1)}, bf16[2,128,384]{2,1,0:T(8,128)(2,1)S(1)}, bf16[2,128,384]{2,1,0:T(8,128)(2,1)S(1)}) custom-call(s32[2]{0:T(128)S(1)} %pad_add_fusion.meta_ref, bf16[3072,768]{1,0:T(8,128)(2,1)S(1)} %shard_map.55.weights_ref, f32[1,1536]{1,0:T(1,128)S(1)} %reshape.6.bias_ref, ...), custom_call_target="tpu_custom_call" | custom-call | flops 7247757312 | bytes 4718592 | tf_op jit(solution)/shard_map/pallas_call | solution.py:139
  56.2 1.3 %collective-permute-start.18 = (bf16[2,128,384]{2,1,0:T(8,128)(2,1)S(1)}, bf16[2,128,384]{2,1,0:T(8,128)(2,1)S(1)}, u32[]{:S(2)}, u32[]{:S(2)}) collective-permute-start(bf16[2,128,384]{2,1,0:T(8,128)(2,1)S(1)} %get-tuple-element.26), channel_id=1, source_target_pairs={{0,8},{4,12},{8,0},{12,4},{16,24},{20,28},{24,16},{28,20},{1,9},{5... | collective-permute-start | bytes 589832 | tf_op jit(solution)/shard_map/ppermute | solution.py:197
  57.5 1.2 %collective-permute-start.19 = (bf16[2,128,384]{2,1,0:T(8,128)(2,1)S(1)}, bf16[2,128,384]{2,1,0:T(8,128)(2,1)S(1)}, u32[]{:S(2)}, u32[]{:S(2)}) collective-permute-start(bf16[2,128,384]{2,1,0:T(8,128)(2,1)S(1)} %get-tuple-element.27), channel_id=1, source_target_pairs={{0,16},{4,20},{8,24},{12,28},{16,0},{20,4},{24,8},{28,12},{1,17},{... | collective-permute-start | bytes 589832 | tf_op jit(solution)/shard_map/ppermute | solution.py:197
  58.9 8.7 %shard_map.57 = (bf16[2,128,384]{2,1,0:T(8,128)(2,1)S(1)}, bf16[2,128,384]{2,1,0:T(8,128)(2,1)S(1)}, bf16[2,128,384]{2,1,0:T(8,128)(2,1)S(1)}, bf16[2,128,384]{2,1,0:T(8,128)(2,1)S(1)}) custom-call(s32[2]{0:T(128)S(1)} %pad_add_fusion.meta_ref, bf16[3072,768]{1,0:T(8,128)(2,1)S(1)} %shard_map.55.weights_ref, f32[1,1536]{1,0:T(1,128)S(1)} %reshape.6.bias_ref, ...), custom_call_target="tpu_custom_call" | custom-call | flops 7247757312 | bytes 4718592 | tf_op jit(solution)/shard_map/pallas_call | solution.py:139
  67.6 1.3 %collective-permute-start.14 = (bf16[2,128,384]{2,1,0:T(8,128)(2,1)S(1)}, bf16[2,128,384]{2,1,0:T(8,128)(2,1)S(1)}, u32[]{:S(2)}, u32[]{:S(2)}) collective-permute-start(bf16[2,128,384]{2,1,0:T(8,128)(2,1)S(1)} %get-tuple-element.22), channel_id=1, source_target_pairs={{0,8},{4,12},{8,0},{12,4},{16,24},{20,28},{24,16},{28,20},{1,9},{5... | collective-permute-start | bytes 589832 | tf_op jit(solution)/shard_map/ppermute | solution.py:197
  68.9 1.2 %collective-permute-start.15 = (bf16[2,128,384]{2,1,0:T(8,128)(2,1)S(1)}, bf16[2,128,384]{2,1,0:T(8,128)(2,1)S(1)}, u32[]{:S(2)}, u32[]{:S(2)}) collective-permute-start(bf16[2,128,384]{2,1,0:T(8,128)(2,1)S(1)} %get-tuple-element.23), channel_id=1, source_target_pairs={{0,16},{4,20},{8,24},{12,28},{16,0},{20,4},{24,8},{28,12},{1,17},{... | collective-permute-start | bytes 589832 | tf_op jit(solution)/shard_map/ppermute | solution.py:197
  70.5 2.1 %collective-permute-start.21 = (bf16[4,128,384]{2,1,0:T(8,128)(2,1)S(1)}, bf16[4,128,384]{2,1,0:T(8,128)(2,1)S(1)}, u32[]{:S(2)}, u32[]{:S(2)}) collective-permute-start(bf16[4,128,384]{2,1,0:T(8,128)(2,1)S(1)} %pad_maximum_fusion.6), channel_id=1, source_target_pairs={{0,4},{4,0},{8,12},{12,8},{16,20},{20,16},{24,28},{28,24},{1,5},{5... | collective-permute-start | bytes 1179656 | tf_op jit(solution)/shard_map/ppermute | solution.py:197
  74.1 3.9 %collective-permute-done.16.rest_3_ = bf16[2,128,384]{2,1,0:T(8,128)(2,1)S(1)} collective-permute-done((bf16[2,128,384]{2,1,0:T(8,128)(2,1)S(1)}, bf16[2,128,384]{2,1,0:T(8,128)(2,1)S(1)}, u32[]{:S(2)}, u32[]{:S(2)}) %collective-permute-start.16) | collective-permute-done | bytes 196640 | tf_op jit(solution)/shard_map/ppermute | solution.py:197
  78.1 2.5 %collective-permute-start.17 = (bf16[4,128,384]{2,1,0:T(8,128)(2,1)S(1)}, bf16[4,128,384]{2,1,0:T(8,128)(2,1)S(1)}, u32[]{:S(2)}, u32[]{:S(2)}) collective-permute-start(bf16[4,128,384]{2,1,0:T(8,128)(2,1)S(1)} %pad_maximum_fusion.5), channel_id=1, source_target_pairs={{0,4},{4,0},{8,12},{12,8},{16,20},{20,16},{24,28},{28,24},{1,5},{5... | collective-permute-start | bytes 1179656 | tf_op jit(solution)/shard_map/ppermute | solution.py:197
  80.6 1.3 %collective-permute-done.17.rest_4_ = bf16[4,128,384]{2,1,0:T(8,128)(2,1)S(1)} collective-permute-done((bf16[4,128,384]{2,1,0:T(8,128)(2,1)S(1)}, bf16[4,128,384]{2,1,0:T(8,128)(2,1)S(1)}, u32[]{:S(2)}, u32[]{:S(2)}) %collective-permute-start.17) | collective-permute-done | bytes 393248 | tf_op jit(solution)/shard_map/ppermute | solution.py:197
  81.9 1.8 %shard_map.59 = bf16[2048,384]{1,0:T(8,128)(2,1)} custom-call(s32[2]{0:T(128)S(1)} %pad_add_fusion.meta_ref, bf16[2,128,384]{2,1,0:T(8,128)(2,1)S(1)} %get-tuple-element.21.rest_0_, bf16[2,128,384]{2,1,0:T(8,128)(2,1)S(1)} %collective-permute-done.14.rest_1_, bf16[2,128,384]{2,1,0:T(8,128)(2,1)S(1)} %collective-permute-done.15.rest_2_, ...), custom_call_target="tpu_custom_call" | custom-call | bytes 3145728 | tf_op jit(solution)/shard_map/pallas_call | solution.py:175
  (69 shorter events, 12.0 us)
Async XLA Ops:
  2.4 20.7 %collective-permute-start.6 = (bf16[192,768]{1,0:T(8,128)(2,1)}, bf16[192,768]{1,0:T(8,128)(2,1)S(1)}, u32[]{:S(2)}, u32[]{:S(2)}) collective-permute-start(bf16[192,768]{1,0:T(8,128)(2,1)} %pad_maximum_fusion.7), channel_id=1, source_target_pairs={{0,3},{1,2},{2,1},{3,0},{4,7},{5,6},{6,5},{7,4},{8,11},{9,10},{10,... | collective-permute-start | bytes 884744 | tf_op jit(solution)/shard_map/ppermute | solution.py:200
  2.6 25.2 %collective-permute-start.2 = (bf16[192,768]{1,0:T(8,128)(2,1)}, bf16[192,768]{1,0:T(8,128)(2,1)S(1)}, u32[]{:S(2)}, u32[]{:S(2)}) collective-permute-start(bf16[192,768]{1,0:T(8,128)(2,1)} %pad_maximum_fusion.7), channel_id=1, source_target_pairs={{0,2},{1,3},{2,0},{3,1},{4,6},{5,7},{6,4},{7,5},{8,10},{9,11},{10,... | collective-permute-start | bytes 884744 | tf_op jit(solution)/shard_map/ppermute | solution.py:200
  7.9 36.1 %collective-permute-start = (bf16[384,768]{1,0:T(8,128)(2,1)}, bf16[384,768]{1,0:T(8,128)(2,1)S(1)}, u32[]{:S(2)}, u32[]{:S(2)}) collective-permute-start(bf16[384,768]{1,0:T(8,128)(2,1)} %pad_maximum_fusion.2), channel_id=1, source_target_pairs={{0,1},{1,0},{2,3},{3,2},{4,5},{5,4},{6,7},{7,6},{8,9},{9,8},{10,11... | collective-permute-start | bytes 1769480 | tf_op jit(solution)/shard_map/ppermute | solution.py:200
  13.3 2.6 %copy-start.5 = (f32[1536]{0:T(1024)S(1)}, f32[1536]{0:T(1024)}, u32[]{:S(2)}) copy-start(f32[1536]{0:T(1024)} %param.9) | copy-start | bytes 18436
  13.3 15.7 %collective-permute-start.10 = (bf16[2,256,384]{2,1,0:T(8,128)(2,1)S(1)}, bf16[2,256,384]{2,1,0:T(8,128)(2,1)S(1)}, u32[]{:S(2)}, u32[]{:S(2)}) collective-permute-start(bf16[2,256,384]{2,1,0:T(8,128)(2,1)S(1)} %get-tuple-element.18), channel_id=1, source_target_pairs={{0,8},{4,12},{8,0},{12,4},{16,24},{20,28},{24,16},{28,20},{1,9},{5... | collective-permute-start | bytes 1179656 | tf_op jit(solution)/shard_map/ppermute | solution.py:197
  14.6 15.8 %collective-permute-start.11 = (bf16[2,256,384]{2,1,0:T(8,128)(2,1)S(1)}, bf16[2,256,384]{2,1,0:T(8,128)(2,1)S(1)}, u32[]{:S(2)}, u32[]{:S(2)}) collective-permute-start(bf16[2,256,384]{2,1,0:T(8,128)(2,1)S(1)} %get-tuple-element.19), channel_id=1, source_target_pairs={{0,16},{4,20},{8,24},{12,28},{16,0},{20,4},{24,8},{28,12},{1,17},{... | collective-permute-start | bytes 1179656 | tf_op jit(solution)/shard_map/ppermute | solution.py:197
  23.2 8.8 %collective-permute-start.12 = (bf16[2,256,384]{2,1,0:T(8,128)(2,1)S(1)}, bf16[2,256,384]{2,1,0:T(8,128)(2,1)S(1)}, u32[]{:S(2)}, u32[]{:S(2)}) collective-permute-start(bf16[2,256,384]{2,1,0:T(8,128)(2,1)S(1)} %get-tuple-element.20), channel_id=1, source_target_pairs={{0,24},{4,28},{8,16},{12,20},{16,8},{20,12},{24,0},{28,4},{1,25},{... | collective-permute-start | bytes 1179656 | tf_op jit(solution)/shard_map/ppermute | solution.py:197
  27.8 7.4 %collective-permute-start.7 = (bf16[96,768]{1,0:T(8,128)(2,1)S(1)}, bf16[96,768]{1,0:T(8,128)(2,1)S(1)}, u32[]{:S(2)}, u32[]{:S(2)}) collective-permute-start(bf16[96,768]{1,0:T(8,128)(2,1)S(1)} %get-tuple-element.46), channel_id=1, source_target_pairs={{0,8},{4,12},{8,0},{12,4},{16,24},{20,28},{24,16},{28,20},{1,9},{5... | collective-permute-start | bytes 442376 | tf_op jit(solution)/shard_map/ppermute | solution.py:197
  29.0 11.5 %collective-permute-start.8 = (bf16[96,768]{1,0:T(8,128)(2,1)S(1)}, bf16[96,768]{1,0:T(8,128)(2,1)S(1)}, u32[]{:S(2)}, u32[]{:S(2)}) collective-permute-start(bf16[96,768]{1,0:T(8,128)(2,1)S(1)} %get-tuple-element.45), channel_id=1, source_target_pairs={{0,16},{4,20},{8,24},{12,28},{16,0},{20,4},{24,8},{28,12},{1,17},{... | collective-permute-start | bytes 442376 | tf_op jit(solution)/shard_map/ppermute | solution.py:197
  30.4 10.3 %collective-permute-start.3 = (bf16[96,768]{1,0:T(8,128)(2,1)S(1)}, bf16[96,768]{1,0:T(8,128)(2,1)S(1)}, u32[]{:S(2)}, u32[]{:S(2)}) collective-permute-start(bf16[96,768]{1,0:T(8,128)(2,1)S(1)} %get-tuple-element.48), channel_id=1, source_target_pairs={{0,8},{4,12},{8,0},{12,4},{16,24},{20,28},{24,16},{28,20},{1,9},{5... | collective-permute-start | bytes 442376 | tf_op jit(solution)/shard_map/ppermute | solution.py:197
  32.0 8.7 %collective-permute-start.4 = (bf16[96,768]{1,0:T(8,128)(2,1)S(1)}, bf16[96,768]{1,0:T(8,128)(2,1)S(1)}, u32[]{:S(2)}, u32[]{:S(2)}) collective-permute-start(bf16[96,768]{1,0:T(8,128)(2,1)S(1)} %get-tuple-element.47), channel_id=1, source_target_pairs={{0,16},{4,20},{8,24},{12,28},{16,0},{20,4},{24,8},{28,12},{1,17},{... | collective-permute-start | bytes 442376 | tf_op jit(solution)/shard_map/ppermute | solution.py:197
  35.2 9.0 %collective-permute-start.13 = (bf16[4,256,384]{2,1,0:T(8,128)(2,1)S(1)}, bf16[4,256,384]{2,1,0:T(8,128)(2,1)S(1)}, u32[]{:S(2)}, u32[]{:S(2)}) collective-permute-start(bf16[4,256,384]{2,1,0:T(8,128)(2,1)S(1)} %pad_maximum_fusion.1), channel_id=1, source_target_pairs={{0,4},{4,0},{8,12},{12,8},{16,20},{20,16},{24,28},{28,24},{1,5},{5... | collective-permute-start | bytes 2359304 | tf_op jit(solution)/shard_map/ppermute | solution.py:197
  40.6 3.7 %collective-permute-start.9 = (bf16[384,768]{1,0:T(8,128)(2,1)S(1)}, bf16[384,768]{1,0:T(8,128)(2,1)S(1)}, u32[]{:S(2)}, u32[]{:S(2)}) collective-permute-start(bf16[384,768]{1,0:T(8,128)(2,1)S(1)} %pad_maximum_fusion.4), channel_id=1, source_target_pairs={{0,4},{4,0},{8,12},{12,8},{16,20},{20,16},{24,28},{28,24},{1,5},{5... | collective-permute-start | bytes 1769480 | tf_op jit(solution)/shard_map/ppermute | solution.py:197
  40.8 4.9 %collective-permute-start.5 = (bf16[384,768]{1,0:T(8,128)(2,1)S(1)}, bf16[384,768]{1,0:T(8,128)(2,1)S(1)}, u32[]{:S(2)}, u32[]{:S(2)}) collective-permute-start(bf16[384,768]{1,0:T(8,128)(2,1)S(1)} %pad_maximum_fusion.3), channel_id=1, source_target_pairs={{0,4},{4,0},{8,12},{12,8},{16,20},{20,16},{24,28},{28,24},{1,5},{5... | collective-permute-start | bytes 1769480 | tf_op jit(solution)/shard_map/ppermute | solution.py:197
  44.0 2.5 %collective-permute-start.1 = (bf16[384,768]{1,0:T(8,128)(2,1)S(1)}, bf16[384,768]{1,0:T(8,128)(2,1)S(1)}, u32[]{:S(2)}, u32[]{:S(2)}) collective-permute-start(bf16[384,768]{1,0:T(8,128)(2,1)S(1)} %collective-permute-done.rest_0_), channel_id=1, source_target_pairs={{0,4},{4,0},{8,12},{12,8},{16,20},{20,16},{24,28},{28,24},{1,5},{5... | collective-permute-start | bytes 1769480 | tf_op jit(solution)/shard_map/ppermute | solution.py:197
  44.1 2.3 %copy-start = (bf16[192,1536]{1,0:T(8,128)(2,1)S(1)}, bf16[192,1536]{1,0:T(8,128)(2,1)}, u32[]{:S(2)}) copy-start(bf16[192,1536]{1,0:T(8,128)(2,1)} %in_ref.1) | copy-start | bytes 1769476
  56.2 13.9 %collective-permute-start.18 = (bf16[2,128,384]{2,1,0:T(8,128)(2,1)S(1)}, bf16[2,128,384]{2,1,0:T(8,128)(2,1)S(1)}, u32[]{:S(2)}, u32[]{:S(2)}) collective-permute-start(bf16[2,128,384]{2,1,0:T(8,128)(2,1)S(1)} %get-tuple-element.26), channel_id=1, source_target_pairs={{0,8},{4,12},{8,0},{12,4},{16,24},{20,28},{24,16},{28,20},{1,9},{5... | collective-permute-start | bytes 589832 | tf_op jit(solution)/shard_map/ppermute | solution.py:197
  57.5 12.9 %collective-permute-start.19 = (bf16[2,128,384]{2,1,0:T(8,128)(2,1)S(1)}, bf16[2,128,384]{2,1,0:T(8,128)(2,1)S(1)}, u32[]{:S(2)}, u32[]{:S(2)}) collective-permute-start(bf16[2,128,384]{2,1,0:T(8,128)(2,1)S(1)} %get-tuple-element.27), channel_id=1, source_target_pairs={{0,16},{4,20},{8,24},{12,28},{16,0},{20,4},{24,8},{28,12},{1,17},{... | collective-permute-start | bytes 589832 | tf_op jit(solution)/shard_map/ppermute | solution.py:197
  58.7 11.7 %collective-permute-start.20 = (bf16[2,128,384]{2,1,0:T(8,128)(2,1)S(1)}, bf16[2,128,384]{2,1,0:T(8,128)(2,1)S(1)}, u32[]{:S(2)}, u32[]{:S(2)}) collective-permute-start(bf16[2,128,384]{2,1,0:T(8,128)(2,1)S(1)} %get-tuple-element.28), channel_id=1, source_target_pairs={{0,24},{4,28},{8,16},{12,20},{16,8},{20,12},{24,0},{28,4},{1,25},{... | collective-permute-start | bytes 589832 | tf_op jit(solution)/shard_map/ppermute | solution.py:197
  67.6 5.2 %collective-permute-start.14 = (bf16[2,128,384]{2,1,0:T(8,128)(2,1)S(1)}, bf16[2,128,384]{2,1,0:T(8,128)(2,1)S(1)}, u32[]{:S(2)}, u32[]{:S(2)}) collective-permute-start(bf16[2,128,384]{2,1,0:T(8,128)(2,1)S(1)} %get-tuple-element.22), channel_id=1, source_target_pairs={{0,8},{4,12},{8,0},{12,4},{16,24},{20,28},{24,16},{28,20},{1,9},{5... | collective-permute-start | bytes 589832 | tf_op jit(solution)/shard_map/ppermute | solution.py:197
  68.9 5.2 %collective-permute-start.15 = (bf16[2,128,384]{2,1,0:T(8,128)(2,1)S(1)}, bf16[2,128,384]{2,1,0:T(8,128)(2,1)S(1)}, u32[]{:S(2)}, u32[]{:S(2)}) collective-permute-start(bf16[2,128,384]{2,1,0:T(8,128)(2,1)S(1)} %get-tuple-element.23), channel_id=1, source_target_pairs={{0,16},{4,20},{8,24},{12,28},{16,0},{20,4},{24,8},{28,12},{1,17},{... | collective-permute-start | bytes 589832 | tf_op jit(solution)/shard_map/ppermute | solution.py:197
  70.1 7.9 %collective-permute-start.16 = (bf16[2,128,384]{2,1,0:T(8,128)(2,1)S(1)}, bf16[2,128,384]{2,1,0:T(8,128)(2,1)S(1)}, u32[]{:S(2)}, u32[]{:S(2)}) collective-permute-start(bf16[2,128,384]{2,1,0:T(8,128)(2,1)S(1)} %get-tuple-element.24), channel_id=1, source_target_pairs={{0,24},{4,28},{8,16},{12,20},{16,8},{20,12},{24,0},{28,4},{1,25},{... | collective-permute-start | bytes 589832 | tf_op jit(solution)/shard_map/ppermute | solution.py:197
  70.5 10.1 %collective-permute-start.21 = (bf16[4,128,384]{2,1,0:T(8,128)(2,1)S(1)}, bf16[4,128,384]{2,1,0:T(8,128)(2,1)S(1)}, u32[]{:S(2)}, u32[]{:S(2)}) collective-permute-start(bf16[4,128,384]{2,1,0:T(8,128)(2,1)S(1)} %pad_maximum_fusion.6), channel_id=1, source_target_pairs={{0,4},{4,0},{8,12},{12,8},{16,20},{20,16},{24,28},{28,24},{1,5},{5... | collective-permute-start | bytes 1179656 | tf_op jit(solution)/shard_map/ppermute | solution.py:197
  78.1 3.8 %collective-permute-start.17 = (bf16[4,128,384]{2,1,0:T(8,128)(2,1)S(1)}, bf16[4,128,384]{2,1,0:T(8,128)(2,1)S(1)}, u32[]{:S(2)}, u32[]{:S(2)}) collective-permute-start(bf16[4,128,384]{2,1,0:T(8,128)(2,1)S(1)} %pad_maximum_fusion.5), channel_id=1, source_target_pairs={{0,4},{4,0},{8,12},{12,8},{16,20},{20,16},{24,28},{28,24},{1,5},{5... | collective-permute-start | bytes 1179656 | tf_op jit(solution)/shard_map/ppermute | solution.py:197
  (4 other events, 6.7 us)

commit v3 on v2

--- a/solution.py
+++ b/solution.py
@@ -12,7 +12,8 @@
 CHIPS = MEMBERS // 2
 LEVELS = 3
 MODES = {1: 'S1', 2: 'S2', 3: 'S2'}
-GROUPS = 2
+CHIP_ORDER = (3, 1, 2)
+PARTS = (5, 3)
 LANES = 128
 INV_SQRT2 = np.float32(np.sqrt(0.5))
 
@@ -29,14 +30,14 @@
     return pl.CostEstimate(flops=int(flops), bytes_accessed=int(moved), transcendentals=0)
 
 
-def gather_kernel(meta_ref, order_ref, features_ref, *rest):
-    out_refs, hot_ref = rest[:CHIPS], rest[CHIPS]
+def gather_kernel(chips, meta_ref, order_ref, features_ref, *rest):
+    out_refs, hot_ref = rest[:-1], rest[-1]
     rows, width = features_ref.shape
     share = rows // MEMBERS
     tiles = share // LANES
     me = meta_ref[0]
     lane = lax.broadcasted_iota(jnp.int32, (LANES, LANES), 1)
-    for chip in range(CHIPS):
+    for out_ref, chip in zip(out_refs, chips, strict=True):
         for n in range(2 * tiles):
             member = jnp.bitwise_xor(me, 2 * chip + n // tiles)
             taken = order_ref[pl.ds(member * tiles + n % tiles, 1), :]
@@ -45,20 +46,20 @@
                 hit = jnp.where(column == lane + j * LANES, 1.0, 0.0)
                 hot_ref[n * LANES : (n + 1) * LANES, j * LANES : (j + 1) * LANES] = hit.astype(jnp.bfloat16)
         found = jnp.dot(hot_ref[...], features_ref[...], preferred_element_type=jnp.float32)
-        out_refs[chip][...] = found.astype(jnp.bfloat16).reshape(2, share, width)
-
-
-def gather(meta, order, features):
+        out_ref[...] = found.astype(jnp.bfloat16).reshape(2, share, width)
+
+
+def gather(chips, meta, order, features):
     rows, width = features.shape
     share = rows // MEMBERS
     return pl.pallas_call(
-        gather_kernel,
-        out_shape=[jax.ShapeDtypeStruct((2, share, width), features.dtype)] * CHIPS,
+        functools.partial(gather_kernel, chips),
+        out_shape=[jax.ShapeDtypeStruct((2, share, width), features.dtype)] * len(chips),
         in_specs=[SMEM, VMEM, VMEM],
-        out_specs=[VMEM] * CHIPS,
+        out_specs=[VMEM] * len(chips),
         scratch_shapes=[pltpu.VMEM((2 * share, rows), features.dtype)],
         compiler_params=limits(32),
-        cost_estimate=cost(2 * rows * rows * width, 4 * rows * width),
+        cost_estimate=cost(4 * len(chips) * share * rows * width, 4 * rows * width),
     )(meta, order, features)
 
 
@@ -147,40 +148,37 @@
     )(meta, weights, bias, *blocks, others)
 
 
-def finish_kernel(meta_ref, *rest):
-    arrays, out_ref, sems = rest[:-2], rest[-2], rest[-1]
-    per_group = CHIPS + 1
-    rows = arrays[0].shape[1]
-    share = rows * (len(arrays) // per_group)
+def finish_kernel(first_row, share, meta_ref, *rest):
+    held, other, (out_ref, sems) = rest[:CHIPS], rest[CHIPS], rest[-2:]
+    rows = other.shape[1]
     me = meta_ref[0]
     copies = []
 
-    def put(src, member, group):
-        dst = out_ref.at[pl.ds(pl.multiple_of(member * share + group * rows, 16), rows), :]
+    def put(src, member):
+        dst = out_ref.at[pl.ds(pl.multiple_of(member * share + first_row, 16), rows), :]
         copies.append(pltpu.make_async_copy(src, dst, sems.at[len(copies)]))
         copies[-1].start()
 
-    for group in range(len(arrays) // per_group):
-        held = arrays[group * per_group : (group + 1) * per_group]
-        for c in range(CHIPS):
-            put(held[c].at[0], jnp.bitwise_xor(me, 2 * c), group)
-            put(held[CHIPS].at[c], jnp.bitwise_xor(me, 2 * c + 1), group)
+    for c in range(CHIPS):
+        put(held[c].at[0], jnp.bitwise_xor(me, 2 * c))
+        put(other.at[c], jnp.bitwise_xor(me, 2 * c + 1))
     for copy in copies:
         copy.wait()
 
 
-def finish(meta, arrays):
+def finish(meta, first_row, share, arrays, out):
     _, rows, width = arrays[0].shape
-    n_blocks = len(arrays) // (CHIPS + 1) * MEMBERS
+    given = [] if out is None else [out]
     return pl.pallas_call(
-        finish_kernel,
-        out_shape=jax.ShapeDtypeStruct((rows * n_blocks, width), arrays[0].dtype),
-        in_specs=[SMEM] + [VMEM] * len(arrays),
+        functools.partial(finish_kernel, first_row, share),
+        out_shape=jax.ShapeDtypeStruct((share * MEMBERS, width), arrays[0].dtype),
+        in_specs=[SMEM] + [VMEM] * len(arrays) + [ANY] * len(given),
         out_specs=ANY,
-        scratch_shapes=[pltpu.SemaphoreType.DMA((n_blocks,))],
+        scratch_shapes=[pltpu.SemaphoreType.DMA((MEMBERS,))],
+        input_output_aliases={1 + len(arrays): 0} if given else {},
         compiler_params=limits(16),
-        cost_estimate=cost(0, 4 * rows * n_blocks * width),
-    )(meta, *arrays)
+        cost_estimate=cost(0, 4 * rows * MEMBERS * width),
+    )(meta, *arrays, *given)
 
 
 def body(features, row_order, switch_in, switch_out, hidden_bias):
@@ -188,7 +186,7 @@
     log_pos = n_pos.bit_length() - 1
     bits = (0, log_pos // 2, log_pos - 1)
     rows = features.shape[0]
-    assert len(set(bits)) == LEVELS and rows % (GROUPS * MEMBERS * LANES) == 0
+    assert len(set(bits)) == LEVELS and rows % (MEMBERS * LANES) == 0
 
     def spread(k):
         return sum(((k >> j) & 1) << bit for j, bit in enumerate(bits))
@@ -203,15 +201,13 @@
     me = sum(((here >> bit) & 1) << j for j, bit in enumerate(bits))
     meta = jnp.stack([me, lax.axis_index("wt")]).astype(jnp.int32)
 
-    half = switch_in.shape[1] // 2
-    quarter = jnp.concatenate([switch_in[:, :half], switch_in[:, half:], switch_out], axis=0)
-    depth, total = switch_in.shape[0], quarter.shape[0]
-    assert total == 4 * depth
-
-    eighth_rows = total // MEMBERS
+    depth, half = switch_in.shape[0], switch_in.shape[1] // 2
+    total = 4 * depth
+    assert switch_out.shape == (2 * depth, half)
+    eighth_rows = depth // 2
 
     def halves(me):
-        return [((me & 1) * (total // 2) + n * depth, depth) for n in range(2)]
+        return [((me & 1) * depth + n * 2 * depth, depth) for n in range(2)]
 
     def eighth(me):
         return [(me * eighth_rows, eighth_rows)]
@@ -222,10 +218,6 @@
     def right(me):
         return [(total // 2 + ((me >> 2) & 1) * 2 * eighth_rows + (me & 1) * eighth_rows, eighth_rows)]
 
-    def cut(*pieces):
-        taken = [lax.dynamic_slice_in_dim(quarter, row, size, axis=0) for p in pieces for row, size in p(me)]
-        return jnp.concatenate(taken, axis=0) if len(taken) > 1 else taken[0]
-
     def after(x, *earlier):
         return lax.optimization_barrier((x, earlier))[0]
 
@@ -234,10 +226,25 @@
 
     share = rows // MEMBERS
     kinds = {"S1": (halves,), "S2": (left, right), "S4": (eighth,)}
-    sources = {mode: cut(*kinds[mode]) for mode in sorted(set(MODES.values()))}
+    core, chip_x, chip_y = [(me >> n) & 1 for n in range(LEVELS)]
+    far = jnp.concatenate(
+        [
+            lax.dynamic_slice(switch_in, (core * eighth_rows, chip_x * half), (eighth_rows, half)),
+            lax.dynamic_slice_in_dim(switch_out, (2 * chip_y + core) * eighth_rows, eighth_rows),
+        ]
+    )
+    near = jnp.concatenate(
+        [
+            lax.dynamic_slice(switch_in, (0, core * half), (depth, half)),
+            lax.dynamic_slice_in_dim(switch_out, core * depth, depth),
+        ]
+    )
+    sources = {"S1": near, "S2": far}
+    order = row_order.reshape(rows // LANES, LANES)
 
     def cross(pairs):
-        pairs = [pairs[0]] + [swap_pos(pairs[c], 2 * c) for c in range(1, CHIPS)]
+        moved = {c: swap_pos(pairs[c], 2 * c) for c in CHIP_ORDER}
+        pairs = [pairs[0]] + [moved[c] for c in range(1, CHIPS)]
         return pairs, swap_pos(jnp.stack([p[1] for p in pairs]), 1)
 
     parts, plan = [], []
@@ -266,26 +273,27 @@
         src = sources[MODES[k]]
         return swap_wt(after(src, *deps) if deps else src, k)
 
-    def gather_all():
-        return gather(meta, row_order.reshape(rows // LANES, LANES), features)
-
-    size = share // GROUPS
+    cuts = [sum(PARTS[:g]) * share // sum(PARTS) for g in range(len(PARTS) + 1)]
 
     def halve(first):
-        return [([p[:, g * size : (g + 1) * size] for p in first[0]], first[1][:, g * size : (g + 1) * size]) for g in range(GROUPS)]
-
-    owned = {k: get(k) for k in range(1, n_wt)}
-    first = cross(gather_all())
+        spans = [slice(low, high) for low, high in zip(cuts, cuts[1:])]
+        return [([p[:, span] for p in first[0]], first[1][:, span]) for span in spans]
+
+    owned = {k: get(k) for k in range(1, n_wt) if k != 2}
+    owned[2] = get(2, owned[3])
+    away = gather((1, 2, 3), meta, order, features)
+    own = gather((0,), meta, order, features)
+    first = cross(own + away)
     for k in range(1, n_wt):
         spread_parts([(k, owned[k])])
     split = halve(first)
     weights = place(n_wt, plan, meta, switch_in, switch_out, parts)
     bias = hidden_bias.reshape(1, -1)
-    done = []
-    for group in range(GROUPS):
-        kept, received = cross(run_levels(meta, weights, bias, *split[group]))
-        done += kept + [received]
-    return finish(meta, done)
+    out = None
+    for group, (blocks, others) in enumerate(split):
+        kept, received = cross(run_levels(meta, weights, bias, blocks, others))
+        out = finish(meta, cuts[group], share, [*kept, received], out)
+    return out
 
 
 def solution(mesh):

time: 84.1 us -> 81.3 us (0.967)
  the two profiles are of different devices: /device:TPU:17 before, /device:TPU:0 now
where the time goes in v3:
time: 81.3 us; the launch traced here: 81 us
  Pallas kernels  27.6 us (34%)
  starting transfers between devices  25.6 us (31%)
  waiting for transfers between devices  19.5 us (24%)
  local copies, waits for them, and re-layouts  6.6 us (8%)
  other arithmetic  1.18 us (1%)
    ppermute x19, waiting for transfers between devices, swap_pos(): return lax.ppermute(x, 'pos', [(i, i ^ spread(k)) for i in range(n_pos)])  19.5 us
    pallas_call x2, Pallas kernels, run_levels(): pl.pallas_call(levels_kernel, out_shape=[jax.ShapeDtypeStruct((2, rows, w...  17.5 us
    ppermute x19, starting transfers between devices, swap_pos(): return lax.ppermute(x, 'pos', [(i, i ^ spread(k)) for i in range(n_pos)])  15.7 us
    ppermute x3, starting transfers between devices, swap_wt(): return lax.ppermute(x, 'wt', [(i, i ^ k) for i in range(n_wt)])  9.87 us
    pallas_call x2, Pallas kernels, gather(): pl.pallas_call(functools.partial(gather_kernel, chips), out_shape=[jax.Sh...  6.24 us
    pallas_call x2, Pallas kernels, finish(): pl.pallas_call(functools.partial(finish_kernel, first_row, share), out_sh...  2.97 us
    slice x8, local copies, waits for them, and re-layouts, halve(): p[:, span]  2.03 us
  transfers between devices with their start and end apart: 22, of which 6 were waited for; matrix products, arithmetic and copies ran while one was open for 5% of the time, Pallas kernels for 18%

profile of v3, /device:TPU:0, one launch (start us, length us, event | category | flops | bytes accessed | tf_op | source)
XLA Modules:
  0.0 81.0 jit_solution(8754081055804562561)
XLA Ops:
  2.6 5.0 %collective-permute-start.2 = (bf16[192,768]{1,0:T(8,128)(2,1)}, bf16[192,768]{1,0:T(8,128)(2,1)S(1)}, u32[]{:S(2)}, u32[]{:S(2)}) collective-permute-start(bf16[192,768]{1,0:T(8,128)(2,1)} %pad_maximum_fusion.5), channel_id=1, source_target_pairs={{0,3},{1,2},{2,1},{3,0},{4,7},{5,6},{6,5},{7,4},{8,11},{9,10},{10,... | collective-permute-start | bytes 884744 | tf_op jit(solution)/shard_map/ppermute | solution.py:198
  7.7 1.4 %copy-done.2 = bf16[2048,384]{1,0:T(8,128)(2,1)S(1)} copy-done((bf16[2048,384]{1,0:T(8,128)(2,1)S(1)}, bf16[2048,384]{1,0:T(8,128)(2,1)}, u32[]{:S(2)}) %copy-start.2) | copy-done | bytes 1572888
  9.1 4.3 %shard_map.57 = (bf16[2,256,384]{2,1,0:T(8,128)(2,1)S(1)}, bf16[2,256,384]{2,1,0:T(8,128)(2,1)S(1)}, bf16[2,256,384]{2,1,0:T(8,128)(2,1)S(1)}) custom-call(s32[2]{0:T(128)S(1)} %pad_add_fusion.meta_ref, s32[16,128]{1,0:T(8,128)S(1)} %bitcast.3, bf16[2048,384]{1,0:T(8,128)(2,1)S(1)} %copy-done.2), custom_call_target="tpu_custom_call" | custom-call | flops 2415919104 | bytes 3145728 | tf_op jit(solution)/shard_map/pallas_call | solution.py:55
  13.4 1.6 %collective-permute-start.10 = (bf16[2,256,384]{2,1,0:T(8,128)(2,1)S(1)}, bf16[2,256,384]{2,1,0:T(8,128)(2,1)S(1)}, u32[]{:S(2)}, u32[]{:S(2)}) collective-permute-start(bf16[2,256,384]{2,1,0:T(8,128)(2,1)S(1)} %get-tuple-element.18), channel_id=1, source_target_pairs={{0,8},{4,12},{8,0},{12,4},{16,24},{20,28},{24,16},{28,20},{1,9},{5... | collective-permute-start | bytes 1179656 | tf_op jit(solution)/shard_map/ppermute | solution.py:195
  15.0 1.5 %collective-permute-start.11 = (bf16[2,256,384]{2,1,0:T(8,128)(2,1)S(1)}, bf16[2,256,384]{2,1,0:T(8,128)(2,1)S(1)}, u32[]{:S(2)}, u32[]{:S(2)}) collective-permute-start(bf16[2,256,384]{2,1,0:T(8,128)(2,1)S(1)} %get-tuple-element.19), channel_id=1, source_target_pairs={{0,16},{4,20},{8,24},{12,28},{16,0},{20,4},{24,8},{28,12},{1,17},{... | collective-permute-start | bytes 1179656 | tf_op jit(solution)/shard_map/ppermute | solution.py:195
  17.2 4.8 %collective-permute-start.3 = (bf16[192,768]{1,0:T(8,128)(2,1)}, bf16[192,768]{1,0:T(8,128)(2,1)S(1)}, u32[]{:S(2)}, u32[]{:S(2)}) collective-permute-start(bf16[192,768]{1,0:T(8,128)(2,1)} %pad_maximum_fusion.5), channel_id=1, source_target_pairs={{0,2},{1,3},{2,0},{3,1},{4,6},{5,7},{6,4},{7,5},{8,10},{9,11},{10,... | collective-permute-start | bytes 884744 | tf_op jit(solution)/shard_map/ppermute | solution.py:198
  21.9 2.0 %shard_map.56 = bf16[2,256,384]{2,1,0:T(8,128)(2,1)S(1)} custom-call(s32[2]{0:T(128)S(1)} %pad_add_fusion.meta_ref, s32[16,128]{1,0:T(8,128)S(1)} %bitcast.4, bf16[2048,384]{1,0:T(8,128)(2,1)S(1)} %copy-done.3), custom_call_target="tpu_custom_call" | custom-call | flops 805306368 | bytes 3145728 | tf_op jit(solution)/shard_map/pallas_call | solution.py:55
  24.0 9.7 %collective-permute-done.12 = bf16[2,256,384]{2,1,0:T(8,128)(2,1)} collective-permute-done((bf16[2,256,384]{2,1,0:T(8,128)(2,1)S(1)}, bf16[2,256,384]{2,1,0:T(8,128)(2,1)}, u32[]{:S(2)}, u32[]{:S(2)}) %collective-permute-start.12) | collective-permute-done | bytes 393248 | tf_op jit(solution)/shard_map/ppermute | solution.py:195
  33.7 1.4 %collective-permute-start.7 = (bf16[96,768]{1,0:T(8,128)(2,1)S(1)}, bf16[96,768]{1,0:T(8,128)(2,1)S(1)}, u32[]{:S(2)}, u32[]{:S(2)}) collective-permute-start(bf16[96,768]{1,0:T(8,128)(2,1)S(1)} %get-tuple-element.30), channel_id=1, source_target_pairs={{0,8},{4,12},{8,0},{12,4},{16,24},{20,28},{24,16},{28,20},{1,9},{5... | collective-permute-start | bytes 442376 | tf_op jit(solution)/shard_map/ppermute | solution.py:195
  35.1 0.9 %slice.115 = bf16[1,256,384]{2,1,0:T(8,128)(2,1)S(1)} slice(bf16[2,256,384]{2,1,0:T(8,128)(2,1)} %collective-permute-done.12), slice={[1:2], [0:256], [0:384]} | slice | bytes 393216 | tf_op jit(solution)/shard_map/slice | solution.py:248
  37.4 1.5 %collective-permute-start.5 = (bf16[96,768]{1,0:T(8,128)(2,1)S(1)}, bf16[96,768]{1,0:T(8,128)(2,1)S(1)}, u32[]{:S(2)}, u32[]{:S(2)}) collective-permute-start(bf16[96,768]{1,0:T(8,128)(2,1)S(1)} %get-tuple-element.31), channel_id=1, source_target_pairs={{0,16},{4,20},{8,24},{12,28},{16,0},{20,4},{24,8},{28,12},{1,17},{... | collective-permute-start | bytes 442376 | tf_op jit(solution)/shard_map/ppermute | solution.py:195
  39.0 1.1 %collective-permute-done.7.rest_7_ = bf16[96,768]{1,0:T(8,128)(2,1)S(1)} collective-permute-done((bf16[96,768]{1,0:T(8,128)(2,1)S(1)}, bf16[96,768]{1,0:T(8,128)(2,1)S(1)}, u32[]{:S(2)}, u32[]{:S(2)}) %collective-permute-start.7) | collective-permute-done | bytes 147488 | tf_op jit(solution)/shard_map/ppermute | solution.py:195
  40.1 1.6 %collective-permute-done.8.rest_8_ = bf16[96,768]{1,0:T(8,128)(2,1)S(1)} collective-permute-done((bf16[96,768]{1,0:T(8,128)(2,1)S(1)}, bf16[96,768]{1,0:T(8,128)(2,1)S(1)}, u32[]{:S(2)}, u32[]{:S(2)}) %collective-permute-start.8) | collective-permute-done | bytes 147488 | tf_op jit(solution)/shard_map/ppermute | solution.py:195
  44.6 1.0 %slice.123.rest_3_ = bf16[2,160,384]{2,1,0:T(8,128)(2,1)S(1)} slice(bf16[2,256,384]{2,1,0:T(8,128)(2,1)} %collective-permute-done.12), slice={[0:2], [0:160], [0:384]} | slice | bytes 491520 | tf_op jit(solution)/shard_map/slice | solution.py:280
  46.6 10.7 %shard_map.59 = (bf16[2,160,384]{2,1,0:T(8,128)(2,1)S(1)}, bf16[2,160,384]{2,1,0:T(8,128)(2,1)S(1)}, bf16[2,160,384]{2,1,0:T(8,128)(2,1)S(1)}, bf16[2,160,384]{2,1,0:T(8,128)(2,1)S(1)}) custom-call(s32[2]{0:T(128)S(1)} %pad_add_fusion.meta_ref, bf16[3072,768]{1,0:T(8,128)(2,1)S(1)} %shard_map.55.weights_ref, f32[1,1536]{1,0:T(1,128)S(1)} %reshape.6.bias_ref, ...), custom_call_target="tpu_custom_call" | custom-call | flops 9059696640 | bytes 4718592 | tf_op jit(solution)/shard_map/pallas_call | solution.py:140
  58.0 1.4 %collective-permute-start.19 = (bf16[2,160,384]{2,1,0:T(8,128)(2,1)S(1)}, bf16[2,160,384]{2,1,0:T(8,128)(2,1)S(1)}, u32[]{:S(2)}, u32[]{:S(2)}) collective-permute-start(bf16[2,160,384]{2,1,0:T(8,128)(2,1)S(1)} %get-tuple-element.27), channel_id=1, source_target_pairs={{0,16},{4,20},{8,24},{12,28},{16,0},{20,4},{24,8},{28,12},{1,17},{... | collective-permute-start | bytes 737288 | tf_op jit(solution)/shard_map/ppermute | solution.py:195
  59.4 1.4 %collective-permute-start.20 = (bf16[2,160,384]{2,1,0:T(8,128)(2,1)S(1)}, bf16[2,160,384]{2,1,0:T(8,128)(2,1)S(1)}, u32[]{:S(2)}, u32[]{:S(2)}) collective-permute-start(bf16[2,160,384]{2,1,0:T(8,128)(2,1)S(1)} %get-tuple-element.28), channel_id=1, source_target_pairs={{0,24},{4,28},{8,16},{12,20},{16,8},{20,12},{24,0},{28,4},{1,25},{... | collective-permute-start | bytes 737288 | tf_op jit(solution)/shard_map/ppermute | solution.py:195
  60.8 6.8 %shard_map.58 = (bf16[2,96,384]{2,1,0:T(8,128)(2,1)S(1)}, bf16[2,96,384]{2,1,0:T(8,128)(2,1)S(1)}, bf16[2,96,384]{2,1,0:T(8,128)(2,1)S(1)}, bf16[2,96,384]{2,1,0:T(8,128)(2,1)S(1)}) custom-call(s32[2]{0:T(128)S(1)} %pad_add_fusion.meta_ref, bf16[3072,768]{1,0:T(8,128)(2,1)S(1)} %shard_map.55.weights_ref, f32[1,1536]{1,0:T(1,128)S(1)} %reshape.6.bias_ref, ...), custom_call_target="tpu_custom_call" | custom-call | flops 5435817984 | bytes 4718592 | tf_op jit(solution)/shard_map/pallas_call | solution.py:140
  68.4 1.4 %collective-permute-start.15 = (bf16[2,96,384]{2,1,0:T(8,128)(2,1)S(1)}, bf16[2,96,384]{2,1,0:T(8,128)(2,1)S(1)}, u32[]{:S(2)}, u32[]{:S(2)}) collective-permute-start(bf16[2,96,384]{2,1,0:T(8,128)(2,1)S(1)} %get-tuple-element.23), channel_id=1, source_target_pairs={{0,16},{4,20},{8,24},{12,28},{16,0},{20,4},{24,8},{28,12},{1,17},{... | collective-permute-start | bytes 442376 | tf_op jit(solution)/shard_map/ppermute | solution.py:195
  69.8 1.7 %collective-permute-done.20.rest_3_ = bf16[2,160,384]{2,1,0:T(8,128)(2,1)S(1)} collective-permute-done((bf16[2,160,384]{2,1,0:T(8,128)(2,1)S(1)}, bf16[2,160,384]{2,1,0:T(8,128)(2,1)S(1)}, u32[]{:S(2)}, u32[]{:S(2)}) %collective-permute-start.20) | collective-permute-done | bytes 245792 | tf_op jit(solution)/shard_map/ppermute | solution.py:195
  71.5 1.4 %collective-permute-start.16 = (bf16[2,96,384]{2,1,0:T(8,128)(2,1)S(1)}, bf16[2,96,384]{2,1,0:T(8,128)(2,1)S(1)}, u32[]{:S(2)}, u32[]{:S(2)}) collective-permute-start(bf16[2,96,384]{2,1,0:T(8,128)(2,1)S(1)} %get-tuple-element.24), channel_id=1, source_target_pairs={{0,24},{4,28},{8,16},{12,20},{16,8},{20,12},{24,0},{28,4},{1,25},{... | collective-permute-start | bytes 442376 | tf_op jit(solution)/shard_map/ppermute | solution.py:195
  73.2 4.4 %collective-permute-done.16.rest_3_ = bf16[2,96,384]{2,1,0:T(8,128)(2,1)S(1)} collective-permute-done((bf16[2,96,384]{2,1,0:T(8,128)(2,1)S(1)}, bf16[2,96,384]{2,1,0:T(8,128)(2,1)S(1)}, u32[]{:S(2)}, u32[]{:S(2)}) %collective-permute-start.16) | collective-permute-done | bytes 147488 | tf_op jit(solution)/shard_map/ppermute | solution.py:195
  77.9 1.5 %shard_map.60.rest_5_ = bf16[2048,384]{1,0:T(8,128)(2,1)} custom-call(s32[2]{0:T(128)S(1)} %pad_add_fusion.meta_ref, bf16[2,160,384]{2,1,0:T(8,128)(2,1)S(1)} %get-tuple-element.25.rest_0_, bf16[2,160,384]{2,1,0:T(8,128)(2,1)S(1)} %collective-permute-done.18.rest_1_, bf16[2,160,384]{2,1,0:T(8,128)(2,1)S(1)} %collective-permute-done.19.rest_2_, ...), custom_call_target="tpu_custom_call" | custom-call | bytes 1966080 | tf_op jit(solution)/shard_map/pallas_call | solution.py:172
  79.4 1.4 %shard_map.61 = bf16[2048,384]{1,0:T(8,128)(2,1)} custom-call(s32[2]{0:T(128)S(1)} %pad_add_fusion.meta_ref, bf16[2,96,384]{2,1,0:T(8,128)(2,1)S(1)} %get-tuple-element.21.rest_0_, bf16[2,96,384]{2,1,0:T(8,128)(2,1)S(1)} %collective-permute-done.14.rest_1_, bf16[2,96,384]{2,1,0:T(8,128)(2,1)S(1)} %collective-permute-done.15.rest_2_, ...), custom_call_target="tpu_custom_call", output_to_operand_aliasing={{}: (6, {})} | custom-call | bytes 1179648 | tf_op jit(solution)/shard_map/pallas_call | solution.py:172
  (75 shorter events, 10.4 us)
Async XLA Ops:
  2.6 14.6 %collective-permute-start.2 = (bf16[192,768]{1,0:T(8,128)(2,1)}, bf16[192,768]{1,0:T(8,128)(2,1)S(1)}, u32[]{:S(2)}, u32[]{:S(2)}) collective-permute-start(bf16[192,768]{1,0:T(8,128)(2,1)} %pad_maximum_fusion.5), channel_id=1, source_target_pairs={{0,3},{1,2},{2,1},{3,0},{4,7},{5,6},{6,5},{7,4},{8,11},{9,10},{10,... | collective-permute-start | bytes 884744 | tf_op jit(solution)/shard_map/ppermute | solution.py:198
  9.1 7.8 %copy-start = (bf16[192,1536]{1,0:T(8,128)(2,1)S(1)}, bf16[192,1536]{1,0:T(8,128)(2,1)}, u32[]{:S(2)}) copy-start(bf16[192,1536]{1,0:T(8,128)(2,1)} %in_ref.1) | copy-start | bytes 1769476
  9.1 7.8 %copy-start.1 = (bf16[384,768]{1,0:T(8,128)(2,1)S(1)}, bf16[384,768]{1,0:T(8,128)(2,1)}, u32[]{:S(2)}) copy-start(bf16[384,768]{1,0:T(8,128)(2,1)} %out_ref.1) | copy-start | bytes 1769476
  13.4 23.3 %collective-permute-start.10 = (bf16[2,256,384]{2,1,0:T(8,128)(2,1)S(1)}, bf16[2,256,384]{2,1,0:T(8,128)(2,1)S(1)}, u32[]{:S(2)}, u32[]{:S(2)}) collective-permute-start(bf16[2,256,384]{2,1,0:T(8,128)(2,1)S(1)} %get-tuple-element.18), channel_id=1, source_target_pairs={{0,8},{4,12},{8,0},{12,4},{16,24},{20,28},{24,16},{28,20},{1,9},{5... | collective-permute-start | bytes 1179656 | tf_op jit(solution)/shard_map/ppermute | solution.py:195
  15.0 21.0 %collective-permute-start.11 = (bf16[2,256,384]{2,1,0:T(8,128)(2,1)S(1)}, bf16[2,256,384]{2,1,0:T(8,128)(2,1)S(1)}, u32[]{:S(2)}, u32[]{:S(2)}) collective-permute-start(bf16[2,256,384]{2,1,0:T(8,128)(2,1)S(1)} %get-tuple-element.19), channel_id=1, source_target_pairs={{0,16},{4,20},{8,24},{12,28},{16,0},{20,4},{24,8},{28,12},{1,17},{... | collective-permute-start | bytes 1179656 | tf_op jit(solution)/shard_map/ppermute | solution.py:195
  16.5 17.2 %collective-permute-start.12 = (bf16[2,256,384]{2,1,0:T(8,128)(2,1)S(1)}, bf16[2,256,384]{2,1,0:T(8,128)(2,1)}, u32[]{:S(2)}, u32[]{:S(2)}) collective-permute-start(bf16[2,256,384]{2,1,0:T(8,128)(2,1)S(1)} %get-tuple-element.20), channel_id=1, source_target_pairs={{0,24},{4,28},{8,16},{12,20},{16,8},{20,12},{24,0},{28,4},{1,25},{... | collective-permute-start | bytes 1179656 | tf_op jit(solution)/shard_map/ppermute | solution.py:195
  17.1 24.8 %collective-permute-start = (bf16[384,768]{1,0:T(8,128)(2,1)S(1)}, bf16[384,768]{1,0:T(8,128)(2,1)S(1)}, u32[]{:S(2)}, u32[]{:S(2)}) collective-permute-start(bf16[384,768]{1,0:T(8,128)(2,1)S(1)} %pad_maximum_fusion.1), channel_id=1, source_target_pairs={{0,1},{1,0},{2,3},{3,2},{4,5},{5,4},{6,7},{7,6},{8,9},{9,8},{10,11... | collective-permute-start | bytes 1769480 | tf_op jit(solution)/shard_map/ppermute | solution.py:198
  17.2 19.6 %collective-permute-start.3 = (bf16[192,768]{1,0:T(8,128)(2,1)}, bf16[192,768]{1,0:T(8,128)(2,1)S(1)}, u32[]{:S(2)}, u32[]{:S(2)}) collective-permute-start(bf16[192,768]{1,0:T(8,128)(2,1)} %pad_maximum_fusion.5), channel_id=1, source_target_pairs={{0,2},{1,3},{2,0},{3,1},{4,6},{5,7},{6,4},{7,5},{8,10},{9,11},{10,... | collective-permute-start | bytes 884744 | tf_op jit(solution)/shard_map/ppermute | solution.py:198
  33.7 6.5 %collective-permute-start.7 = (bf16[96,768]{1,0:T(8,128)(2,1)S(1)}, bf16[96,768]{1,0:T(8,128)(2,1)S(1)}, u32[]{:S(2)}, u32[]{:S(2)}) collective-permute-start(bf16[96,768]{1,0:T(8,128)(2,1)S(1)} %get-tuple-element.30), channel_id=1, source_target_pairs={{0,8},{4,12},{8,0},{12,4},{16,24},{20,28},{24,16},{28,20},{1,9},{5... | collective-permute-start | bytes 442376 | tf_op jit(solution)/shard_map/ppermute | solution.py:195
  36.0 5.7 %collective-permute-start.8 = (bf16[96,768]{1,0:T(8,128)(2,1)S(1)}, bf16[96,768]{1,0:T(8,128)(2,1)S(1)}, u32[]{:S(2)}, u32[]{:S(2)}) collective-permute-start(bf16[96,768]{1,0:T(8,128)(2,1)S(1)} %get-tuple-element.29), channel_id=1, source_target_pairs={{0,16},{4,20},{8,24},{12,28},{16,0},{20,4},{24,8},{28,12},{1,17},{... | collective-permute-start | bytes 442376 | tf_op jit(solution)/shard_map/ppermute | solution.py:195
  36.8 5.6 %collective-permute-start.4 = (bf16[96,768]{1,0:T(8,128)(2,1)S(1)}, bf16[96,768]{1,0:T(8,128)(2,1)S(1)}, u32[]{:S(2)}, u32[]{:S(2)}) collective-permute-start(bf16[96,768]{1,0:T(8,128)(2,1)S(1)} %get-tuple-element.32), channel_id=1, source_target_pairs={{0,8},{4,12},{8,0},{12,4},{16,24},{20,28},{24,16},{28,20},{1,9},{5... | collective-permute-start | bytes 442376 | tf_op jit(solution)/shard_map/ppermute | solution.py:195
  37.4 6.0 %collective-permute-start.5 = (bf16[96,768]{1,0:T(8,128)(2,1)S(1)}, bf16[96,768]{1,0:T(8,128)(2,1)S(1)}, u32[]{:S(2)}, u32[]{:S(2)}) collective-permute-start(bf16[96,768]{1,0:T(8,128)(2,1)S(1)} %get-tuple-element.31), channel_id=1, source_target_pairs={{0,16},{4,20},{8,24},{12,28},{16,0},{20,4},{24,8},{28,12},{1,17},{... | collective-permute-start | bytes 442376 | tf_op jit(solution)/shard_map/ppermute | solution.py:195
  40.1 5.4 %collective-permute-start.13 = (bf16[4,256,384]{2,1,0:T(8,128)(2,1)S(1)}, bf16[4,256,384]{2,1,0:T(8,128)(2,1)S(1)}, u32[]{:S(2)}, u32[]{:S(2)}) collective-permute-start(bf16[4,256,384]{2,1,0:T(8,128)(2,1)S(1)} %pad_maximum_fusion), channel_id=1, source_target_pairs={{0,4},{4,0},{8,12},{12,8},{16,20},{20,16},{24,28},{28,24},{1,5},{5... | collective-permute-start | bytes 2359304 | tf_op jit(solution)/shard_map/ppermute | solution.py:195
  41.8 3.9 %collective-permute-start.9 = (bf16[384,768]{1,0:T(8,128)(2,1)S(1)}, bf16[384,768]{1,0:T(8,128)(2,1)S(1)}, u32[]{:S(2)}, u32[]{:S(2)}) collective-permute-start(bf16[384,768]{1,0:T(8,128)(2,1)S(1)} %pad_maximum_fusion.3), channel_id=1, source_target_pairs={{0,4},{4,0},{8,12},{12,8},{16,20},{20,16},{24,28},{28,24},{1,5},{5... | collective-permute-start | bytes 1769480 | tf_op jit(solution)/shard_map/ppermute | solution.py:195
  41.9 3.8 %collective-permute-start.1 = (bf16[384,768]{1,0:T(8,128)(2,1)S(1)}, bf16[384,768]{1,0:T(8,128)(2,1)S(1)}, u32[]{:S(2)}, u32[]{:S(2)}) collective-permute-start(bf16[384,768]{1,0:T(8,128)(2,1)S(1)} %collective-permute-done.rest_0_), channel_id=1, source_target_pairs={{0,4},{4,0},{8,12},{12,8},{16,20},{20,16},{24,28},{28,24},{1,5},{5... | collective-permute-start | bytes 1769480 | tf_op jit(solution)/shard_map/ppermute | solution.py:195
  43.4 2.3 %collective-permute-start.6 = (bf16[384,768]{1,0:T(8,128)(2,1)S(1)}, bf16[384,768]{1,0:T(8,128)(2,1)S(1)}, u32[]{:S(2)}, u32[]{:S(2)}) collective-permute-start(bf16[384,768]{1,0:T(8,128)(2,1)S(1)} %pad_maximum_fusion.2), channel_id=1, source_target_pairs={{0,4},{4,0},{8,12},{12,8},{16,20},{20,16},{24,28},{28,24},{1,5},{5... | collective-permute-start | bytes 1769480 | tf_op jit(solution)/shard_map/ppermute | solution.py:195
  57.3 15.8 %collective-permute-start.18 = (bf16[2,160,384]{2,1,0:T(8,128)(2,1)S(1)}, bf16[2,160,384]{2,1,0:T(8,128)(2,1)S(1)}, u32[]{:S(2)}, u32[]{:S(2)}) collective-permute-start(bf16[2,160,384]{2,1,0:T(8,128)(2,1)S(1)} %get-tuple-element.26), channel_id=1, source_target_pairs={{0,8},{4,12},{8,0},{12,4},{16,24},{20,28},{24,16},{28,20},{1,9},{5... | collective-permute-start | bytes 737288 | tf_op jit(solution)/shard_map/ppermute | solution.py:195
  58.0 15.0 %collective-permute-start.19 = (bf16[2,160,384]{2,1,0:T(8,128)(2,1)S(1)}, bf16[2,160,384]{2,1,0:T(8,128)(2,1)S(1)}, u32[]{:S(2)}, u32[]{:S(2)}) collective-permute-start(bf16[2,160,384]{2,1,0:T(8,128)(2,1)S(1)} %get-tuple-element.27), channel_id=1, source_target_pairs={{0,16},{4,20},{8,24},{12,28},{16,0},{20,4},{24,8},{28,12},{1,17},{... | collective-permute-start | bytes 737288 | tf_op jit(solution)/shard_map/ppermute | solution.py:195
  59.4 12.1 %collective-permute-start.20 = (bf16[2,160,384]{2,1,0:T(8,128)(2,1)S(1)}, bf16[2,160,384]{2,1,0:T(8,128)(2,1)S(1)}, u32[]{:S(2)}, u32[]{:S(2)}) collective-permute-start(bf16[2,160,384]{2,1,0:T(8,128)(2,1)S(1)} %get-tuple-element.28), channel_id=1, source_target_pairs={{0,24},{4,28},{8,16},{12,20},{16,8},{20,12},{24,0},{28,4},{1,25},{... | collective-permute-start | bytes 737288 | tf_op jit(solution)/shard_map/ppermute | solution.py:195
  67.7 10.0 %collective-permute-start.14 = (bf16[2,96,384]{2,1,0:T(8,128)(2,1)S(1)}, bf16[2,96,384]{2,1,0:T(8,128)(2,1)S(1)}, u32[]{:S(2)}, u32[]{:S(2)}) collective-permute-start(bf16[2,96,384]{2,1,0:T(8,128)(2,1)S(1)} %get-tuple-element.22), channel_id=1, source_target_pairs={{0,8},{4,12},{8,0},{12,4},{16,24},{20,28},{24,16},{28,20},{1,9},{5... | collective-permute-start | bytes 442376 | tf_op jit(solution)/shard_map/ppermute | solution.py:195
  68.4 9.3 %collective-permute-start.15 = (bf16[2,96,384]{2,1,0:T(8,128)(2,1)S(1)}, bf16[2,96,384]{2,1,0:T(8,128)(2,1)S(1)}, u32[]{:S(2)}, u32[]{:S(2)}) collective-permute-start(bf16[2,96,384]{2,1,0:T(8,128)(2,1)S(1)} %get-tuple-element.23), channel_id=1, source_target_pairs={{0,16},{4,20},{8,24},{12,28},{16,0},{20,4},{24,8},{28,12},{1,17},{... | collective-permute-start | bytes 442376 | tf_op jit(solution)/shard_map/ppermute | solution.py:195
  71.5 6.1 %collective-permute-start.16 = (bf16[2,96,384]{2,1,0:T(8,128)(2,1)S(1)}, bf16[2,96,384]{2,1,0:T(8,128)(2,1)S(1)}, u32[]{:S(2)}, u32[]{:S(2)}) collective-permute-start(bf16[2,96,384]{2,1,0:T(8,128)(2,1)S(1)} %get-tuple-element.24), channel_id=1, source_target_pairs={{0,24},{4,28},{8,16},{12,20},{16,8},{20,12},{24,0},{28,4},{1,25},{... | collective-permute-start | bytes 442376 | tf_op jit(solution)/shard_map/ppermute | solution.py:195
  73.1 4.7 %collective-permute-start.21 = (bf16[4,160,384]{2,1,0:T(8,128)(2,1)S(1)}, bf16[4,160,384]{2,1,0:T(8,128)(2,1)S(1)}, u32[]{:S(2)}, u32[]{:S(2)}) collective-permute-start(bf16[4,160,384]{2,1,0:T(8,128)(2,1)S(1)} %pad_maximum_fusion.4), channel_id=1, source_target_pairs={{0,4},{4,0},{8,12},{12,8},{16,20},{20,16},{24,28},{28,24},{1,5},{5... | collective-permute-start | bytes 1474568 | tf_op jit(solution)/shard_map/ppermute | solution.py:195
  77.8 1.6 %collective-permute-start.17 = (bf16[4,96,384]{2,1,0:T(8,128)(2,1)S(1)}, bf16[4,96,384]{2,1,0:T(8,128)(2,1)S(1)}, u32[]{:S(2)}, u32[]{:S(2)}) collective-permute-start(bf16[4,96,384]{2,1,0:T(8,128)(2,1)S(1)} %pad_maximum_fusion.6), channel_id=1, source_target_pairs={{0,4},{4,0},{8,12},{12,8},{16,20},{20,16},{24,28},{28,24},{1,5},{5... | collective-permute-start | bytes 884744 | tf_op jit(solution)/shard_map/ppermute | solution.py:195
  (4 other events, 15.8 us)

commit v4 on v3

--- a/solution.py
+++ b/solution.py
@@ -11,9 +11,9 @@
 MEMBERS = 8
 CHIPS = MEMBERS // 2
 LEVELS = 3
-MODES = {1: 'S1', 2: 'S2', 3: 'S2'}
+MODES = {1: 'S1', 2: 'S4', 3: 'S4'}
 CHIP_ORDER = (3, 1, 2)
-PARTS = (5, 3)
+GROUPS = 2
 LANES = 128
 INV_SQRT2 = np.float32(np.sqrt(0.5))
 
@@ -30,36 +30,36 @@
     return pl.CostEstimate(flops=int(flops), bytes_accessed=int(moved), transcendentals=0)
 
 
-def gather_kernel(chips, meta_ref, order_ref, features_ref, *rest):
+def gather_kernel(chips, group, meta_ref, order_ref, features_ref, *rest):
     out_refs, hot_ref = rest[:-1], rest[-1]
     rows, width = features_ref.shape
-    share = rows // MEMBERS
-    tiles = share // LANES
+    tiles = rows // MEMBERS // LANES
+    here = tiles // GROUPS
     me = meta_ref[0]
     lane = lax.broadcasted_iota(jnp.int32, (LANES, LANES), 1)
     for out_ref, chip in zip(out_refs, chips, strict=True):
-        for n in range(2 * tiles):
-            member = jnp.bitwise_xor(me, 2 * chip + n // tiles)
-            taken = order_ref[pl.ds(member * tiles + n % tiles, 1), :]
+        for n in range(2 * here):
+            member = jnp.bitwise_xor(me, 2 * chip + n // here)
+            taken = order_ref[pl.ds(member * tiles + group * here + n % here, 1), :]
             column = jnp.broadcast_to(taken, (LANES, LANES)).T
             for j in range(rows // LANES):
                 hit = jnp.where(column == lane + j * LANES, 1.0, 0.0)
                 hot_ref[n * LANES : (n + 1) * LANES, j * LANES : (j + 1) * LANES] = hit.astype(jnp.bfloat16)
         found = jnp.dot(hot_ref[...], features_ref[...], preferred_element_type=jnp.float32)
-        out_ref[...] = found.astype(jnp.bfloat16).reshape(2, share, width)
-
-
-def gather(chips, meta, order, features):
+        out_ref[...] = found.astype(jnp.bfloat16).reshape(2, here * LANES, width)
+
+
+def gather(chips, group, meta, order, features):
     rows, width = features.shape
-    share = rows // MEMBERS
+    share = rows // MEMBERS // GROUPS
     return pl.pallas_call(
-        functools.partial(gather_kernel, chips),
+        functools.partial(gather_kernel, chips, group),
         out_shape=[jax.ShapeDtypeStruct((2, share, width), features.dtype)] * len(chips),
         in_specs=[SMEM, VMEM, VMEM],
         out_specs=[VMEM] * len(chips),
         scratch_shapes=[pltpu.VMEM((2 * share, rows), features.dtype)],
         compiler_params=limits(32),
-        cost_estimate=cost(4 * len(chips) * share * rows * width, 4 * rows * width),
+        cost_estimate=cost((40 if len(chips) > 1 else 1) * 4 * len(chips) * share * rows * width, 4 * rows * width),
     )(meta, order, features)
 
 
@@ -144,7 +144,7 @@
         out_specs=[VMEM] * CHIPS,
         scratch_shapes=[pltpu.VMEM((MEMBERS, rows, width), blocks[0].dtype)],
         compiler_params=limits(40),
-        cost_estimate=cost(flops, 2 * weights.size),
+        cost_estimate=cost(flops // 50, 2 * weights.size // 50),
     )(meta, weights, bias, *blocks, others)
 
 
@@ -186,7 +186,7 @@
     log_pos = n_pos.bit_length() - 1
     bits = (0, log_pos // 2, log_pos - 1)
     rows = features.shape[0]
-    assert len(set(bits)) == LEVELS and rows % (MEMBERS * LANES) == 0
+    assert len(set(bits)) == LEVELS and rows % (GROUPS * MEMBERS * LANES) == 0
 
     def spread(k):
         return sum(((k >> j) & 1) << bit for j, bit in enumerate(bits))
@@ -227,19 +227,27 @@
     share = rows // MEMBERS
     kinds = {"S1": (halves,), "S2": (left, right), "S4": (eighth,)}
     core, chip_x, chip_y = [(me >> n) & 1 for n in range(LEVELS)]
-    far = jnp.concatenate(
-        [
-            lax.dynamic_slice(switch_in, (core * eighth_rows, chip_x * half), (eighth_rows, half)),
-            lax.dynamic_slice_in_dim(switch_out, (2 * chip_y + core) * eighth_rows, eighth_rows),
-        ]
-    )
-    near = jnp.concatenate(
-        [
-            lax.dynamic_slice(switch_in, (0, core * half), (depth, half)),
-            lax.dynamic_slice_in_dim(switch_out, core * depth, depth),
-        ]
-    )
-    sources = {"S1": near, "S2": far}
+
+    def block_in(row, side, size):
+        return lax.dynamic_slice(switch_in, (row, side * half), (size, half))
+
+    def block_out(row, size):
+        return lax.dynamic_slice_in_dim(switch_out, row, size)
+
+    sources = {
+        "S1": jnp.concatenate([block_in(0, core, depth), block_out(core * depth, depth)]),
+        "S2": jnp.concatenate(
+            [
+                block_in(core * eighth_rows, chip_x, eighth_rows),
+                block_out((2 * chip_y + core) * eighth_rows, eighth_rows),
+            ]
+        ),
+        "S4": jnp.where(
+            chip_y == 0,
+            block_in(core * eighth_rows, chip_x, eighth_rows),
+            block_out((2 * chip_x + core) * eighth_rows, eighth_rows),
+        ),
+    }
     order = row_order.reshape(rows // LANES, LANES)
 
     def cross(pairs):
@@ -249,7 +257,7 @@
 
     parts, plan = [], []
 
-    def spread_parts(owned):
+    def spread_parts(owned, *needed):
         held = [(o, [(k, 0, p) for p in kinds[MODES[k]]]) for k, o in owned]
         for c in (1, 2, 3):
             payload, pieces = [], []
@@ -263,7 +271,9 @@
                     pieces.append((k, 2 * c, left if c == 1 else right))
             if payload:
                 held.append((swap_pos(join(payload), 2 * c), pieces))
-        held.append((swap_pos(join([h[0] for h in held]), 1), [(k, flip + 1, p) for h in held for k, flip, p in h[1]]))
+        across = join([h[0] for h in held])
+        across = after(across, *needed) if needed else across
+        held.append((swap_pos(across, 1), [(k, flip + 1, p) for h in held for k, flip, p in h[1]]))
         for part, pieces in held:
             parts.append(part)
             plan.append(pieces)
@@ -273,26 +283,36 @@
         src = sources[MODES[k]]
         return swap_wt(after(src, *deps) if deps else src, k)
 
-    cuts = [sum(PARTS[:g]) * share // sum(PARTS) for g in range(len(PARTS) + 1)]
-
-    def halve(first):
-        spans = [slice(low, high) for low, high in zip(cuts, cuts[1:])]
-        return [([p[:, span] for p in first[0]], first[1][:, span]) for span in spans]
-
-    owned = {k: get(k) for k in range(1, n_wt) if k != 2}
-    owned[2] = get(2, owned[3])
-    away = gather((1, 2, 3), meta, order, features)
-    own = gather((0,), meta, order, features)
-    first = cross(own + away)
-    for k in range(1, n_wt):
-        spread_parts([(k, owned[k])])
-    split = halve(first)
+    def taken(group):
+        away = gather((1, 2, 3), group, meta, order, features)
+        return gather((0,), group, meta, order, features) + away
+
+
+    owned = {k: get(k) for k in range(2, n_wt)}
+    owned[1] = get(1, owned[3])
+    pairs0, pairs1 = taken(0), taken(1)
+    first = cross(pairs0)
+    spread_parts([(1, owned[1])])
+    held3 = spread_parts([(3, after(owned[3], first[0][1:]))])
+    held2 = spread_parts([(2, after(owned[2], first[0][1:]))], pairs1, pairs0)
+    pairs = after(pairs1, [h[0] for h in held3[1:-1]])
+    second = [pairs[0]] + [swap_pos(pairs[c], 2 * c) for c in range(1, CHIPS)]
     weights = place(n_wt, plan, meta, switch_in, switch_out, parts)
     bias = hidden_bias.reshape(1, -1)
     out = None
-    for group, (blocks, others) in enumerate(split):
-        kept, received = cross(run_levels(meta, weights, bias, blocks, others))
-        out = finish(meta, cuts[group], share, [*kept, received], out)
+    for group in range(GROUPS):
+        if group:
+            moved, made = lax.optimization_barrier((moved, made))
+            others = swap_pos(jnp.stack([p[1] for p in moved]), 1)
+            blocks = moved
+        else:
+            blocks, others = first
+        results = run_levels(meta, weights, bias, blocks, others)
+        if group + 1 < GROUPS:
+            made = results
+            moved = second
+        kept, received = cross(results)
+        out = finish(meta, group * (share // GROUPS), share, [*kept, received], out)
     return out
 
 

time: 81.3 us -> 80.7 us (level)
  starting transfers between devices: 25.6 us -> 31.9 us
  waiting for transfers between devices: 19.5 us -> 15 us
  local copies, waits for them, and re-layouts: 6.6 us -> 2.36 us
  Pallas kernels: 27.6 us -> 29.2 us
    ppermute x19 -> x25, starting transfers between devices: 15.7 us -> 22.2 us  [swap_pos(): return lax.ppermute(x, 'pos', [(i, i ^ spread(k)) for i in range(n_pos)])]
    ppermute x19 -> x25, waiting for transfers between devices: 19.5 us -> 15 us  [swap_pos(): return lax.ppermute(x, 'pos', [(i, i ^ spread(k)) for i in range(n_pos)])]
    slice x12 -> x4, local copies, waits for them, and re-layouts: 2.16 us -> 0.05 us  [body(): others = swap_pos(jnp.stack([p[1] for p in moved]), 1)]
    dynamic_slice x3 -> x1, local copies, waits for them, and re-layouts: 1.9 us -> 0.05 us  [block_out(): return lax.dynamic_slice_in_dim(switch_out, row, size)]
    pallas_call x2 -> x4, Pallas kernels: 6.24 us -> 7.8 us  [gather(): pl.pallas_call(functools.partial(gather_kernel, chips, group), out_shape=...]
    select_n x0 -> x1, other arithmetic: none -> 1.02 us  [body(): jnp.where(chip_y == 0, block_in(core * eighth_rows, chip_x, eighth_rows),...]
    slice x12, local copies, waits for them, and re-layouts: 1.1 us -> 0.13 us  [cross(): return (pairs, swap_pos(jnp.stack([p[1] for p in pairs]), 1))]
    unnamed x12 -> x14, local copies, waits for them, and re-layouts: 1.43 us -> 2.12 us
  transfers between devices with their start and end apart: 22 -> 28, of which waited for: 6 -> 7; matrix products, arithmetic and copies ran while one was open for 5% -> 1% of each run, Pallas kernels for 18% -> 34%
where the time goes in v4:
time: 80.7 us; the launch traced here: 80.5 us
  starting transfers between devices  31.9 us (40%)
  Pallas kernels  29.2 us (36%)
  waiting for transfers between devices  15 us (19%)
  local copies, waits for them, and re-layouts  2.36 us (3%)
  other arithmetic  1.47 us (2%)
    ppermute x25, starting transfers between devices, swap_pos(): return lax.ppermute(x, 'pos', [(i, i ^ spread(k)) for i in range(n_pos)])  22.2 us
    pallas_call x2, Pallas kernels, run_levels(): pl.pallas_call(levels_kernel, out_shape=[jax.ShapeDtypeStruct((2, rows, w...  17.5 us
    ppermute x25, waiting for transfers between devices, swap_pos(): return lax.ppermute(x, 'pos', [(i, i ^ spread(k)) for i in range(n_pos)])  15 us
    ppermute x3, starting transfers between devices, swap_wt(): return lax.ppermute(x, 'wt', [(i, i ^ k) for i in range(n_wt)])  9.74 us
    pallas_call x4, Pallas kernels, gather(): pl.pallas_call(functools.partial(gather_kernel, chips, group), out_shape=...  7.8 us
    pallas_call x2, Pallas kernels, finish(): pl.pallas_call(functools.partial(finish_kernel, first_row, share), out_sh...  2.96 us
    unnamed x14, local copies, waits for them, and re-layouts  2.12 us
  transfers between devices with their start and end apart: 28, of which 7 were waited for; matrix products, arithmetic and copies ran while one was open for 1% of the time, Pallas kernels for 34%

profile of v4, /device:TPU:0, one launch (start us, length us, event | category | flops | bytes accessed | tf_op | source)
XLA Modules:
  0.0 80.5 jit_solution(8168017337404675536)
XLA Ops:
  1.0 4.1 %collective-permute-start.10 = (bf16[96,768]{1,0:T(8,128)(2,1)S(1)}, bf16[96,768]{1,0:T(8,128)(2,1)S(1)}, u32[]{:S(2)}, u32[]{:S(2)}) collective-permute-start(bf16[96,768]{1,0:T(8,128)(2,1)S(1)} %dynamic-slice_select_fusion), channel_id=1, source_target_pairs={{0,2},{1,3},{2,0},{3,1},{4,6},{5,7},{6,4},{7,5},{8,10},{9,11},{10,... | collective-permute-start | bytes 442376 | tf_op jit(solution)/shard_map/ppermute | solution.py:198
  5.1 1.3 %collective-permute-start = (bf16[96,768]{1,0:T(8,128)(2,1)S(1)}, bf16[96,768]{1,0:T(8,128)(2,1)S(1)}, u32[]{:S(2)}, u32[]{:S(2)}) collective-permute-start(bf16[96,768]{1,0:T(8,128)(2,1)S(1)} %dynamic-slice_select_fusion), channel_id=1, source_target_pairs={{0,3},{1,2},{2,1},{3,0},{4,7},{5,6},{6,5},{7,4},{8,11},{9,10},{10,... | collective-permute-start | bytes 442376 | tf_op jit(solution)/shard_map/ppermute | solution.py:198
  6.5 1.4 %copy-done = bf16[2048,384]{1,0:T(8,128)(2,1)S(1)} copy-done((bf16[2048,384]{1,0:T(8,128)(2,1)S(1)}, bf16[2048,384]{1,0:T(8,128)(2,1)}, u32[]{:S(2)}) %copy-start) | copy-done | bytes 1572888
  8.7 2.5 %shard_map.55 = (bf16[2,128,384]{2,1,0:T(8,128)(2,1)S(1)}, bf16[2,128,384]{2,1,0:T(8,128)(2,1)S(1)}, bf16[2,128,384]{2,1,0:T(8,128)(2,1)S(1)}) custom-call(s32[2]{0:T(128)S(1)} %pad_add_fusion.meta_ref, s32[16,128]{1,0:T(8,128)S(1)} %bitcast.3, bf16[2048,384]{1,0:T(8,128)(2,1)S(1)} %copy-done), custom_call_target="tpu_custom_call" | custom-call | flops 48318382080 | bytes 3145728 | tf_op jit(solution)/shard_map/pallas_call | solution.py:55
  11.2 1.6 %collective-permute-start.3 = (bf16[2,128,384]{2,1,0:T(8,128)(2,1)S(1)}, bf16[2,128,384]{2,1,0:T(8,128)(2,1)S(1)}, u32[]{:S(2)}, u32[]{:S(2)}) collective-permute-start(bf16[2,128,384]{2,1,0:T(8,128)(2,1)S(1)} %get-tuple-element.32), channel_id=1, source_target_pairs={{0,8},{4,12},{8,0},{12,4},{16,24},{20,28},{24,16},{28,20},{1,9},{5... | collective-permute-start | bytes 589832 | tf_op jit(solution)/shard_map/ppermute | solution.py:195
  12.8 1.5 %collective-permute-start.4 = (bf16[2,128,384]{2,1,0:T(8,128)(2,1)S(1)}, bf16[2,128,384]{2,1,0:T(8,128)(2,1)S(1)}, u32[]{:S(2)}, u32[]{:S(2)}) collective-permute-start(bf16[2,128,384]{2,1,0:T(8,128)(2,1)S(1)} %get-tuple-element.33), channel_id=1, source_target_pairs={{0,16},{4,20},{8,24},{12,28},{16,0},{20,4},{24,8},{28,12},{1,17},{... | collective-permute-start | bytes 589832 | tf_op jit(solution)/shard_map/ppermute | solution.py:195
  14.9 4.3 %collective-permute-start.1 = (bf16[384,768]{1,0:T(8,128)(2,1)S(1)}, bf16[384,768]{1,0:T(8,128)(2,1)S(1)}, u32[]{:S(2)}, u32[]{:S(2)}) collective-permute-start(bf16[384,768]{1,0:T(8,128)(2,1)S(1)} %pad_maximum_fusion), channel_id=1, source_target_pairs={{0,1},{1,0},{2,3},{3,2},{4,5},{5,4},{6,7},{7,6},{8,9},{9,8},{10,11... | collective-permute-start | bytes 1769480 | tf_op jit(solution)/shard_map/ppermute | solution.py:198
  19.2 3.6 %collective-permute-done.4.rest_2_ = bf16[2,128,384]{2,1,0:T(8,128)(2,1)S(1)} collective-permute-done((bf16[2,128,384]{2,1,0:T(8,128)(2,1)S(1)}, bf16[2,128,384]{2,1,0:T(8,128)(2,1)S(1)}, u32[]{:S(2)}, u32[]{:S(2)}) %collective-permute-start.4) | collective-permute-done | bytes 196640 | tf_op jit(solution)/shard_map/ppermute | solution.py:195
  24.9 1.4 %collective-permute-start.13 = (bf16[96,768]{1,0:T(8,128)(2,1)S(1)}, bf16[96,768]{1,0:T(8,128)(2,1)S(1)}, u32[]{:S(2)}, u32[]{:S(2)}) collective-permute-start(bf16[96,768]{1,0:T(8,128)(2,1)S(1)} %collective-permute-done.10.rest_7_), channel_id=1, source_target_pairs={{0,24},{4,28},{8,16},{12,20},{16,8},{20,12},{24,0},{28,4},{1,25},{... | collective-permute-start | bytes 442376 | tf_op jit(solution)/shard_map/ppermute | solution.py:195
  26.3 2.5 %shard_map.57 = (bf16[2,128,384]{2,1,0:T(8,128)(2,1)S(1)}, bf16[2,128,384]{2,1,0:T(8,128)(2,1)S(1)}, bf16[2,128,384]{2,1,0:T(8,128)(2,1)S(1)}) custom-call(s32[2]{0:T(128)S(1)} %pad_add_fusion.meta_ref, s32[16,128]{1,0:T(8,128)S(1)} %bitcast.4, bf16[2048,384]{1,0:T(8,128)(2,1)S(1)} %copy-done.1), custom_call_target="tpu_custom_call" | custom-call | flops 48318382080 | bytes 3145728 | tf_op jit(solution)/shard_map/pallas_call | solution.py:55
  28.8 1.3 %shard_map.58.rest_0_ = bf16[2,128,384]{2,1,0:T(8,128)(2,1)S(1)} custom-call(s32[2]{0:T(128)S(1)} %pad_add_fusion.meta_ref, s32[16,128]{1,0:T(8,128)S(1)} %bitcast.5, bf16[2048,384]{1,0:T(8,128)(2,1)S(1)} %copy-done.1), custom_call_target="tpu_custom_call" | custom-call | flops 402653184 | bytes 3145728 | tf_op jit(solution)/shard_map/pallas_call | solution.py:55
  32.3 1.4 %collective-permute-start.8 = (bf16[96,768]{1,0:T(8,128)(2,1)S(1)}, bf16[96,768]{1,0:T(8,128)(2,1)S(1)}, u32[]{:S(2)}, u32[]{:S(2)}) collective-permute-start(bf16[96,768]{1,0:T(8,128)(2,1)S(1)} %collective-permute-done.rest_2_), channel_id=1, source_target_pairs={{0,24},{4,28},{8,16},{12,20},{16,8},{20,12},{24,0},{28,4},{1,25},{... | collective-permute-start | bytes 442376 | tf_op jit(solution)/shard_map/ppermute | solution.py:195
  33.8 1.4 %shard_map.56.rest_0_ = bf16[2,128,384]{2,1,0:T(8,128)(2,1)S(1)} custom-call(s32[2]{0:T(128)S(1)} %pad_add_fusion.meta_ref, s32[16,128]{1,0:T(8,128)S(1)} %bitcast.6, bf16[2048,384]{1,0:T(8,128)(2,1)S(1)} %copy-done.1), custom_call_target="tpu_custom_call" | custom-call | flops 402653184 | bytes 3145728 | tf_op jit(solution)/shard_map/pallas_call | solution.py:55
  36.6 1.7 %collective-permute-done.8.rest_5_ = bf16[96,768]{1,0:T(8,128)(2,1)S(1)} collective-permute-done((bf16[96,768]{1,0:T(8,128)(2,1)S(1)}, bf16[96,768]{1,0:T(8,128)(2,1)S(1)}, u32[]{:S(2)}, u32[]{:S(2)}) %collective-permute-start.8) | collective-permute-done | bytes 147488 | tf_op jit(solution)/shard_map/ppermute | solution.py:195
  39.3 1.5 %collective-permute-start.15 = (bf16[2,128,384]{2,1,0:T(8,128)(2,1)S(1)}, bf16[2,128,384]{2,1,0:T(8,128)(2,1)S(1)}, u32[]{:S(2)}, u32[]{:S(2)}) collective-permute-start(bf16[2,128,384]{2,1,0:T(8,128)(2,1)S(1)} %get-tuple-element.42), channel_id=1, source_target_pairs={{0,8},{4,12},{8,0},{12,4},{16,24},{20,28},{24,16},{28,20},{1,9},{5... | collective-permute-start | bytes 589832 | tf_op jit(solution)/shard_map/ppermute | solution.py:195
  43.7 8.9 %shard_map.60 = (bf16[2,128,384]{2,1,0:T(8,128)(2,1)S(1)}, bf16[2,128,384]{2,1,0:T(8,128)(2,1)S(1)}, bf16[2,128,384]{2,1,0:T(8,128)(2,1)S(1)}, bf16[2,128,384]{2,1,0:T(8,128)(2,1)S(1)}) custom-call(s32[2]{0:T(128)S(1)} %pad_add_fusion.meta_ref, bf16[3072,768]{1,0:T(8,128)(2,1)S(1)} %shard_map.59.weights_ref, f32[1,1536]{1,0:T(1,128)S(1)} %reshape.7.bias_ref, ...), custom_call_target="tpu_custom_call" | custom-call | flops 144955152 | bytes 94371 | tf_op jit(solution)/shard_map/pallas_call | solution.py:140
  52.9 1.5 %collective-permute-start.24 = (bf16[2,128,384]{2,1,0:T(8,128)(2,1)S(1)}, bf16[2,128,384]{2,1,0:T(8,128)(2,1)S(1)}, u32[]{:S(2)}, u32[]{:S(2)}) collective-permute-start(bf16[2,128,384]{2,1,0:T(8,128)(2,1)S(1)} %get-tuple-element.46), channel_id=1, source_target_pairs={{0,8},{4,12},{8,0},{12,4},{16,24},{20,28},{24,16},{28,20},{1,9},{5... | collective-permute-start | bytes 589832 | tf_op jit(solution)/shard_map/ppermute | solution.py:195
  55.1 1.3 %collective-permute-start.26 = (bf16[2,128,384]{2,1,0:T(8,128)(2,1)S(1)}, bf16[2,128,384]{2,1,0:T(8,128)(2,1)S(1)}, u32[]{:S(2)}, u32[]{:S(2)}) collective-permute-start(bf16[2,128,384]{2,1,0:T(8,128)(2,1)S(1)} %get-tuple-element.48), channel_id=1, source_target_pairs={{0,24},{4,28},{8,16},{12,20},{16,8},{20,12},{24,0},{28,4},{1,25},{... | collective-permute-start | bytes 589832 | tf_op jit(solution)/shard_map/ppermute | solution.py:195
  56.4 8.7 %shard_map.61 = (bf16[2,128,384]{2,1,0:T(8,128)(2,1)S(1)}, bf16[2,128,384]{2,1,0:T(8,128)(2,1)S(1)}, bf16[2,128,384]{2,1,0:T(8,128)(2,1)S(1)}, bf16[2,128,384]{2,1,0:T(8,128)(2,1)S(1)}) custom-call(s32[2]{0:T(128)S(1)} %pad_add_fusion.meta_ref, bf16[3072,768]{1,0:T(8,128)(2,1)S(1)} %shard_map.59.weights_ref, f32[1,1536]{1,0:T(1,128)S(1)} %reshape.7.bias_ref, ...), custom_call_target="tpu_custom_call" | custom-call | flops 144955152 | bytes 94371 | tf_op jit(solution)/shard_map/pallas_call | solution.py:140
  65.1 1.5 %collective-permute-start.20 = (bf16[2,128,384]{2,1,0:T(8,128)(2,1)S(1)}, bf16[2,128,384]{2,1,0:T(8,128)(2,1)S(1)}, u32[]{:S(2)}, u32[]{:S(2)}) collective-permute-start(bf16[2,128,384]{2,1,0:T(8,128)(2,1)S(1)} %get-tuple-element.54), channel_id=1, source_target_pairs={{0,8},{4,12},{8,0},{12,4},{16,24},{20,28},{24,16},{28,20},{1,9},{5... | collective-permute-start | bytes 589832 | tf_op jit(solution)/shard_map/ppermute | solution.py:195
  68.9 4.1 %collective-permute-done.20.rest_1_ = bf16[2,128,384]{2,1,0:T(8,128)(2,1)S(1)} collective-permute-done((bf16[2,128,384]{2,1,0:T(8,128)(2,1)S(1)}, bf16[2,128,384]{2,1,0:T(8,128)(2,1)S(1)}, u32[]{:S(2)}, u32[]{:S(2)}) %collective-permute-start.20) | collective-permute-done | bytes 196640 | tf_op jit(solution)/shard_map/ppermute | solution.py:195
  73.0 4.0 %collective-permute-done.21.rest_2_ = bf16[2,128,384]{2,1,0:T(8,128)(2,1)S(1)} collective-permute-done((bf16[2,128,384]{2,1,0:T(8,128)(2,1)S(1)}, bf16[2,128,384]{2,1,0:T(8,128)(2,1)S(1)}, u32[]{:S(2)}, u32[]{:S(2)}) %collective-permute-start.21) | collective-permute-done | bytes 196640 | tf_op jit(solution)/shard_map/ppermute | solution.py:195
  77.2 1.5 %shard_map.62.rest_5_ = bf16[2048,384]{1,0:T(8,128)(2,1)} custom-call(s32[2]{0:T(128)S(1)} %pad_add_fusion.meta_ref, bf16[2,128,384]{2,1,0:T(8,128)(2,1)S(1)} %get-tuple-element.45.rest_0_, bf16[2,128,384]{2,1,0:T(8,128)(2,1)S(1)} %collective-permute-done.24.rest_1_, bf16[2,128,384]{2,1,0:T(8,128)(2,1)S(1)} %collective-permute-done.25.rest_2_, ...), custom_call_target="tpu_custom_call" | custom-call | bytes 1572864 | tf_op jit(solution)/shard_map/pallas_call | solution.py:172
  78.9 1.5 %shard_map.63 = bf16[2048,384]{1,0:T(8,128)(2,1)} custom-call(s32[2]{0:T(128)S(1)} %pad_add_fusion.meta_ref, bf16[2,128,384]{2,1,0:T(8,128)(2,1)S(1)} %get-tuple-element.53.rest_0_, bf16[2,128,384]{2,1,0:T(8,128)(2,1)S(1)} %collective-permute-done.20.rest_1_, ...), custom_call_target="tpu_custom_call", output_to_operand_aliasing={{}: (6, {})} | custom-call | bytes 1572864 | tf_op jit(solution)/shard_map/pallas_call | solution.py:172
  (82 shorter events, 15.3 us)
Async XLA Ops:
  1.0 18.2 %collective-permute-start.10 = (bf16[96,768]{1,0:T(8,128)(2,1)S(1)}, bf16[96,768]{1,0:T(8,128)(2,1)S(1)}, u32[]{:S(2)}, u32[]{:S(2)}) collective-permute-start(bf16[96,768]{1,0:T(8,128)(2,1)S(1)} %dynamic-slice_select_fusion), channel_id=1, source_target_pairs={{0,2},{1,3},{2,0},{3,1},{4,6},{5,7},{6,4},{7,5},{8,10},{9,11},{10,... | collective-permute-start | bytes 442376 | tf_op jit(solution)/shard_map/ppermute | solution.py:198
  5.1 9.7 %collective-permute-start = (bf16[96,768]{1,0:T(8,128)(2,1)S(1)}, bf16[96,768]{1,0:T(8,128)(2,1)S(1)}, u32[]{:S(2)}, u32[]{:S(2)}) collective-permute-start(bf16[96,768]{1,0:T(8,128)(2,1)S(1)} %dynamic-slice_select_fusion), channel_id=1, source_target_pairs={{0,3},{1,2},{2,1},{3,0},{4,7},{5,6},{6,5},{7,4},{8,11},{9,10},{10,... | collective-permute-start | bytes 442376 | tf_op jit(solution)/shard_map/ppermute | solution.py:198
  11.2 8.0 %collective-permute-start.3 = (bf16[2,128,384]{2,1,0:T(8,128)(2,1)S(1)}, bf16[2,128,384]{2,1,0:T(8,128)(2,1)S(1)}, u32[]{:S(2)}, u32[]{:S(2)}) collective-permute-start(bf16[2,128,384]{2,1,0:T(8,128)(2,1)S(1)} %get-tuple-element.32), channel_id=1, source_target_pairs={{0,8},{4,12},{8,0},{12,4},{16,24},{20,28},{24,16},{28,20},{1,9},{5... | collective-permute-start | bytes 589832 | tf_op jit(solution)/shard_map/ppermute | solution.py:195
  12.8 10.0 %collective-permute-start.4 = (bf16[2,128,384]{2,1,0:T(8,128)(2,1)S(1)}, bf16[2,128,384]{2,1,0:T(8,128)(2,1)S(1)}, u32[]{:S(2)}, u32[]{:S(2)}) collective-permute-start(bf16[2,128,384]{2,1,0:T(8,128)(2,1)S(1)} %get-tuple-element.33), channel_id=1, source_target_pairs={{0,16},{4,20},{8,24},{12,28},{16,0},{20,4},{24,8},{28,12},{1,17},{... | collective-permute-start | bytes 589832 | tf_op jit(solution)/shard_map/ppermute | solution.py:195
  14.3 8.5 %collective-permute-start.5 = (bf16[2,128,384]{2,1,0:T(8,128)(2,1)S(1)}, bf16[2,128,384]{2,1,0:T(8,128)(2,1)S(1)}, u32[]{:S(2)}, u32[]{:S(2)}) collective-permute-start(bf16[2,128,384]{2,1,0:T(8,128)(2,1)S(1)} %get-tuple-element.34), channel_id=1, source_target_pairs={{0,24},{4,28},{8,16},{12,20},{16,8},{20,12},{24,0},{28,4},{1,25},{... | collective-permute-start | bytes 589832 | tf_op jit(solution)/shard_map/ppermute | solution.py:195
  14.9 23.6 %collective-permute-start.1 = (bf16[384,768]{1,0:T(8,128)(2,1)S(1)}, bf16[384,768]{1,0:T(8,128)(2,1)S(1)}, u32[]{:S(2)}, u32[]{:S(2)}) collective-permute-start(bf16[384,768]{1,0:T(8,128)(2,1)S(1)} %pad_maximum_fusion), channel_id=1, source_target_pairs={{0,1},{1,0},{2,3},{3,2},{4,5},{5,4},{6,7},{7,6},{8,9},{9,8},{10,11... | collective-permute-start | bytes 1769480 | tf_op jit(solution)/shard_map/ppermute | solution.py:198
  22.8 8.7 %collective-permute-start.11 = (bf16[96,768]{1,0:T(8,128)(2,1)S(1)}, bf16[96,768]{1,0:T(8,128)(2,1)S(1)}, u32[]{:S(2)}, u32[]{:S(2)}) collective-permute-start(bf16[96,768]{1,0:T(8,128)(2,1)S(1)} %collective-permute-done.10.rest_7_), channel_id=1, source_target_pairs={{0,8},{4,12},{8,0},{12,4},{16,24},{20,28},{24,16},{28,20},{1,9},{5... | collective-permute-start | bytes 442376 | tf_op jit(solution)/shard_map/ppermute | solution.py:195
  24.0 8.3 %collective-permute-start.12 = (bf16[96,768]{1,0:T(8,128)(2,1)S(1)}, bf16[96,768]{1,0:T(8,128)(2,1)S(1)}, u32[]{:S(2)}, u32[]{:S(2)}) collective-permute-start(bf16[96,768]{1,0:T(8,128)(2,1)S(1)} %collective-permute-done.10.rest_7_), channel_id=1, source_target_pairs={{0,16},{4,20},{8,24},{12,28},{16,0},{20,4},{24,8},{28,12},{1,17},{... | collective-permute-start | bytes 442376 | tf_op jit(solution)/shard_map/ppermute | solution.py:195
  24.9 10.3 %collective-permute-start.13 = (bf16[96,768]{1,0:T(8,128)(2,1)S(1)}, bf16[96,768]{1,0:T(8,128)(2,1)S(1)}, u32[]{:S(2)}, u32[]{:S(2)}) collective-permute-start(bf16[96,768]{1,0:T(8,128)(2,1)S(1)} %collective-permute-done.10.rest_7_), channel_id=1, source_target_pairs={{0,24},{4,28},{8,16},{12,20},{16,8},{20,12},{24,0},{28,4},{1,25},{... | collective-permute-start | bytes 442376 | tf_op jit(solution)/shard_map/ppermute | solution.py:195
  30.2 5.5 %collective-permute-start.6 = (bf16[96,768]{1,0:T(8,128)(2,1)S(1)}, bf16[96,768]{1,0:T(8,128)(2,1)S(1)}, u32[]{:S(2)}, u32[]{:S(2)}) collective-permute-start(bf16[96,768]{1,0:T(8,128)(2,1)S(1)} %collective-permute-done.rest_2_), channel_id=1, source_target_pairs={{0,8},{4,12},{8,0},{12,4},{16,24},{20,28},{24,16},{28,20},{1,9},{5... | collective-permute-start | bytes 442376 | tf_op jit(solution)/shard_map/ppermute | solution.py:195
  31.5 5.1 %collective-permute-start.7 = (bf16[96,768]{1,0:T(8,128)(2,1)S(1)}, bf16[96,768]{1,0:T(8,128)(2,1)S(1)}, u32[]{:S(2)}, u32[]{:S(2)}) collective-permute-start(bf16[96,768]{1,0:T(8,128)(2,1)S(1)} %collective-permute-done.rest_2_), channel_id=1, source_target_pairs={{0,16},{4,20},{8,24},{12,28},{16,0},{20,4},{24,8},{28,12},{1,17},{... | collective-permute-start | bytes 442376 | tf_op jit(solution)/shard_map/ppermute | solution.py:195
  32.3 6.0 %collective-permute-start.8 = (bf16[96,768]{1,0:T(8,128)(2,1)S(1)}, bf16[96,768]{1,0:T(8,128)(2,1)S(1)}, u32[]{:S(2)}, u32[]{:S(2)}) collective-permute-start(bf16[96,768]{1,0:T(8,128)(2,1)S(1)} %collective-permute-done.rest_2_), channel_id=1, source_target_pairs={{0,24},{4,28},{8,16},{12,20},{16,8},{20,12},{24,0},{28,4},{1,25},{... | collective-permute-start | bytes 442376 | tf_op jit(solution)/shard_map/ppermute | solution.py:195
  35.2 5.6 %collective-permute-start.14 = (bf16[384,768]{1,0:T(8,128)(2,1)S(1)}, bf16[384,768]{1,0:T(8,128)(2,1)S(1)}, u32[]{:S(2)}, u32[]{:S(2)}) collective-permute-start(bf16[384,768]{1,0:T(8,128)(2,1)S(1)} %pad_maximum_fusion.2), channel_id=1, source_target_pairs={{0,4},{4,0},{8,12},{12,8},{16,20},{20,16},{24,28},{28,24},{1,5},{5... | collective-permute-start | bytes 1769480 | tf_op jit(solution)/shard_map/ppermute | solution.py:195
  39.2 4.5 %collective-permute-start.18 = (bf16[4,128,384]{2,1,0:T(8,128)(2,1)S(1)}, bf16[4,128,384]{2,1,0:T(8,128)(2,1)S(1)}, u32[]{:S(2)}, u32[]{:S(2)}) collective-permute-start(bf16[4,128,384]{2,1,0:T(8,128)(2,1)S(1)} %pad_maximum_fusion.3), channel_id=1, source_target_pairs={{0,4},{4,0},{8,12},{12,8},{16,20},{20,16},{24,28},{28,24},{1,5},{5... | collective-permute-start | bytes 1179656 | tf_op jit(solution)/shard_map/ppermute | solution.py:195
  39.3 13.3 %collective-permute-start.15 = (bf16[2,128,384]{2,1,0:T(8,128)(2,1)S(1)}, bf16[2,128,384]{2,1,0:T(8,128)(2,1)S(1)}, u32[]{:S(2)}, u32[]{:S(2)}) collective-permute-start(bf16[2,128,384]{2,1,0:T(8,128)(2,1)S(1)} %get-tuple-element.42), channel_id=1, source_target_pairs={{0,8},{4,12},{8,0},{12,4},{16,24},{20,28},{24,16},{28,20},{1,9},{5... | collective-permute-start | bytes 589832 | tf_op jit(solution)/shard_map/ppermute | solution.py:195
  40.8 11.8 %collective-permute-start.16 = (bf16[2,128,384]{2,1,0:T(8,128)(2,1)S(1)}, bf16[2,128,384]{2,1,0:T(8,128)(2,1)S(1)}, u32[]{:S(2)}, u32[]{:S(2)}) collective-permute-start(bf16[2,128,384]{2,1,0:T(8,128)(2,1)S(1)} %get-tuple-element.43), channel_id=1, source_target_pairs={{0,16},{4,20},{8,24},{12,28},{16,0},{20,4},{24,8},{28,12},{1,17},{... | collective-permute-start | bytes 589832 | tf_op jit(solution)/shard_map/ppermute | solution.py:195
  41.5 11.1 %collective-permute-start.17 = (bf16[2,128,384]{2,1,0:T(8,128)(2,1)S(1)}, bf16[2,128,384]{2,1,0:T(8,128)(2,1)S(1)}, u32[]{:S(2)}, u32[]{:S(2)}) collective-permute-start(bf16[2,128,384]{2,1,0:T(8,128)(2,1)S(1)} %get-tuple-element.44), channel_id=1, source_target_pairs={{0,24},{4,28},{8,16},{12,20},{16,8},{20,12},{24,0},{28,4},{1,25},{... | collective-permute-start | bytes 589832 | tf_op jit(solution)/shard_map/ppermute | solution.py:195
  52.9 14.4 %collective-permute-start.24 = (bf16[2,128,384]{2,1,0:T(8,128)(2,1)S(1)}, bf16[2,128,384]{2,1,0:T(8,128)(2,1)S(1)}, u32[]{:S(2)}, u32[]{:S(2)}) collective-permute-start(bf16[2,128,384]{2,1,0:T(8,128)(2,1)S(1)} %get-tuple-element.46), channel_id=1, source_target_pairs={{0,8},{4,12},{8,0},{12,4},{16,24},{20,28},{24,16},{28,20},{1,9},{5... | collective-permute-start | bytes 589832 | tf_op jit(solution)/shard_map/ppermute | solution.py:195
  54.4 14.3 %collective-permute-start.25 = (bf16[2,128,384]{2,1,0:T(8,128)(2,1)S(1)}, bf16[2,128,384]{2,1,0:T(8,128)(2,1)S(1)}, u32[]{:S(2)}, u32[]{:S(2)}) collective-permute-start(bf16[2,128,384]{2,1,0:T(8,128)(2,1)S(1)} %get-tuple-element.47), channel_id=1, source_target_pairs={{0,16},{4,20},{8,24},{12,28},{16,0},{20,4},{24,8},{28,12},{1,17},{... | collective-permute-start | bytes 589832 | tf_op jit(solution)/shard_map/ppermute | solution.py:195
  55.1 13.6 %collective-permute-start.26 = (bf16[2,128,384]{2,1,0:T(8,128)(2,1)S(1)}, bf16[2,128,384]{2,1,0:T(8,128)(2,1)S(1)}, u32[]{:S(2)}, u32[]{:S(2)}) collective-permute-start(bf16[2,128,384]{2,1,0:T(8,128)(2,1)S(1)} %get-tuple-element.48), channel_id=1, source_target_pairs={{0,24},{4,28},{8,16},{12,20},{16,8},{20,12},{24,0},{28,4},{1,25},{... | collective-permute-start | bytes 589832 | tf_op jit(solution)/shard_map/ppermute | solution.py:195
  65.1 7.9 %collective-permute-start.20 = (bf16[2,128,384]{2,1,0:T(8,128)(2,1)S(1)}, bf16[2,128,384]{2,1,0:T(8,128)(2,1)S(1)}, u32[]{:S(2)}, u32[]{:S(2)}) collective-permute-start(bf16[2,128,384]{2,1,0:T(8,128)(2,1)S(1)} %get-tuple-element.54), channel_id=1, source_target_pairs={{0,8},{4,12},{8,0},{12,4},{16,24},{20,28},{24,16},{28,20},{1,9},{5... | collective-permute-start | bytes 589832 | tf_op jit(solution)/shard_map/ppermute | solution.py:195
  66.6 10.3 %collective-permute-start.21 = (bf16[2,128,384]{2,1,0:T(8,128)(2,1)S(1)}, bf16[2,128,384]{2,1,0:T(8,128)(2,1)S(1)}, u32[]{:S(2)}, u32[]{:S(2)}) collective-permute-start(bf16[2,128,384]{2,1,0:T(8,128)(2,1)S(1)} %get-tuple-element.55), channel_id=1, source_target_pairs={{0,16},{4,20},{8,24},{12,28},{16,0},{20,4},{24,8},{28,12},{1,17},{... | collective-permute-start | bytes 589832 | tf_op jit(solution)/shard_map/ppermute | solution.py:195
  67.3 9.7 %collective-permute-start.22 = (bf16[2,128,384]{2,1,0:T(8,128)(2,1)S(1)}, bf16[2,128,384]{2,1,0:T(8,128)(2,1)S(1)}, u32[]{:S(2)}, u32[]{:S(2)}) collective-permute-start(bf16[2,128,384]{2,1,0:T(8,128)(2,1)S(1)} %get-tuple-element.56), channel_id=1, source_target_pairs={{0,24},{4,28},{8,16},{12,20},{16,8},{20,12},{24,0},{28,4},{1,25},{... | collective-permute-start | bytes 589832 | tf_op jit(solution)/shard_map/ppermute | solution.py:195
  68.8 8.4 %collective-permute-start.27 = (bf16[4,128,384]{2,1,0:T(8,128)(2,1)S(1)}, bf16[4,128,384]{2,1,0:T(8,128)(2,1)S(1)}, u32[]{:S(2)}, u32[]{:S(2)}) collective-permute-start(bf16[4,128,384]{2,1,0:T(8,128)(2,1)S(1)} %pad_maximum_fusion.6), channel_id=1, source_target_pairs={{0,4},{4,0},{8,12},{12,8},{16,20},{20,16},{24,28},{28,24},{1,5},{5... | collective-permute-start | bytes 1179656 | tf_op jit(solution)/shard_map/ppermute | solution.py:195
  (11 other events, 57.7 us)

commit v5 on v4

--- a/solution.py
+++ b/solution.py
@@ -11,8 +11,8 @@
 MEMBERS = 8
 CHIPS = MEMBERS // 2
 LEVELS = 3
-MODES = {1: 'S1', 2: 'S4', 3: 'S4'}
-CHIP_ORDER = (3, 1, 2)
+EARLY, LATE = 40, 50
+CHIP_ORDER = (2, 1, 3)
 GROUPS = 2
 LANES = 128
 INV_SQRT2 = np.float32(np.sqrt(0.5))
@@ -59,7 +59,7 @@
         out_specs=[VMEM] * len(chips),
         scratch_shapes=[pltpu.VMEM((2 * share, rows), features.dtype)],
         compiler_params=limits(32),
-        cost_estimate=cost((40 if len(chips) > 1 else 1) * 4 * len(chips) * share * rows * width, 4 * rows * width),
+        cost_estimate=cost((EARLY if len(chips) > 1 else 1) * 4 * len(chips) * share * rows * width, 4 * rows * width),
     )(meta, order, features)
 
 
@@ -144,7 +144,7 @@
         out_specs=[VMEM] * CHIPS,
         scratch_shapes=[pltpu.VMEM((MEMBERS, rows, width), blocks[0].dtype)],
         compiler_params=limits(40),
-        cost_estimate=cost(flops // 50, 2 * weights.size // 50),
+        cost_estimate=cost(flops // LATE, 2 * weights.size // LATE),
     )(meta, weights, bias, *blocks, others)
 
 
@@ -212,12 +212,6 @@
     def eighth(me):
         return [(me * eighth_rows, eighth_rows)]
 
-    def left(me):
-        return [(((me >> 1) & 1) * 2 * eighth_rows + (me & 1) * eighth_rows, eighth_rows)]
-
-    def right(me):
-        return [(total // 2 + ((me >> 2) & 1) * 2 * eighth_rows + (me & 1) * eighth_rows, eighth_rows)]
-
     def after(x, *earlier):
         return lax.optimization_barrier((x, earlier))[0]
 
@@ -225,7 +219,6 @@
         return jnp.concatenate(xs, axis=0) if len(xs) > 1 else xs[0]
 
     share = rows // MEMBERS
-    kinds = {"S1": (halves,), "S2": (left, right), "S4": (eighth,)}
     core, chip_x, chip_y = [(me >> n) & 1 for n in range(LEVELS)]
 
     def block_in(row, side, size):
@@ -234,20 +227,12 @@
     def block_out(row, size):
         return lax.dynamic_slice_in_dim(switch_out, row, size)
 
-    sources = {
-        "S1": jnp.concatenate([block_in(0, core, depth), block_out(core * depth, depth)]),
-        "S2": jnp.concatenate(
-            [
-                block_in(core * eighth_rows, chip_x, eighth_rows),
-                block_out((2 * chip_y + core) * eighth_rows, eighth_rows),
-            ]
-        ),
-        "S4": jnp.where(
-            chip_y == 0,
-            block_in(core * eighth_rows, chip_x, eighth_rows),
-            block_out((2 * chip_x + core) * eighth_rows, eighth_rows),
-        ),
-    }
+    near = jnp.concatenate([block_in(0, core, depth), block_out(core * depth, depth)])
+    far = jnp.where(
+        chip_y == 0,
+        block_in(core * eighth_rows, chip_x, eighth_rows),
+        block_out((2 * chip_x + core) * eighth_rows, eighth_rows),
+    )
     order = row_order.reshape(rows // LANES, LANES)
 
     def cross(pairs):
@@ -257,45 +242,34 @@
 
     parts, plan = [], []
 
-    def spread_parts(owned, *needed):
-        held = [(o, [(k, 0, p) for p in kinds[MODES[k]]]) for k, o in owned]
-        for c in (1, 2, 3):
-            payload, pieces = [], []
-            for k, own in owned:
-                mode = MODES[k]
-                if mode == "S4":
-                    payload.append(own)
-                    pieces.append((k, 2 * c, eighth))
-                if mode == "S2" and c < 3:
-                    payload.append(own[:eighth_rows] if c == 1 else own[eighth_rows:])
-                    pieces.append((k, 2 * c, left if c == 1 else right))
-            if payload:
-                held.append((swap_pos(join(payload), 2 * c), pieces))
+    def spread_parts(k, own, kind, *needed):
+        held = [(own, [(k, 0, kind)])]
+        if kind is eighth:
+            held += [(swap_pos(own, 2 * c), [(k, 2 * c, kind)]) for c in range(1, CHIPS)]
         across = join([h[0] for h in held])
         across = after(across, *needed) if needed else across
         held.append((swap_pos(across, 1), [(k, flip + 1, p) for h in held for k, flip, p in h[1]]))
         for part, pieces in held:
             parts.append(part)
             plan.append(pieces)
-        return held
-
-    def get(k, *deps):
-        src = sources[MODES[k]]
-        return swap_wt(after(src, *deps) if deps else src, k)
+        return [h[0] for h in held[1:-1]]
 
     def taken(group):
         away = gather((1, 2, 3), group, meta, order, features)
         return gather((0,), group, meta, order, features) + away
 
 
-    owned = {k: get(k) for k in range(2, n_wt)}
-    owned[1] = get(1, owned[3])
+    owned = {k: swap_wt(far, k) for k in range(2, n_wt)}
+    owned[1] = swap_wt(after(near, owned[n_wt - 1]) if n_wt > 2 else near, 1)
     pairs0, pairs1 = taken(0), taken(1)
     first = cross(pairs0)
-    spread_parts([(1, owned[1])])
-    held3 = spread_parts([(3, after(owned[3], first[0][1:]))])
-    held2 = spread_parts([(2, after(owned[2], first[0][1:]))], pairs1, pairs0)
-    pairs = after(pairs1, [h[0] for h in held3[1:-1]])
+    spread_parts(1, owned[1], halves)
+    shared = []
+    for k in range(n_wt - 1, 1, -1):
+        needed = (pairs1, pairs0) if k == 2 else ()
+        moved = spread_parts(k, after(owned[k], first[0][1:]), eighth, *needed)
+        shared = shared or moved
+    pairs = after(pairs1, shared)
     second = [pairs[0]] + [swap_pos(pairs[c], 2 * c) for c in range(1, CHIPS)]
     weights = place(n_wt, plan, meta, switch_in, switch_out, parts)
     bias = hidden_bias.reshape(1, -1)

time: 80.7 us -> 80.7 us (level)
  no operation moved by 1% of the time
where the time goes in v5:
time: 80.7 us; the launch traced here: 80.5 us
  starting transfers between devices  31.9 us (40%)
  Pallas kernels  29.2 us (36%)
  waiting for transfers between devices  15 us (19%)
  local copies, waits for them, and re-layouts  2.36 us (3%)
  other arithmetic  1.47 us (2%)
    ppermute x25, starting transfers between devices, swap_pos(): return lax.ppermute(x, 'pos', [(i, i ^ spread(k)) for i in range(n_pos)])  22.2 us
    pallas_call x2, Pallas kernels, run_levels(): pl.pallas_call(levels_kernel, out_shape=[jax.ShapeDtypeStruct((2, rows, w...  17.5 us
    ppermute x25, waiting for transfers between devices, swap_pos(): return lax.ppermute(x, 'pos', [(i, i ^ spread(k)) for i in range(n_pos)])  15 us
    ppermute x3, starting transfers between devices, swap_wt(): return lax.ppermute(x, 'wt', [(i, i ^ k) for i in range(n_wt)])  9.74 us
    pallas_call x4, Pallas kernels, gather(): pl.pallas_call(functools.partial(gather_kernel, chips, group), out_shape=...  7.8 us
    pallas_call x2, Pallas kernels, finish(): pl.pallas_call(functools.partial(finish_kernel, first_row, share), out_sh...  2.96 us
    unnamed x14, local copies, waits for them, and re-layouts  2.12 us
  transfers between devices with their start and end apart: 28, of which 7 were waited for; matrix products, arithmetic and copies ran while one was open for 1% of the time, Pallas kernels for 34%

profile of v5, /device:TPU:0, one launch (start us, length us, event | category | flops | bytes accessed | tf_op | source)
XLA Modules:
  0.0 80.5 jit_solution(8168017337404675536)
XLA Ops:
  1.0 4.1 %collective-permute-start.10 = (bf16[96,768]{1,0:T(8,128)(2,1)S(1)}, bf16[96,768]{1,0:T(8,128)(2,1)S(1)}, u32[]{:S(2)}, u32[]{:S(2)}) collective-permute-start(bf16[96,768]{1,0:T(8,128)(2,1)S(1)} %dynamic-slice_select_fusion), channel_id=1, source_target_pairs={{0,2},{1,3},{2,0},{3,1},{4,6},{5,7},{6,4},{7,5},{8,10},{9,11},{10,... | collective-permute-start | bytes 442376 | tf_op jit(solution)/shard_map/ppermute | solution.py:198
  5.1 1.3 %collective-permute-start = (bf16[96,768]{1,0:T(8,128)(2,1)S(1)}, bf16[96,768]{1,0:T(8,128)(2,1)S(1)}, u32[]{:S(2)}, u32[]{:S(2)}) collective-permute-start(bf16[96,768]{1,0:T(8,128)(2,1)S(1)} %dynamic-slice_select_fusion), channel_id=1, source_target_pairs={{0,3},{1,2},{2,1},{3,0},{4,7},{5,6},{6,5},{7,4},{8,11},{9,10},{10,... | collective-permute-start | bytes 442376 | tf_op jit(solution)/shard_map/ppermute | solution.py:198
  6.5 1.4 %copy-done = bf16[2048,384]{1,0:T(8,128)(2,1)S(1)} copy-done((bf16[2048,384]{1,0:T(8,128)(2,1)S(1)}, bf16[2048,384]{1,0:T(8,128)(2,1)}, u32[]{:S(2)}) %copy-start) | copy-done | bytes 1572888
  8.7 2.5 %shard_map.55 = (bf16[2,128,384]{2,1,0:T(8,128)(2,1)S(1)}, bf16[2,128,384]{2,1,0:T(8,128)(2,1)S(1)}, bf16[2,128,384]{2,1,0:T(8,128)(2,1)S(1)}) custom-call(s32[2]{0:T(128)S(1)} %pad_add_fusion.meta_ref, s32[16,128]{1,0:T(8,128)S(1)} %bitcast.3, bf16[2048,384]{1,0:T(8,128)(2,1)S(1)} %copy-done), custom_call_target="tpu_custom_call" | custom-call | flops 48318382080 | bytes 3145728 | tf_op jit(solution)/shard_map/pallas_call | solution.py:55
  11.2 1.6 %collective-permute-start.3 = (bf16[2,128,384]{2,1,0:T(8,128)(2,1)S(1)}, bf16[2,128,384]{2,1,0:T(8,128)(2,1)S(1)}, u32[]{:S(2)}, u32[]{:S(2)}) collective-permute-start(bf16[2,128,384]{2,1,0:T(8,128)(2,1)S(1)} %get-tuple-element.32), channel_id=1, source_target_pairs={{0,8},{4,12},{8,0},{12,4},{16,24},{20,28},{24,16},{28,20},{1,9},{5... | collective-permute-start | bytes 589832 | tf_op jit(solution)/shard_map/ppermute | solution.py:195
  12.8 1.5 %collective-permute-start.4 = (bf16[2,128,384]{2,1,0:T(8,128)(2,1)S(1)}, bf16[2,128,384]{2,1,0:T(8,128)(2,1)S(1)}, u32[]{:S(2)}, u32[]{:S(2)}) collective-permute-start(bf16[2,128,384]{2,1,0:T(8,128)(2,1)S(1)} %get-tuple-element.33), channel_id=1, source_target_pairs={{0,16},{4,20},{8,24},{12,28},{16,0},{20,4},{24,8},{28,12},{1,17},{... | collective-permute-start | bytes 589832 | tf_op jit(solution)/shard_map/ppermute | solution.py:195
  14.9 4.3 %collective-permute-start.1 = (bf16[384,768]{1,0:T(8,128)(2,1)S(1)}, bf16[384,768]{1,0:T(8,128)(2,1)S(1)}, u32[]{:S(2)}, u32[]{:S(2)}) collective-permute-start(bf16[384,768]{1,0:T(8,128)(2,1)S(1)} %pad_maximum_fusion), channel_id=1, source_target_pairs={{0,1},{1,0},{2,3},{3,2},{4,5},{5,4},{6,7},{7,6},{8,9},{9,8},{10,11... | collective-permute-start | bytes 1769480 | tf_op jit(solution)/shard_map/ppermute | solution.py:198
  19.2 3.6 %collective-permute-done.4.rest_2_ = bf16[2,128,384]{2,1,0:T(8,128)(2,1)S(1)} collective-permute-done((bf16[2,128,384]{2,1,0:T(8,128)(2,1)S(1)}, bf16[2,128,384]{2,1,0:T(8,128)(2,1)S(1)}, u32[]{:S(2)}, u32[]{:S(2)}) %collective-permute-start.4) | collective-permute-done | bytes 196640 | tf_op jit(solution)/shard_map/ppermute | solution.py:195
  24.9 1.4 %collective-permute-start.13 = (bf16[96,768]{1,0:T(8,128)(2,1)S(1)}, bf16[96,768]{1,0:T(8,128)(2,1)S(1)}, u32[]{:S(2)}, u32[]{:S(2)}) collective-permute-start(bf16[96,768]{1,0:T(8,128)(2,1)S(1)} %collective-permute-done.10.rest_7_), channel_id=1, source_target_pairs={{0,24},{4,28},{8,16},{12,20},{16,8},{20,12},{24,0},{28,4},{1,25},{... | collective-permute-start | bytes 442376 | tf_op jit(solution)/shard_map/ppermute | solution.py:195
  26.3 2.5 %shard_map.57 = (bf16[2,128,384]{2,1,0:T(8,128)(2,1)S(1)}, bf16[2,128,384]{2,1,0:T(8,128)(2,1)S(1)}, bf16[2,128,384]{2,1,0:T(8,128)(2,1)S(1)}) custom-call(s32[2]{0:T(128)S(1)} %pad_add_fusion.meta_ref, s32[16,128]{1,0:T(8,128)S(1)} %bitcast.4, bf16[2048,384]{1,0:T(8,128)(2,1)S(1)} %copy-done.1), custom_call_target="tpu_custom_call" | custom-call | flops 48318382080 | bytes 3145728 | tf_op jit(solution)/shard_map/pallas_call | solution.py:55
  28.8 1.3 %shard_map.58.rest_0_ = bf16[2,128,384]{2,1,0:T(8,128)(2,1)S(1)} custom-call(s32[2]{0:T(128)S(1)} %pad_add_fusion.meta_ref, s32[16,128]{1,0:T(8,128)S(1)} %bitcast.5, bf16[2048,384]{1,0:T(8,128)(2,1)S(1)} %copy-done.1), custom_call_target="tpu_custom_call" | custom-call | flops 402653184 | bytes 3145728 | tf_op jit(solution)/shard_map/pallas_call | solution.py:55
  32.3 1.4 %collective-permute-start.8 = (bf16[96,768]{1,0:T(8,128)(2,1)S(1)}, bf16[96,768]{1,0:T(8,128)(2,1)S(1)}, u32[]{:S(2)}, u32[]{:S(2)}) collective-permute-start(bf16[96,768]{1,0:T(8,128)(2,1)S(1)} %collective-permute-done.rest_2_), channel_id=1, source_target_pairs={{0,24},{4,28},{8,16},{12,20},{16,8},{20,12},{24,0},{28,4},{1,25},{... | collective-permute-start | bytes 442376 | tf_op jit(solution)/shard_map/ppermute | solution.py:195
  33.8 1.4 %shard_map.56.rest_0_ = bf16[2,128,384]{2,1,0:T(8,128)(2,1)S(1)} custom-call(s32[2]{0:T(128)S(1)} %pad_add_fusion.meta_ref, s32[16,128]{1,0:T(8,128)S(1)} %bitcast.6, bf16[2048,384]{1,0:T(8,128)(2,1)S(1)} %copy-done.1), custom_call_target="tpu_custom_call" | custom-call | flops 402653184 | bytes 3145728 | tf_op jit(solution)/shard_map/pallas_call | solution.py:55
  36.6 1.7 %collective-permute-done.8.rest_5_ = bf16[96,768]{1,0:T(8,128)(2,1)S(1)} collective-permute-done((bf16[96,768]{1,0:T(8,128)(2,1)S(1)}, bf16[96,768]{1,0:T(8,128)(2,1)S(1)}, u32[]{:S(2)}, u32[]{:S(2)}) %collective-permute-start.8) | collective-permute-done | bytes 147488 | tf_op jit(solution)/shard_map/ppermute | solution.py:195
  39.3 1.5 %collective-permute-start.15 = (bf16[2,128,384]{2,1,0:T(8,128)(2,1)S(1)}, bf16[2,128,384]{2,1,0:T(8,128)(2,1)S(1)}, u32[]{:S(2)}, u32[]{:S(2)}) collective-permute-start(bf16[2,128,384]{2,1,0:T(8,128)(2,1)S(1)} %get-tuple-element.42), channel_id=1, source_target_pairs={{0,8},{4,12},{8,0},{12,4},{16,24},{20,28},{24,16},{28,20},{1,9},{5... | collective-permute-start | bytes 589832 | tf_op jit(solution)/shard_map/ppermute | solution.py:195
  43.7 8.9 %shard_map.60 = (bf16[2,128,384]{2,1,0:T(8,128)(2,1)S(1)}, bf16[2,128,384]{2,1,0:T(8,128)(2,1)S(1)}, bf16[2,128,384]{2,1,0:T(8,128)(2,1)S(1)}, bf16[2,128,384]{2,1,0:T(8,128)(2,1)S(1)}) custom-call(s32[2]{0:T(128)S(1)} %pad_add_fusion.meta_ref, bf16[3072,768]{1,0:T(8,128)(2,1)S(1)} %shard_map.59.weights_ref, f32[1,1536]{1,0:T(1,128)S(1)} %reshape.7.bias_ref, ...), custom_call_target="tpu_custom_call" | custom-call | flops 144955152 | bytes 94371 | tf_op jit(solution)/shard_map/pallas_call | solution.py:140
  52.9 1.5 %collective-permute-start.24 = (bf16[2,128,384]{2,1,0:T(8,128)(2,1)S(1)}, bf16[2,128,384]{2,1,0:T(8,128)(2,1)S(1)}, u32[]{:S(2)}, u32[]{:S(2)}) collective-permute-start(bf16[2,128,384]{2,1,0:T(8,128)(2,1)S(1)} %get-tuple-element.46), channel_id=1, source_target_pairs={{0,8},{4,12},{8,0},{12,4},{16,24},{20,28},{24,16},{28,20},{1,9},{5... | collective-permute-start | bytes 589832 | tf_op jit(solution)/shard_map/ppermute | solution.py:195
  55.1 1.3 %collective-permute-start.26 = (bf16[2,128,384]{2,1,0:T(8,128)(2,1)S(1)}, bf16[2,128,384]{2,1,0:T(8,128)(2,1)S(1)}, u32[]{:S(2)}, u32[]{:S(2)}) collective-permute-start(bf16[2,128,384]{2,1,0:T(8,128)(2,1)S(1)} %get-tuple-element.48), channel_id=1, source_target_pairs={{0,24},{4,28},{8,16},{12,20},{16,8},{20,12},{24,0},{28,4},{1,25},{... | collective-permute-start | bytes 589832 | tf_op jit(solution)/shard_map/ppermute | solution.py:195
  56.4 8.7 %shard_map.61 = (bf16[2,128,384]{2,1,0:T(8,128)(2,1)S(1)}, bf16[2,128,384]{2,1,0:T(8,128)(2,1)S(1)}, bf16[2,128,384]{2,1,0:T(8,128)(2,1)S(1)}, bf16[2,128,384]{2,1,0:T(8,128)(2,1)S(1)}) custom-call(s32[2]{0:T(128)S(1)} %pad_add_fusion.meta_ref, bf16[3072,768]{1,0:T(8,128)(2,1)S(1)} %shard_map.59.weights_ref, f32[1,1536]{1,0:T(1,128)S(1)} %reshape.7.bias_ref, ...), custom_call_target="tpu_custom_call" | custom-call | flops 144955152 | bytes 94371 | tf_op jit(solution)/shard_map/pallas_call | solution.py:140
  65.1 1.5 %collective-permute-start.20 = (bf16[2,128,384]{2,1,0:T(8,128)(2,1)S(1)}, bf16[2,128,384]{2,1,0:T(8,128)(2,1)S(1)}, u32[]{:S(2)}, u32[]{:S(2)}) collective-permute-start(bf16[2,128,384]{2,1,0:T(8,128)(2,1)S(1)} %get-tuple-element.54), channel_id=1, source_target_pairs={{0,8},{4,12},{8,0},{12,4},{16,24},{20,28},{24,16},{28,20},{1,9},{5... | collective-permute-start | bytes 589832 | tf_op jit(solution)/shard_map/ppermute | solution.py:195
  68.9 4.1 %collective-permute-done.20.rest_1_ = bf16[2,128,384]{2,1,0:T(8,128)(2,1)S(1)} collective-permute-done((bf16[2,128,384]{2,1,0:T(8,128)(2,1)S(1)}, bf16[2,128,384]{2,1,0:T(8,128)(2,1)S(1)}, u32[]{:S(2)}, u32[]{:S(2)}) %collective-permute-start.20) | collective-permute-done | bytes 196640 | tf_op jit(solution)/shard_map/ppermute | solution.py:195
  73.0 4.0 %collective-permute-done.21.rest_2_ = bf16[2,128,384]{2,1,0:T(8,128)(2,1)S(1)} collective-permute-done((bf16[2,128,384]{2,1,0:T(8,128)(2,1)S(1)}, bf16[2,128,384]{2,1,0:T(8,128)(2,1)S(1)}, u32[]{:S(2)}, u32[]{:S(2)}) %collective-permute-start.21) | collective-permute-done | bytes 196640 | tf_op jit(solution)/shard_map/ppermute | solution.py:195
  77.2 1.5 %shard_map.62.rest_5_ = bf16[2048,384]{1,0:T(8,128)(2,1)} custom-call(s32[2]{0:T(128)S(1)} %pad_add_fusion.meta_ref, bf16[2,128,384]{2,1,0:T(8,128)(2,1)S(1)} %get-tuple-element.45.rest_0_, bf16[2,128,384]{2,1,0:T(8,128)(2,1)S(1)} %collective-permute-done.24.rest_1_, bf16[2,128,384]{2,1,0:T(8,128)(2,1)S(1)} %collective-permute-done.25.rest_2_, ...), custom_call_target="tpu_custom_call" | custom-call | bytes 1572864 | tf_op jit(solution)/shard_map/pallas_call | solution.py:172
  78.9 1.5 %shard_map.63 = bf16[2048,384]{1,0:T(8,128)(2,1)} custom-call(s32[2]{0:T(128)S(1)} %pad_add_fusion.meta_ref, bf16[2,128,384]{2,1,0:T(8,128)(2,1)S(1)} %get-tuple-element.53.rest_0_, bf16[2,128,384]{2,1,0:T(8,128)(2,1)S(1)} %collective-permute-done.20.rest_1_, ...), custom_call_target="tpu_custom_call", output_to_operand_aliasing={{}: (6, {})} | custom-call | bytes 1572864 | tf_op jit(solution)/shard_map/pallas_call | solution.py:172
  (82 shorter events, 15.3 us)
Async XLA Ops:
  1.0 18.2 %collective-permute-start.10 = (bf16[96,768]{1,0:T(8,128)(2,1)S(1)}, bf16[96,768]{1,0:T(8,128)(2,1)S(1)}, u32[]{:S(2)}, u32[]{:S(2)}) collective-permute-start(bf16[96,768]{1,0:T(8,128)(2,1)S(1)} %dynamic-slice_select_fusion), channel_id=1, source_target_pairs={{0,2},{1,3},{2,0},{3,1},{4,6},{5,7},{6,4},{7,5},{8,10},{9,11},{10,... | collective-permute-start | bytes 442376 | tf_op jit(solution)/shard_map/ppermute | solution.py:198
  5.1 9.7 %collective-permute-start = (bf16[96,768]{1,0:T(8,128)(2,1)S(1)}, bf16[96,768]{1,0:T(8,128)(2,1)S(1)}, u32[]{:S(2)}, u32[]{:S(2)}) collective-permute-start(bf16[96,768]{1,0:T(8,128)(2,1)S(1)} %dynamic-slice_select_fusion), channel_id=1, source_target_pairs={{0,3},{1,2},{2,1},{3,0},{4,7},{5,6},{6,5},{7,4},{8,11},{9,10},{10,... | collective-permute-start | bytes 442376 | tf_op jit(solution)/shard_map/ppermute | solution.py:198
  11.2 8.0 %collective-permute-start.3 = (bf16[2,128,384]{2,1,0:T(8,128)(2,1)S(1)}, bf16[2,128,384]{2,1,0:T(8,128)(2,1)S(1)}, u32[]{:S(2)}, u32[]{:S(2)}) collective-permute-start(bf16[2,128,384]{2,1,0:T(8,128)(2,1)S(1)} %get-tuple-element.32), channel_id=1, source_target_pairs={{0,8},{4,12},{8,0},{12,4},{16,24},{20,28},{24,16},{28,20},{1,9},{5... | collective-permute-start | bytes 589832 | tf_op jit(solution)/shard_map/ppermute | solution.py:195
  12.8 10.0 %collective-permute-start.4 = (bf16[2,128,384]{2,1,0:T(8,128)(2,1)S(1)}, bf16[2,128,384]{2,1,0:T(8,128)(2,1)S(1)}, u32[]{:S(2)}, u32[]{:S(2)}) collective-permute-start(bf16[2,128,384]{2,1,0:T(8,128)(2,1)S(1)} %get-tuple-element.33), channel_id=1, source_target_pairs={{0,16},{4,20},{8,24},{12,28},{16,0},{20,4},{24,8},{28,12},{1,17},{... | collective-permute-start | bytes 589832 | tf_op jit(solution)/shard_map/ppermute | solution.py:195
  14.3 8.5 %collective-permute-start.5 = (bf16[2,128,384]{2,1,0:T(8,128)(2,1)S(1)}, bf16[2,128,384]{2,1,0:T(8,128)(2,1)S(1)}, u32[]{:S(2)}, u32[]{:S(2)}) collective-permute-start(bf16[2,128,384]{2,1,0:T(8,128)(2,1)S(1)} %get-tuple-element.34), channel_id=1, source_target_pairs={{0,24},{4,28},{8,16},{12,20},{16,8},{20,12},{24,0},{28,4},{1,25},{... | collective-permute-start | bytes 589832 | tf_op jit(solution)/shard_map/ppermute | solution.py:195
  14.9 23.6 %collective-permute-start.1 = (bf16[384,768]{1,0:T(8,128)(2,1)S(1)}, bf16[384,768]{1,0:T(8,128)(2,1)S(1)}, u32[]{:S(2)}, u32[]{:S(2)}) collective-permute-start(bf16[384,768]{1,0:T(8,128)(2,1)S(1)} %pad_maximum_fusion), channel_id=1, source_target_pairs={{0,1},{1,0},{2,3},{3,2},{4,5},{5,4},{6,7},{7,6},{8,9},{9,8},{10,11... | collective-permute-start | bytes 1769480 | tf_op jit(solution)/shard_map/ppermute | solution.py:198
  22.8 8.7 %collective-permute-start.11 = (bf16[96,768]{1,0:T(8,128)(2,1)S(1)}, bf16[96,768]{1,0:T(8,128)(2,1)S(1)}, u32[]{:S(2)}, u32[]{:S(2)}) collective-permute-start(bf16[96,768]{1,0:T(8,128)(2,1)S(1)} %collective-permute-done.10.rest_7_), channel_id=1, source_target_pairs={{0,8},{4,12},{8,0},{12,4},{16,24},{20,28},{24,16},{28,20},{1,9},{5... | collective-permute-start | bytes 442376 | tf_op jit(solution)/shard_map/ppermute | solution.py:195
  24.0 8.3 %collective-permute-start.12 = (bf16[96,768]{1,0:T(8,128)(2,1)S(1)}, bf16[96,768]{1,0:T(8,128)(2,1)S(1)}, u32[]{:S(2)}, u32[]{:S(2)}) collective-permute-start(bf16[96,768]{1,0:T(8,128)(2,1)S(1)} %collective-permute-done.10.rest_7_), channel_id=1, source_target_pairs={{0,16},{4,20},{8,24},{12,28},{16,0},{20,4},{24,8},{28,12},{1,17},{... | collective-permute-start | bytes 442376 | tf_op jit(solution)/shard_map/ppermute | solution.py:195
  24.9 10.3 %collective-permute-start.13 = (bf16[96,768]{1,0:T(8,128)(2,1)S(1)}, bf16[96,768]{1,0:T(8,128)(2,1)S(1)}, u32[]{:S(2)}, u32[]{:S(2)}) collective-permute-start(bf16[96,768]{1,0:T(8,128)(2,1)S(1)} %collective-permute-done.10.rest_7_), channel_id=1, source_target_pairs={{0,24},{4,28},{8,16},{12,20},{16,8},{20,12},{24,0},{28,4},{1,25},{... | collective-permute-start | bytes 442376 | tf_op jit(solution)/shard_map/ppermute | solution.py:195
  30.2 5.5 %collective-permute-start.6 = (bf16[96,768]{1,0:T(8,128)(2,1)S(1)}, bf16[96,768]{1,0:T(8,128)(2,1)S(1)}, u32[]{:S(2)}, u32[]{:S(2)}) collective-permute-start(bf16[96,768]{1,0:T(8,128)(2,1)S(1)} %collective-permute-done.rest_2_), channel_id=1, source_target_pairs={{0,8},{4,12},{8,0},{12,4},{16,24},{20,28},{24,16},{28,20},{1,9},{5... | collective-permute-start | bytes 442376 | tf_op jit(solution)/shard_map/ppermute | solution.py:195
  31.5 5.1 %collective-permute-start.7 = (bf16[96,768]{1,0:T(8,128)(2,1)S(1)}, bf16[96,768]{1,0:T(8,128)(2,1)S(1)}, u32[]{:S(2)}, u32[]{:S(2)}) collective-permute-start(bf16[96,768]{1,0:T(8,128)(2,1)S(1)} %collective-permute-done.rest_2_), channel_id=1, source_target_pairs={{0,16},{4,20},{8,24},{12,28},{16,0},{20,4},{24,8},{28,12},{1,17},{... | collective-permute-start | bytes 442376 | tf_op jit(solution)/shard_map/ppermute | solution.py:195
  32.3 6.0 %collective-permute-start.8 = (bf16[96,768]{1,0:T(8,128)(2,1)S(1)}, bf16[96,768]{1,0:T(8,128)(2,1)S(1)}, u32[]{:S(2)}, u32[]{:S(2)}) collective-permute-start(bf16[96,768]{1,0:T(8,128)(2,1)S(1)} %collective-permute-done.rest_2_), channel_id=1, source_target_pairs={{0,24},{4,28},{8,16},{12,20},{16,8},{20,12},{24,0},{28,4},{1,25},{... | collective-permute-start | bytes 442376 | tf_op jit(solution)/shard_map/ppermute | solution.py:195
  35.2 5.6 %collective-permute-start.14 = (bf16[384,768]{1,0:T(8,128)(2,1)S(1)}, bf16[384,768]{1,0:T(8,128)(2,1)S(1)}, u32[]{:S(2)}, u32[]{:S(2)}) collective-permute-start(bf16[384,768]{1,0:T(8,128)(2,1)S(1)} %pad_maximum_fusion.2), channel_id=1, source_target_pairs={{0,4},{4,0},{8,12},{12,8},{16,20},{20,16},{24,28},{28,24},{1,5},{5... | collective-permute-start | bytes 1769480 | tf_op jit(solution)/shard_map/ppermute | solution.py:195
  39.2 4.5 %collective-permute-start.18 = (bf16[4,128,384]{2,1,0:T(8,128)(2,1)S(1)}, bf16[4,128,384]{2,1,0:T(8,128)(2,1)S(1)}, u32[]{:S(2)}, u32[]{:S(2)}) collective-permute-start(bf16[4,128,384]{2,1,0:T(8,128)(2,1)S(1)} %pad_maximum_fusion.3), channel_id=1, source_target_pairs={{0,4},{4,0},{8,12},{12,8},{16,20},{20,16},{24,28},{28,24},{1,5},{5... | collective-permute-start | bytes 1179656 | tf_op jit(solution)/shard_map/ppermute | solution.py:195
  39.3 13.3 %collective-permute-start.15 = (bf16[2,128,384]{2,1,0:T(8,128)(2,1)S(1)}, bf16[2,128,384]{2,1,0:T(8,128)(2,1)S(1)}, u32[]{:S(2)}, u32[]{:S(2)}) collective-permute-start(bf16[2,128,384]{2,1,0:T(8,128)(2,1)S(1)} %get-tuple-element.42), channel_id=1, source_target_pairs={{0,8},{4,12},{8,0},{12,4},{16,24},{20,28},{24,16},{28,20},{1,9},{5... | collective-permute-start | bytes 589832 | tf_op jit(solution)/shard_map/ppermute | solution.py:195
  40.8 11.8 %collective-permute-start.16 = (bf16[2,128,384]{2,1,0:T(8,128)(2,1)S(1)}, bf16[2,128,384]{2,1,0:T(8,128)(2,1)S(1)}, u32[]{:S(2)}, u32[]{:S(2)}) collective-permute-start(bf16[2,128,384]{2,1,0:T(8,128)(2,1)S(1)} %get-tuple-element.43), channel_id=1, source_target_pairs={{0,16},{4,20},{8,24},{12,28},{16,0},{20,4},{24,8},{28,12},{1,17},{... | collective-permute-start | bytes 589832 | tf_op jit(solution)/shard_map/ppermute | solution.py:195
  41.5 11.1 %collective-permute-start.17 = (bf16[2,128,384]{2,1,0:T(8,128)(2,1)S(1)}, bf16[2,128,384]{2,1,0:T(8,128)(2,1)S(1)}, u32[]{:S(2)}, u32[]{:S(2)}) collective-permute-start(bf16[2,128,384]{2,1,0:T(8,128)(2,1)S(1)} %get-tuple-element.44), channel_id=1, source_target_pairs={{0,24},{4,28},{8,16},{12,20},{16,8},{20,12},{24,0},{28,4},{1,25},{... | collective-permute-start | bytes 589832 | tf_op jit(solution)/shard_map/ppermute | solution.py:195
  52.9 14.4 %collective-permute-start.24 = (bf16[2,128,384]{2,1,0:T(8,128)(2,1)S(1)}, bf16[2,128,384]{2,1,0:T(8,128)(2,1)S(1)}, u32[]{:S(2)}, u32[]{:S(2)}) collective-permute-start(bf16[2,128,384]{2,1,0:T(8,128)(2,1)S(1)} %get-tuple-element.46), channel_id=1, source_target_pairs={{0,8},{4,12},{8,0},{12,4},{16,24},{20,28},{24,16},{28,20},{1,9},{5... | collective-permute-start | bytes 589832 | tf_op jit(solution)/shard_map/ppermute | solution.py:195
  54.4 14.3 %collective-permute-start.25 = (bf16[2,128,384]{2,1,0:T(8,128)(2,1)S(1)}, bf16[2,128,384]{2,1,0:T(8,128)(2,1)S(1)}, u32[]{:S(2)}, u32[]{:S(2)}) collective-permute-start(bf16[2,128,384]{2,1,0:T(8,128)(2,1)S(1)} %get-tuple-element.47), channel_id=1, source_target_pairs={{0,16},{4,20},{8,24},{12,28},{16,0},{20,4},{24,8},{28,12},{1,17},{... | collective-permute-start | bytes 589832 | tf_op jit(solution)/shard_map/ppermute | solution.py:195
  55.1 13.6 %collective-permute-start.26 = (bf16[2,128,384]{2,1,0:T(8,128)(2,1)S(1)}, bf16[2,128,384]{2,1,0:T(8,128)(2,1)S(1)}, u32[]{:S(2)}, u32[]{:S(2)}) collective-permute-start(bf16[2,128,384]{2,1,0:T(8,128)(2,1)S(1)} %get-tuple-element.48), channel_id=1, source_target_pairs={{0,24},{4,28},{8,16},{12,20},{16,8},{20,12},{24,0},{28,4},{1,25},{... | collective-permute-start | bytes 589832 | tf_op jit(solution)/shard_map/ppermute | solution.py:195
  65.1 7.9 %collective-permute-start.20 = (bf16[2,128,384]{2,1,0:T(8,128)(2,1)S(1)}, bf16[2,128,384]{2,1,0:T(8,128)(2,1)S(1)}, u32[]{:S(2)}, u32[]{:S(2)}) collective-permute-start(bf16[2,128,384]{2,1,0:T(8,128)(2,1)S(1)} %get-tuple-element.54), channel_id=1, source_target_pairs={{0,8},{4,12},{8,0},{12,4},{16,24},{20,28},{24,16},{28,20},{1,9},{5... | collective-permute-start | bytes 589832 | tf_op jit(solution)/shard_map/ppermute | solution.py:195
  66.6 10.3 %collective-permute-start.21 = (bf16[2,128,384]{2,1,0:T(8,128)(2,1)S(1)}, bf16[2,128,384]{2,1,0:T(8,128)(2,1)S(1)}, u32[]{:S(2)}, u32[]{:S(2)}) collective-permute-start(bf16[2,128,384]{2,1,0:T(8,128)(2,1)S(1)} %get-tuple-element.55), channel_id=1, source_target_pairs={{0,16},{4,20},{8,24},{12,28},{16,0},{20,4},{24,8},{28,12},{1,17},{... | collective-permute-start | bytes 589832 | tf_op jit(solution)/shard_map/ppermute | solution.py:195
  67.3 9.7 %collective-permute-start.22 = (bf16[2,128,384]{2,1,0:T(8,128)(2,1)S(1)}, bf16[2,128,384]{2,1,0:T(8,128)(2,1)S(1)}, u32[]{:S(2)}, u32[]{:S(2)}) collective-permute-start(bf16[2,128,384]{2,1,0:T(8,128)(2,1)S(1)} %get-tuple-element.56), channel_id=1, source_target_pairs={{0,24},{4,28},{8,16},{12,20},{16,8},{20,12},{24,0},{28,4},{1,25},{... | collective-permute-start | bytes 589832 | tf_op jit(solution)/shard_map/ppermute | solution.py:195
  68.8 8.4 %collective-permute-start.27 = (bf16[4,128,384]{2,1,0:T(8,128)(2,1)S(1)}, bf16[4,128,384]{2,1,0:T(8,128)(2,1)S(1)}, u32[]{:S(2)}, u32[]{:S(2)}) collective-permute-start(bf16[4,128,384]{2,1,0:T(8,128)(2,1)S(1)} %pad_maximum_fusion.6), channel_id=1, source_target_pairs={{0,4},{4,0},{8,12},{12,8},{16,20},{20,16},{24,28},{28,24},{1,5},{5... | collective-permute-start | bytes 1179656 | tf_op jit(solution)/shard_map/ppermute | solution.py:195
  (11 other events, 57.7 us)

commit v6 on v5

--- a/solution.py
+++ b/solution.py
@@ -112,8 +112,11 @@
     for level in range(LEVELS):
         bit = 1 << level
         lower = [i for i in range(MEMBERS) if not i & bit]
+        last = level == LEVELS - 1
+        if last:
+            lower = [jnp.bitwise_xor(me, k) & (CHIPS - 1) for k in range(CHIPS)]
         pair = jnp.concatenate(
-            [jnp.concatenate([state[i], state[i | bit]], axis=1) for i in lower], axis=0
+            [jnp.concatenate([state[i], state[i + bit]], axis=1) for i in lower], axis=0
         )
         made = []
         for c in range(2):
@@ -127,11 +130,14 @@
         mixed = (0.8 * pair.astype(jnp.float32) + 0.6 * total).astype(jnp.bfloat16)
         for j, i in enumerate(lower):
             made = mixed[j * rows : (j + 1) * rows]
-            state[i] = made[:, :width]
-            state[i | bit] = made[:, width:]
-    for c in range(CHIPS):
-        out_refs[c][0] = state[jnp.bitwise_xor(me, 2 * c)]
-        out_refs[c][1] = state[jnp.bitwise_xor(me, 2 * c + 1)]
+            low, high = made[:, :width], made[:, width:]
+            if last:
+                upper_here = (me & bit) != 0
+                out_refs[j // 2][j % 2] = jnp.where(upper_here, high, low)
+                out_refs[(j + bit) // 2][j % 2] = jnp.where(upper_here, low, high)
+            else:
+                state[i] = low
+                state[i + bit] = high
 
 
 def run_levels(meta, weights, bias, blocks, others):

time: 80.7 us -> 80.9 us (level)
  transfers between devices with their start and end apart: 28 -> 28, of which waited for: 7 -> 7; matrix products, arithmetic and copies ran while one was open for 1% -> 1% of each run, Pallas kernels for 34% -> 35%
where the time goes in v6:
time: 80.9 us; the launch traced here: 80.7 us
  starting transfers between devices  31.9 us (39%)
  Pallas kernels  29.4 us (36%)
  waiting for transfers between devices  15 us (19%)
  local copies, waits for them, and re-layouts  2.36 us (3%)
  other arithmetic  1.47 us (2%)
    ppermute x25, starting transfers between devices, swap_pos(): return lax.ppermute(x, 'pos', [(i, i ^ spread(k)) for i in range(n_pos)])  22.2 us
    pallas_call x2, Pallas kernels, run_levels(): pl.pallas_call(levels_kernel, out_shape=[jax.ShapeDtypeStruct((2, rows, w...  17.8 us
    ppermute x25, waiting for transfers between devices, swap_pos(): return lax.ppermute(x, 'pos', [(i, i ^ spread(k)) for i in range(n_pos)])  15 us
    ppermute x3, starting transfers between devices, swap_wt(): return lax.ppermute(x, 'wt', [(i, i ^ k) for i in range(n_wt)])  9.74 us
    pallas_call x4, Pallas kernels, gather(): pl.pallas_call(functools.partial(gather_kernel, chips, group), out_shape=...  7.8 us
    pallas_call x2, Pallas kernels, finish(): pl.pallas_call(functools.partial(finish_kernel, first_row, share), out_sh...  2.96 us
    unnamed x14, local copies, waits for them, and re-layouts  2.12 us
  transfers between devices with their start and end apart: 28, of which 7 were waited for; matrix products, arithmetic and copies ran while one was open for 1% of the time, Pallas kernels for 35%

profile of v6, /device:TPU:0, one launch (start us, length us, event | category | flops | bytes accessed | tf_op | source)
XLA Modules:
  0.0 80.7 jit_solution(1063397287729356672)
XLA Ops:
  1.0 4.1 %collective-permute-start.10 = (bf16[96,768]{1,0:T(8,128)(2,1)S(1)}, bf16[96,768]{1,0:T(8,128)(2,1)S(1)}, u32[]{:S(2)}, u32[]{:S(2)}) collective-permute-start(bf16[96,768]{1,0:T(8,128)(2,1)S(1)} %dynamic-slice_select_fusion), channel_id=1, source_target_pairs={{0,2},{1,3},{2,0},{3,1},{4,6},{5,7},{6,4},{7,5},{8,10},{9,11},{10,... | collective-permute-start | bytes 442376 | tf_op jit(solution)/shard_map/ppermute | solution.py:204
  5.1 1.3 %collective-permute-start = (bf16[96,768]{1,0:T(8,128)(2,1)S(1)}, bf16[96,768]{1,0:T(8,128)(2,1)S(1)}, u32[]{:S(2)}, u32[]{:S(2)}) collective-permute-start(bf16[96,768]{1,0:T(8,128)(2,1)S(1)} %dynamic-slice_select_fusion), channel_id=1, source_target_pairs={{0,3},{1,2},{2,1},{3,0},{4,7},{5,6},{6,5},{7,4},{8,11},{9,10},{10,... | collective-permute-start | bytes 442376 | tf_op jit(solution)/shard_map/ppermute | solution.py:204
  6.5 1.4 %copy-done = bf16[2048,384]{1,0:T(8,128)(2,1)S(1)} copy-done((bf16[2048,384]{1,0:T(8,128)(2,1)S(1)}, bf16[2048,384]{1,0:T(8,128)(2,1)}, u32[]{:S(2)}) %copy-start) | copy-done | bytes 1572888
  8.7 2.5 %shard_map.55 = (bf16[2,128,384]{2,1,0:T(8,128)(2,1)S(1)}, bf16[2,128,384]{2,1,0:T(8,128)(2,1)S(1)}, bf16[2,128,384]{2,1,0:T(8,128)(2,1)S(1)}) custom-call(s32[2]{0:T(128)S(1)} %pad_add_fusion.meta_ref, s32[16,128]{1,0:T(8,128)S(1)} %bitcast.3, bf16[2048,384]{1,0:T(8,128)(2,1)S(1)} %copy-done), custom_call_target="tpu_custom_call" | custom-call | flops 48318382080 | bytes 3145728 | tf_op jit(solution)/shard_map/pallas_call | solution.py:55
  11.2 1.6 %collective-permute-start.3 = (bf16[2,128,384]{2,1,0:T(8,128)(2,1)S(1)}, bf16[2,128,384]{2,1,0:T(8,128)(2,1)S(1)}, u32[]{:S(2)}, u32[]{:S(2)}) collective-permute-start(bf16[2,128,384]{2,1,0:T(8,128)(2,1)S(1)} %get-tuple-element.32), channel_id=1, source_target_pairs={{0,8},{4,12},{8,0},{12,4},{16,24},{20,28},{24,16},{28,20},{1,9},{5... | collective-permute-start | bytes 589832 | tf_op jit(solution)/shard_map/ppermute | solution.py:201
  12.8 1.5 %collective-permute-start.4 = (bf16[2,128,384]{2,1,0:T(8,128)(2,1)S(1)}, bf16[2,128,384]{2,1,0:T(8,128)(2,1)S(1)}, u32[]{:S(2)}, u32[]{:S(2)}) collective-permute-start(bf16[2,128,384]{2,1,0:T(8,128)(2,1)S(1)} %get-tuple-element.33), channel_id=1, source_target_pairs={{0,16},{4,20},{8,24},{12,28},{16,0},{20,4},{24,8},{28,12},{1,17},{... | collective-permute-start | bytes 589832 | tf_op jit(solution)/shard_map/ppermute | solution.py:201
  14.9 4.3 %collective-permute-start.1 = (bf16[384,768]{1,0:T(8,128)(2,1)S(1)}, bf16[384,768]{1,0:T(8,128)(2,1)S(1)}, u32[]{:S(2)}, u32[]{:S(2)}) collective-permute-start(bf16[384,768]{1,0:T(8,128)(2,1)S(1)} %pad_maximum_fusion), channel_id=1, source_target_pairs={{0,1},{1,0},{2,3},{3,2},{4,5},{5,4},{6,7},{7,6},{8,9},{9,8},{10,11... | collective-permute-start | bytes 1769480 | tf_op jit(solution)/shard_map/ppermute | solution.py:204
  19.2 3.6 %collective-permute-done.4.rest_2_ = bf16[2,128,384]{2,1,0:T(8,128)(2,1)S(1)} collective-permute-done((bf16[2,128,384]{2,1,0:T(8,128)(2,1)S(1)}, bf16[2,128,384]{2,1,0:T(8,128)(2,1)S(1)}, u32[]{:S(2)}, u32[]{:S(2)}) %collective-permute-start.4) | collective-permute-done | bytes 196640 | tf_op jit(solution)/shard_map/ppermute | solution.py:201
  24.9 1.4 %collective-permute-start.13 = (bf16[96,768]{1,0:T(8,128)(2,1)S(1)}, bf16[96,768]{1,0:T(8,128)(2,1)S(1)}, u32[]{:S(2)}, u32[]{:S(2)}) collective-permute-start(bf16[96,768]{1,0:T(8,128)(2,1)S(1)} %collective-permute-done.10.rest_7_), channel_id=1, source_target_pairs={{0,24},{4,28},{8,16},{12,20},{16,8},{20,12},{24,0},{28,4},{1,25},{... | collective-permute-start | bytes 442376 | tf_op jit(solution)/shard_map/ppermute | solution.py:201
  26.3 2.5 %shard_map.57 = (bf16[2,128,384]{2,1,0:T(8,128)(2,1)S(1)}, bf16[2,128,384]{2,1,0:T(8,128)(2,1)S(1)}, bf16[2,128,384]{2,1,0:T(8,128)(2,1)S(1)}) custom-call(s32[2]{0:T(128)S(1)} %pad_add_fusion.meta_ref, s32[16,128]{1,0:T(8,128)S(1)} %bitcast.4, bf16[2048,384]{1,0:T(8,128)(2,1)S(1)} %copy-done.1), custom_call_target="tpu_custom_call" | custom-call | flops 48318382080 | bytes 3145728 | tf_op jit(solution)/shard_map/pallas_call | solution.py:55
  28.8 1.3 %shard_map.58.rest_0_ = bf16[2,128,384]{2,1,0:T(8,128)(2,1)S(1)} custom-call(s32[2]{0:T(128)S(1)} %pad_add_fusion.meta_ref, s32[16,128]{1,0:T(8,128)S(1)} %bitcast.5, bf16[2048,384]{1,0:T(8,128)(2,1)S(1)} %copy-done.1), custom_call_target="tpu_custom_call" | custom-call | flops 402653184 | bytes 3145728 | tf_op jit(solution)/shard_map/pallas_call | solution.py:55
  32.3 1.4 %collective-permute-start.8 = (bf16[96,768]{1,0:T(8,128)(2,1)S(1)}, bf16[96,768]{1,0:T(8,128)(2,1)S(1)}, u32[]{:S(2)}, u32[]{:S(2)}) collective-permute-start(bf16[96,768]{1,0:T(8,128)(2,1)S(1)} %collective-permute-done.rest_2_), channel_id=1, source_target_pairs={{0,24},{4,28},{8,16},{12,20},{16,8},{20,12},{24,0},{28,4},{1,25},{... | collective-permute-start | bytes 442376 | tf_op jit(solution)/shard_map/ppermute | solution.py:201
  33.8 1.4 %shard_map.56.rest_0_ = bf16[2,128,384]{2,1,0:T(8,128)(2,1)S(1)} custom-call(s32[2]{0:T(128)S(1)} %pad_add_fusion.meta_ref, s32[16,128]{1,0:T(8,128)S(1)} %bitcast.6, bf16[2048,384]{1,0:T(8,128)(2,1)S(1)} %copy-done.1), custom_call_target="tpu_custom_call" | custom-call | flops 402653184 | bytes 3145728 | tf_op jit(solution)/shard_map/pallas_call | solution.py:55
  36.6 1.7 %collective-permute-done.8.rest_5_ = bf16[96,768]{1,0:T(8,128)(2,1)S(1)} collective-permute-done((bf16[96,768]{1,0:T(8,128)(2,1)S(1)}, bf16[96,768]{1,0:T(8,128)(2,1)S(1)}, u32[]{:S(2)}, u32[]{:S(2)}) %collective-permute-start.8) | collective-permute-done | bytes 147488 | tf_op jit(solution)/shard_map/ppermute | solution.py:201
  39.3 1.5 %collective-permute-start.15 = (bf16[2,128,384]{2,1,0:T(8,128)(2,1)S(1)}, bf16[2,128,384]{2,1,0:T(8,128)(2,1)S(1)}, u32[]{:S(2)}, u32[]{:S(2)}) collective-permute-start(bf16[2,128,384]{2,1,0:T(8,128)(2,1)S(1)} %get-tuple-element.42), channel_id=1, source_target_pairs={{0,8},{4,12},{8,0},{12,4},{16,24},{20,28},{24,16},{28,20},{1,9},{5... | collective-permute-start | bytes 589832 | tf_op jit(solution)/shard_map/ppermute | solution.py:201
  43.7 9.0 %shard_map.60 = (bf16[2,128,384]{2,1,0:T(8,128)(2,1)S(1)}, bf16[2,128,384]{2,1,0:T(8,128)(2,1)S(1)}, bf16[2,128,384]{2,1,0:T(8,128)(2,1)S(1)}, bf16[2,128,384]{2,1,0:T(8,128)(2,1)S(1)}) custom-call(s32[2]{0:T(128)S(1)} %pad_add_fusion.meta_ref, bf16[3072,768]{1,0:T(8,128)(2,1)S(1)} %shard_map.59.weights_ref, f32[1,1536]{1,0:T(1,128)S(1)} %reshape.7.bias_ref, ...), custom_call_target="tpu_custom_call" | custom-call | flops 144955152 | bytes 94371 | tf_op jit(solution)/shard_map/pallas_call | solution.py:146
  52.9 1.5 %collective-permute-start.24 = (bf16[2,128,384]{2,1,0:T(8,128)(2,1)S(1)}, bf16[2,128,384]{2,1,0:T(8,128)(2,1)S(1)}, u32[]{:S(2)}, u32[]{:S(2)}) collective-permute-start(bf16[2,128,384]{2,1,0:T(8,128)(2,1)S(1)} %get-tuple-element.46), channel_id=1, source_target_pairs={{0,8},{4,12},{8,0},{12,4},{16,24},{20,28},{24,16},{28,20},{1,9},{5... | collective-permute-start | bytes 589832 | tf_op jit(solution)/shard_map/ppermute | solution.py:201
  56.5 8.8 %shard_map.61 = (bf16[2,128,384]{2,1,0:T(8,128)(2,1)S(1)}, bf16[2,128,384]{2,1,0:T(8,128)(2,1)S(1)}, bf16[2,128,384]{2,1,0:T(8,128)(2,1)S(1)}, bf16[2,128,384]{2,1,0:T(8,128)(2,1)S(1)}) custom-call(s32[2]{0:T(128)S(1)} %pad_add_fusion.meta_ref, bf16[3072,768]{1,0:T(8,128)(2,1)S(1)} %shard_map.59.weights_ref, f32[1,1536]{1,0:T(1,128)S(1)} %reshape.7.bias_ref, ...), custom_call_target="tpu_custom_call" | custom-call | flops 144955152 | bytes 94371 | tf_op jit(solution)/shard_map/pallas_call | solution.py:146
  65.3 1.5 %collective-permute-start.20 = (bf16[2,128,384]{2,1,0:T(8,128)(2,1)S(1)}, bf16[2,128,384]{2,1,0:T(8,128)(2,1)S(1)}, u32[]{:S(2)}, u32[]{:S(2)}) collective-permute-start(bf16[2,128,384]{2,1,0:T(8,128)(2,1)S(1)} %get-tuple-element.54), channel_id=1, source_target_pairs={{0,8},{4,12},{8,0},{12,4},{16,24},{20,28},{24,16},{28,20},{1,9},{5... | collective-permute-start | bytes 589832 | tf_op jit(solution)/shard_map/ppermute | solution.py:201
  67.5 1.3 %collective-permute-start.22 = (bf16[2,128,384]{2,1,0:T(8,128)(2,1)S(1)}, bf16[2,128,384]{2,1,0:T(8,128)(2,1)S(1)}, u32[]{:S(2)}, u32[]{:S(2)}) collective-permute-start(bf16[2,128,384]{2,1,0:T(8,128)(2,1)S(1)} %get-tuple-element.56), channel_id=1, source_target_pairs={{0,24},{4,28},{8,16},{12,20},{16,8},{20,12},{24,0},{28,4},{1,25},{... | collective-permute-start | bytes 589832 | tf_op jit(solution)/shard_map/ppermute | solution.py:201
  69.1 4.1 %collective-permute-done.20.rest_1_ = bf16[2,128,384]{2,1,0:T(8,128)(2,1)S(1)} collective-permute-done((bf16[2,128,384]{2,1,0:T(8,128)(2,1)S(1)}, bf16[2,128,384]{2,1,0:T(8,128)(2,1)S(1)}, u32[]{:S(2)}, u32[]{:S(2)}) %collective-permute-start.20) | collective-permute-done | bytes 196640 | tf_op jit(solution)/shard_map/ppermute | solution.py:201
  73.2 4.0 %collective-permute-done.21.rest_2_ = bf16[2,128,384]{2,1,0:T(8,128)(2,1)S(1)} collective-permute-done((bf16[2,128,384]{2,1,0:T(8,128)(2,1)S(1)}, bf16[2,128,384]{2,1,0:T(8,128)(2,1)S(1)}, u32[]{:S(2)}, u32[]{:S(2)}) %collective-permute-start.21) | collective-permute-done | bytes 196640 | tf_op jit(solution)/shard_map/ppermute | solution.py:201
  77.4 1.5 %shard_map.62.rest_5_ = bf16[2048,384]{1,0:T(8,128)(2,1)} custom-call(s32[2]{0:T(128)S(1)} %pad_add_fusion.meta_ref, bf16[2,128,384]{2,1,0:T(8,128)(2,1)S(1)} %get-tuple-element.45.rest_0_, bf16[2,128,384]{2,1,0:T(8,128)(2,1)S(1)} %collective-permute-done.24.rest_1_, bf16[2,128,384]{2,1,0:T(8,128)(2,1)S(1)} %collective-permute-done.25.rest_2_, ...), custom_call_target="tpu_custom_call" | custom-call | bytes 1572864 | tf_op jit(solution)/shard_map/pallas_call | solution.py:178
  79.1 1.5 %shard_map.63 = bf16[2048,384]{1,0:T(8,128)(2,1)} custom-call(s32[2]{0:T(128)S(1)} %pad_add_fusion.meta_ref, bf16[2,128,384]{2,1,0:T(8,128)(2,1)S(1)} %get-tuple-element.53.rest_0_, bf16[2,128,384]{2,1,0:T(8,128)(2,1)S(1)} %collective-permute-done.20.rest_1_, ...), custom_call_target="tpu_custom_call", output_to_operand_aliasing={{}: (6, {})} | custom-call | bytes 1572864 | tf_op jit(solution)/shard_map/pallas_call | solution.py:178
  (82 shorter events, 15.3 us)
Async XLA Ops:
  1.0 18.2 %collective-permute-start.10 = (bf16[96,768]{1,0:T(8,128)(2,1)S(1)}, bf16[96,768]{1,0:T(8,128)(2,1)S(1)}, u32[]{:S(2)}, u32[]{:S(2)}) collective-permute-start(bf16[96,768]{1,0:T(8,128)(2,1)S(1)} %dynamic-slice_select_fusion), channel_id=1, source_target_pairs={{0,2},{1,3},{2,0},{3,1},{4,6},{5,7},{6,4},{7,5},{8,10},{9,11},{10,... | collective-permute-start | bytes 442376 | tf_op jit(solution)/shard_map/ppermute | solution.py:204
  5.1 9.7 %collective-permute-start = (bf16[96,768]{1,0:T(8,128)(2,1)S(1)}, bf16[96,768]{1,0:T(8,128)(2,1)S(1)}, u32[]{:S(2)}, u32[]{:S(2)}) collective-permute-start(bf16[96,768]{1,0:T(8,128)(2,1)S(1)} %dynamic-slice_select_fusion), channel_id=1, source_target_pairs={{0,3},{1,2},{2,1},{3,0},{4,7},{5,6},{6,5},{7,4},{8,11},{9,10},{10,... | collective-permute-start | bytes 442376 | tf_op jit(solution)/shard_map/ppermute | solution.py:204
  11.2 8.0 %collective-permute-start.3 = (bf16[2,128,384]{2,1,0:T(8,128)(2,1)S(1)}, bf16[2,128,384]{2,1,0:T(8,128)(2,1)S(1)}, u32[]{:S(2)}, u32[]{:S(2)}) collective-permute-start(bf16[2,128,384]{2,1,0:T(8,128)(2,1)S(1)} %get-tuple-element.32), channel_id=1, source_target_pairs={{0,8},{4,12},{8,0},{12,4},{16,24},{20,28},{24,16},{28,20},{1,9},{5... | collective-permute-start | bytes 589832 | tf_op jit(solution)/shard_map/ppermute | solution.py:201
  12.8 10.0 %collective-permute-start.4 = (bf16[2,128,384]{2,1,0:T(8,128)(2,1)S(1)}, bf16[2,128,384]{2,1,0:T(8,128)(2,1)S(1)}, u32[]{:S(2)}, u32[]{:S(2)}) collective-permute-start(bf16[2,128,384]{2,1,0:T(8,128)(2,1)S(1)} %get-tuple-element.33), channel_id=1, source_target_pairs={{0,16},{4,20},{8,24},{12,28},{16,0},{20,4},{24,8},{28,12},{1,17},{... | collective-permute-start | bytes 589832 | tf_op jit(solution)/shard_map/ppermute | solution.py:201
  14.3 8.5 %collective-permute-start.5 = (bf16[2,128,384]{2,1,0:T(8,128)(2,1)S(1)}, bf16[2,128,384]{2,1,0:T(8,128)(2,1)S(1)}, u32[]{:S(2)}, u32[]{:S(2)}) collective-permute-start(bf16[2,128,384]{2,1,0:T(8,128)(2,1)S(1)} %get-tuple-element.34), channel_id=1, source_target_pairs={{0,24},{4,28},{8,16},{12,20},{16,8},{20,12},{24,0},{28,4},{1,25},{... | collective-permute-start | bytes 589832 | tf_op jit(solution)/shard_map/ppermute | solution.py:201
  14.9 23.6 %collective-permute-start.1 = (bf16[384,768]{1,0:T(8,128)(2,1)S(1)}, bf16[384,768]{1,0:T(8,128)(2,1)S(1)}, u32[]{:S(2)}, u32[]{:S(2)}) collective-permute-start(bf16[384,768]{1,0:T(8,128)(2,1)S(1)} %pad_maximum_fusion), channel_id=1, source_target_pairs={{0,1},{1,0},{2,3},{3,2},{4,5},{5,4},{6,7},{7,6},{8,9},{9,8},{10,11... | collective-permute-start | bytes 1769480 | tf_op jit(solution)/shard_map/ppermute | solution.py:204
  22.8 8.7 %collective-permute-start.11 = (bf16[96,768]{1,0:T(8,128)(2,1)S(1)}, bf16[96,768]{1,0:T(8,128)(2,1)S(1)}, u32[]{:S(2)}, u32[]{:S(2)}) collective-permute-start(bf16[96,768]{1,0:T(8,128)(2,1)S(1)} %collective-permute-done.10.rest_7_), channel_id=1, source_target_pairs={{0,8},{4,12},{8,0},{12,4},{16,24},{20,28},{24,16},{28,20},{1,9},{5... | collective-permute-start | bytes 442376 | tf_op jit(solution)/shard_map/ppermute | solution.py:201
  24.0 8.3 %collective-permute-start.12 = (bf16[96,768]{1,0:T(8,128)(2,1)S(1)}, bf16[96,768]{1,0:T(8,128)(2,1)S(1)}, u32[]{:S(2)}, u32[]{:S(2)}) collective-permute-start(bf16[96,768]{1,0:T(8,128)(2,1)S(1)} %collective-permute-done.10.rest_7_), channel_id=1, source_target_pairs={{0,16},{4,20},{8,24},{12,28},{16,0},{20,4},{24,8},{28,12},{1,17},{... | collective-permute-start | bytes 442376 | tf_op jit(solution)/shard_map/ppermute | solution.py:201
  24.9 10.3 %collective-permute-start.13 = (bf16[96,768]{1,0:T(8,128)(2,1)S(1)}, bf16[96,768]{1,0:T(8,128)(2,1)S(1)}, u32[]{:S(2)}, u32[]{:S(2)}) collective-permute-start(bf16[96,768]{1,0:T(8,128)(2,1)S(1)} %collective-permute-done.10.rest_7_), channel_id=1, source_target_pairs={{0,24},{4,28},{8,16},{12,20},{16,8},{20,12},{24,0},{28,4},{1,25},{... | collective-permute-start | bytes 442376 | tf_op jit(solution)/shard_map/ppermute | solution.py:201
  30.2 5.5 %collective-permute-start.6 = (bf16[96,768]{1,0:T(8,128)(2,1)S(1)}, bf16[96,768]{1,0:T(8,128)(2,1)S(1)}, u32[]{:S(2)}, u32[]{:S(2)}) collective-permute-start(bf16[96,768]{1,0:T(8,128)(2,1)S(1)} %collective-permute-done.rest_2_), channel_id=1, source_target_pairs={{0,8},{4,12},{8,0},{12,4},{16,24},{20,28},{24,16},{28,20},{1,9},{5... | collective-permute-start | bytes 442376 | tf_op jit(solution)/shard_map/ppermute | solution.py:201
  31.5 5.1 %collective-permute-start.7 = (bf16[96,768]{1,0:T(8,128)(2,1)S(1)}, bf16[96,768]{1,0:T(8,128)(2,1)S(1)}, u32[]{:S(2)}, u32[]{:S(2)}) collective-permute-start(bf16[96,768]{1,0:T(8,128)(2,1)S(1)} %collective-permute-done.rest_2_), channel_id=1, source_target_pairs={{0,16},{4,20},{8,24},{12,28},{16,0},{20,4},{24,8},{28,12},{1,17},{... | collective-permute-start | bytes 442376 | tf_op jit(solution)/shard_map/ppermute | solution.py:201
  32.3 6.0 %collective-permute-start.8 = (bf16[96,768]{1,0:T(8,128)(2,1)S(1)}, bf16[96,768]{1,0:T(8,128)(2,1)S(1)}, u32[]{:S(2)}, u32[]{:S(2)}) collective-permute-start(bf16[96,768]{1,0:T(8,128)(2,1)S(1)} %collective-permute-done.rest_2_), channel_id=1, source_target_pairs={{0,24},{4,28},{8,16},{12,20},{16,8},{20,12},{24,0},{28,4},{1,25},{... | collective-permute-start | bytes 442376 | tf_op jit(solution)/shard_map/ppermute | solution.py:201
  35.2 5.6 %collective-permute-start.14 = (bf16[384,768]{1,0:T(8,128)(2,1)S(1)}, bf16[384,768]{1,0:T(8,128)(2,1)S(1)}, u32[]{:S(2)}, u32[]{:S(2)}) collective-permute-start(bf16[384,768]{1,0:T(8,128)(2,1)S(1)} %pad_maximum_fusion.2), channel_id=1, source_target_pairs={{0,4},{4,0},{8,12},{12,8},{16,20},{20,16},{24,28},{28,24},{1,5},{5... | collective-permute-start | bytes 1769480 | tf_op jit(solution)/shard_map/ppermute | solution.py:201
  39.2 4.5 %collective-permute-start.18 = (bf16[4,128,384]{2,1,0:T(8,128)(2,1)S(1)}, bf16[4,128,384]{2,1,0:T(8,128)(2,1)S(1)}, u32[]{:S(2)}, u32[]{:S(2)}) collective-permute-start(bf16[4,128,384]{2,1,0:T(8,128)(2,1)S(1)} %pad_maximum_fusion.3), channel_id=1, source_target_pairs={{0,4},{4,0},{8,12},{12,8},{16,20},{20,16},{24,28},{28,24},{1,5},{5... | collective-permute-start | bytes 1179656 | tf_op jit(solution)/shard_map/ppermute | solution.py:201
  39.3 13.4 %collective-permute-start.15 = (bf16[2,128,384]{2,1,0:T(8,128)(2,1)S(1)}, bf16[2,128,384]{2,1,0:T(8,128)(2,1)S(1)}, u32[]{:S(2)}, u32[]{:S(2)}) collective-permute-start(bf16[2,128,384]{2,1,0:T(8,128)(2,1)S(1)} %get-tuple-element.42), channel_id=1, source_target_pairs={{0,8},{4,12},{8,0},{12,4},{16,24},{20,28},{24,16},{28,20},{1,9},{5... | collective-permute-start | bytes 589832 | tf_op jit(solution)/shard_map/ppermute | solution.py:201
  40.8 11.9 %collective-permute-start.16 = (bf16[2,128,384]{2,1,0:T(8,128)(2,1)S(1)}, bf16[2,128,384]{2,1,0:T(8,128)(2,1)S(1)}, u32[]{:S(2)}, u32[]{:S(2)}) collective-permute-start(bf16[2,128,384]{2,1,0:T(8,128)(2,1)S(1)} %get-tuple-element.43), channel_id=1, source_target_pairs={{0,16},{4,20},{8,24},{12,28},{16,0},{20,4},{24,8},{28,12},{1,17},{... | collective-permute-start | bytes 589832 | tf_op jit(solution)/shard_map/ppermute | solution.py:201
  41.5 11.2 %collective-permute-start.17 = (bf16[2,128,384]{2,1,0:T(8,128)(2,1)S(1)}, bf16[2,128,384]{2,1,0:T(8,128)(2,1)S(1)}, u32[]{:S(2)}, u32[]{:S(2)}) collective-permute-start(bf16[2,128,384]{2,1,0:T(8,128)(2,1)S(1)} %get-tuple-element.44), channel_id=1, source_target_pairs={{0,24},{4,28},{8,16},{12,20},{16,8},{20,12},{24,0},{28,4},{1,25},{... | collective-permute-start | bytes 589832 | tf_op jit(solution)/shard_map/ppermute | solution.py:201
  52.9 14.6 %collective-permute-start.24 = (bf16[2,128,384]{2,1,0:T(8,128)(2,1)S(1)}, bf16[2,128,384]{2,1,0:T(8,128)(2,1)S(1)}, u32[]{:S(2)}, u32[]{:S(2)}) collective-permute-start(bf16[2,128,384]{2,1,0:T(8,128)(2,1)S(1)} %get-tuple-element.46), channel_id=1, source_target_pairs={{0,8},{4,12},{8,0},{12,4},{16,24},{20,28},{24,16},{28,20},{1,9},{5... | collective-permute-start | bytes 589832 | tf_op jit(solution)/shard_map/ppermute | solution.py:201
  54.5 14.4 %collective-permute-start.25 = (bf16[2,128,384]{2,1,0:T(8,128)(2,1)S(1)}, bf16[2,128,384]{2,1,0:T(8,128)(2,1)S(1)}, u32[]{:S(2)}, u32[]{:S(2)}) collective-permute-start(bf16[2,128,384]{2,1,0:T(8,128)(2,1)S(1)} %get-tuple-element.47), channel_id=1, source_target_pairs={{0,16},{4,20},{8,24},{12,28},{16,0},{20,4},{24,8},{28,12},{1,17},{... | collective-permute-start | bytes 589832 | tf_op jit(solution)/shard_map/ppermute | solution.py:201
  55.2 13.8 %collective-permute-start.26 = (bf16[2,128,384]{2,1,0:T(8,128)(2,1)S(1)}, bf16[2,128,384]{2,1,0:T(8,128)(2,1)S(1)}, u32[]{:S(2)}, u32[]{:S(2)}) collective-permute-start(bf16[2,128,384]{2,1,0:T(8,128)(2,1)S(1)} %get-tuple-element.48), channel_id=1, source_target_pairs={{0,24},{4,28},{8,16},{12,20},{16,8},{20,12},{24,0},{28,4},{1,25},{... | collective-permute-start | bytes 589832 | tf_op jit(solution)/shard_map/ppermute | solution.py:201
  65.3 7.9 %collective-permute-start.20 = (bf16[2,128,384]{2,1,0:T(8,128)(2,1)S(1)}, bf16[2,128,384]{2,1,0:T(8,128)(2,1)S(1)}, u32[]{:S(2)}, u32[]{:S(2)}) collective-permute-start(bf16[2,128,384]{2,1,0:T(8,128)(2,1)S(1)} %get-tuple-element.54), channel_id=1, source_target_pairs={{0,8},{4,12},{8,0},{12,4},{16,24},{20,28},{24,16},{28,20},{1,9},{5... | collective-permute-start | bytes 589832 | tf_op jit(solution)/shard_map/ppermute | solution.py:201
  66.8 10.4 %collective-permute-start.21 = (bf16[2,128,384]{2,1,0:T(8,128)(2,1)S(1)}, bf16[2,128,384]{2,1,0:T(8,128)(2,1)S(1)}, u32[]{:S(2)}, u32[]{:S(2)}) collective-permute-start(bf16[2,128,384]{2,1,0:T(8,128)(2,1)S(1)} %get-tuple-element.55), channel_id=1, source_target_pairs={{0,16},{4,20},{8,24},{12,28},{16,0},{20,4},{24,8},{28,12},{1,17},{... | collective-permute-start | bytes 589832 | tf_op jit(solution)/shard_map/ppermute | solution.py:201
  67.5 9.7 %collective-permute-start.22 = (bf16[2,128,384]{2,1,0:T(8,128)(2,1)S(1)}, bf16[2,128,384]{2,1,0:T(8,128)(2,1)S(1)}, u32[]{:S(2)}, u32[]{:S(2)}) collective-permute-start(bf16[2,128,384]{2,1,0:T(8,128)(2,1)S(1)} %get-tuple-element.56), channel_id=1, source_target_pairs={{0,24},{4,28},{8,16},{12,20},{16,8},{20,12},{24,0},{28,4},{1,25},{... | collective-permute-start | bytes 589832 | tf_op jit(solution)/shard_map/ppermute | solution.py:201
  69.0 8.4 %collective-permute-start.27 = (bf16[4,128,384]{2,1,0:T(8,128)(2,1)S(1)}, bf16[4,128,384]{2,1,0:T(8,128)(2,1)S(1)}, u32[]{:S(2)}, u32[]{:S(2)}) collective-permute-start(bf16[4,128,384]{2,1,0:T(8,128)(2,1)S(1)} %pad_maximum_fusion.6), channel_id=1, source_target_pairs={{0,4},{4,0},{8,12},{12,8},{16,20},{20,16},{24,28},{28,24},{1,5},{5... | collective-permute-start | bytes 1179656 | tf_op jit(solution)/shard_map/ppermute | solution.py:201
  (11 other events, 57.7 us)
